TPU v7x, 32 devices: a whole 2x2x4 slice. The times are simulated.
32 devices in a mesh: seqhi: 4 (over x, core), seqlo: 8 (over z, y).
Axes of the slice: x: 2, y: 2, z: 4, core: 2. Of those that a mesh axis runs over, the one named last changes fastest.
Arguments:
- features: float32 [8192, 256], P(('seqhi', 'seqlo')), may hold values from -6 to 6
- norm_gain: float32 [8, 512], replicated, may hold values from 0.1 to 1.9
- bias_hidden: float32 [8, 1024], replicated, may hold values from -4 to 4
- gate_logit: float32 [8, 512], replicated, may hold values from -2 to 2
- w_in: float32 [512, 1024], replicated, may hold values from -0.25 to 0.25
- w_out: float32 [1024, 512], replicated, may hold values from -0.1875 to 0.1875
Outputs:
- switched: float32 [8192, 256], P(('seqhi', 'seqlo'))
All inputs are finite; a program needn't handle non-finite values.
Results may differ from a plain program's by a relative error of at most 0.0001.
Values sent between devices are 32-bit elements; how exact they have to be, the bound alone decides.
No kernel may reach another device: no remote copies, remote signals or barrier semaphores. Data moves between devices by JAX's collectives and lax.ppermute only.
A program may use at most 64 MiB of HBM per device.

v0:
```python
import jax
import jax.numpy as jnp
from jax import lax
from jax.sharding import PartitionSpec as P

HI_LAYERS = 4


NORM_EPS = 1e-05


def switch_unit(lower_rows, upper_rows, layer_params):
    norm_gain, bias_hidden, gate_logit, w_in, w_out = layer_params
    feature_count = lower_rows.shape[-1]
    paired = jnp.concatenate([lower_rows, upper_rows], axis=-1)
    center = paired - jnp.mean(paired, axis=-1, keepdims=True)
    spread = jnp.mean(center * center, axis=-1, keepdims=True)
    normed = center * lax.rsqrt(spread + NORM_EPS) * norm_gain
    hidden = jax.nn.gelu(
        jnp.dot(normed, w_in, precision=lax.Precision.HIGHEST, preferred_element_type=jnp.float32)
        + bias_hidden
    )
    mixed_out = jax.nn.sigmoid(gate_logit) * paired + jnp.dot(
        hidden, w_out, precision=lax.Precision.HIGHEST, preferred_element_type=jnp.float32
    )
    return (mixed_out[:, :feature_count], mixed_out[:, feature_count:])


def pair_layer(states, distance, layer_params):
    row_count, feature_count = states.shape
    groups = row_count // (2 * distance)
    grouped = states.reshape(groups, 2, distance, feature_count)
    new_lower, new_upper = switch_unit(
        grouped[:, 0].reshape(-1, feature_count),
        grouped[:, 1].reshape(-1, feature_count),
        layer_params,
    )
    joined = jnp.stack(
        [
            new_lower.reshape(groups, distance, feature_count),
            new_upper.reshape(groups, distance, feature_count),
        ],
        axis=1,
    )
    return joined.reshape(row_count, feature_count)


def body(features, norm_gain, bias_hidden, gate_logit, w_in, w_out):
    local_rows = features.shape[0]
    high_count = lax.axis_size("seqhi")
    low_count = lax.axis_size("seqlo")
    high_bits = high_count.bit_length() - 1
    low_bits = low_count.bit_length() - 1
    layer_total = norm_gain.shape[0]
    high_layers = HI_LAYERS

    def params_of(layer_index):
        return (
            norm_gain[layer_index],
            bias_hidden[layer_index],
            gate_logit[layer_index],
            w_in,
            w_out,
        )

    states = features
    states = lax.all_to_all(states, "seqhi", split_axis=0, concat_axis=0, tiled=True)
    for layer_index in range(high_layers):
        distance = local_rows // high_count * 2 ** (layer_index % high_bits)
        states = pair_layer(states, distance, params_of(layer_index))
    states = lax.all_to_all(states, "seqhi", split_axis=0, concat_axis=0, tiled=True)
    low_states = states
    low_states = lax.all_to_all(low_states, "seqlo", split_axis=0, concat_axis=0, tiled=True)
    states = low_states
    for layer_index in range(high_layers, layer_total):
        distance = local_rows // low_count * 2 ** ((layer_index - high_layers) % low_bits)
        states = pair_layer(states, distance, params_of(layer_index))
    return lax.all_to_all(states, "seqlo", split_axis=0, concat_axis=0, tiled=True)


def solution(mesh):
    placed = (P(("seqhi", "seqlo"), None), P(), P(), P(), P(), P())
    return jax.shard_map(
        body, mesh=mesh, in_specs=placed, out_specs=P(("seqhi", "seqlo"), None), check_vma=False
    )
```

profile of v0, /device:TPU:0, one launch (start us, length us, event | category | flops | bytes accessed | tf_op | source)
XLA Modules:
  0.0 71.3 jit_solution(9511273918941494144)
XLA Ops:
  0.0 0.0 copy-start
  0.0 4.3 %all-to-all-start = ((f32[4,64,256]{2,1,0:T(8,128)}), f32[4,64,256]{2,1,0:T(8,128)S(1)}, u32[]{:S(2)}, u32[]{:S(2)}) async-start(f32[4,64,256]{2,1,0:T(8,128)} %bitcast.163), calls=%async_computation | async-start | bytes 524288 | tf_op jit(solution)/shard_map/all_to_all | solution.py:67
  4.3 1.0 %fusion.123 = (f32[1,512]{1,0:T(1,128)S(1)}, f32[1,512]{1,0:T(1,128)S(1)}, f32[1,512]{1,0:T(1,128)S(1)}, f32[1,512]{1,0:T(1,128)S(1)}, f32[1,512]{1,0:T(1,128)S(...) fusion(f32[8,512]{1,0:T(8,128)} %param.7), kind=kLoop, calls=%fused_computation.220 | loop fusion | bytes 32768 | tf_op jit(solution)/shard_map/slice | solution.py:59
  5.4 1.1 %fusion.122 = (f32[1,1024]{1,0:T(1,128)S(1)}, f32[1,1024]{1,0:T(1,128)S(1)}, f32[1,1024]{1,0:T(1,128)S(1)}, f32[1,1024]{1,0:T(1,128)S(1)}, f32[1,1024]{1,0:T(1,1...) fusion(f32[8,1024]{1,0:T(8,128)} %param.8), kind=kLoop, calls=%fused_computation.219 | loop fusion | bytes 65536 | tf_op jit(solution)/shard_map/slice | solution.py:60
  6.5 1.1 %add_divide_fusion.7 = (f32[1,512]{1,0:T(1,128)S(1)}, f32[1,512]{1,0:T(1,128)S(1)}, f32[1,512]{1,0:T(1,128)S(1)}, f32[1,512]{1,0:T(1,128)S(1)}, f32[1,512]{1,0:T...) fusion(f32[8,512]{1,0:T(8,128)} %param.9), kind=kLoop, calls=%fused_computation.180 | loop fusion | flops 12288 | bytes 32768 | tf_op jit(solution)/shard_map/div | solution.py:23
  7.5 2.9 %all-to-all-done = f32[4,64,256]{2,1,0:T(8,128)S(1)} async-done(((f32[4,64,256]{2,1,0:T(8,128)}), f32[4,64,256]{2,1,0:T(8,128)S(1)}, u32[]{:S(2)}, u32[]{:S(2)}) %all-to-all-start) | async-done | bytes 262176 | tf_op jit(solution)/shard_map/all_to_all | solution.py:67
  10.4 0.1 slice_reduce_fusion.12
  10.5 0.1 div.99
  10.6 0.0 copy-start.1
  10.6 0.2 multiply_reduce_fusion.7
  10.8 0.0 copy-done
  10.8 1.4 %fusion.6 = f32[128,1024]{1,0:T(8,128)S(1)} fusion(f32[512,1024]{1,0:T(8,128)S(1)} %copy-done, f32[1024]{0:T(1024)S(1)} %bitcast.171, f32[128,256]{1,0:T(8,128)S(1)} %bitcast.123, f32[128,256]{1,0:T(8,128)S(1)} %bitcast.126, f32[512]{0:T(512)S(1)} %bitcast.179, f32[128]{0:T(128)S(1)} %add_rsqrt_fusion.7, f32[128]{0:T(128)S(1)} %div.99), kind=kOutput, calls=%fused_computation.30 | convolution fusion | flops 806748160 | bytes 2890752 | tf_op jit(solution)/shard_map/dot_general | solution.py:20
  12.2 0.0 copy-done.1
  12.2 1.3 %convolution_add_fusion.15 = f32[128,512]{1,0:T(8,128)S(1)} fusion(f32[128,1024]{1,0:T(8,128)S(1)} %fusion.6, f32[1024,512]{1,0:T(8,128)S(1)} %copy-done.1, f32[128,256]{1,0:T(8,128)S(1)} %bitcast.124, f32[128,256]{1,0:T(8,128)S(1)} %bitcast.127, f32[512]{0:T(512)S(1)} %bitcast.187), kind=kOutput, calls=%fused_computation.15 | convolution fusion | flops 805502976 | bytes 3147776 | tf_op jit(solution)/shard_map/dot_general | solution.py:23
  13.6 0.1 slice_reduce_fusion.4
  13.7 0.2 multiply_reduce_fusion.6
  13.9 1.4 %fusion.13 = f32[128,1024]{1,0:T(8,128)S(1)} fusion(f32[512,1024]{1,0:T(8,128)S(1)} %copy-done, f32[1024]{0:T(1024)S(1)} %bitcast.170, f32[128,256]{1,0:T(8,128)S(1)} %get-tuple-element.49, f32[128,256]{1,0:T(8,128)S(1)} %get-tuple-element.50, f32[512]{0:T(512)S(1)} %bitcast.178, f32[128]{0:T(128)S(1)} %add_rsqrt_fusion.6, f32[128]{0:T(128)S(1)} %add_multiply_fusion.7), kind=kOutput, calls=%fused_computation.37 | convolution fusion | flops 806748160 | bytes 2890752 | tf_op jit(solution)/shard_map/dot_general | solution.py:20
  15.3 1.3 %convolution_add_fusion.14 = f32[128,512]{1,0:T(8,128)S(1)} fusion(f32[128,1024]{1,0:T(8,128)S(1)} %fusion.13, f32[1024,512]{1,0:T(8,128)S(1)} %copy-done.1, f32[128,256]{1,0:T(8,128)S(1)} %get-tuple-element.49, f32[128,256]{1,0:T(8,128)S(1)} %get-tuple-element.50, f32[512]{0:T(512)S(1)} %bitcast.186), kind=kOutput, calls=%fused_computation.14 | convolution fusion | flops 805502976 | bytes 3147776 | tf_op jit(solution)/shard_map/dot_general | solution.py:23
  16.6 0.1 fusion.114
  16.8 0.1 div.104
  16.8 0.0 copy-start.2
  16.8 0.2 multiply_reduce_fusion.5
  17.0 1.4 %fusion.20 = f32[128,1024]{1,0:T(8,128)S(1)} fusion(f32[512,1024]{1,0:T(8,128)S(1)} %copy-done, f32[1024]{0:T(1024)S(1)} %bitcast.169, f32[128,256]{1,0:T(8,128)S(1)} %bitcast.120, f32[128,256]{1,0:T(8,128)S(1)} %bitcast.117, f32[512]{0:T(512)S(1)} %bitcast.177, f32[128]{0:T(128)S(1)} %add_rsqrt_fusion.5, f32[128]{0:T(128)S(1)} %div.104), kind=kOutput, calls=%fused_computation.44 | convolution fusion | flops 806748160 | bytes 2890752 | tf_op jit(solution)/shard_map/dot_general | solution.py:20
  18.4 0.0 copy-done.2
  18.4 1.3 %convolution_add_fusion.13 = f32[128,512]{1,0:T(8,128)S(1)} fusion(f32[128,1024]{1,0:T(8,128)S(1)} %fusion.20, f32[1024,512]{1,0:T(8,128)S(1)} %copy-done.2, f32[128,256]{1,0:T(8,128)S(1)} %bitcast.121, f32[128,256]{1,0:T(8,128)S(1)} %bitcast.118, f32[512]{0:T(512)S(1)} %bitcast.185), kind=kOutput, calls=%fused_computation.13 | convolution fusion | flops 805502976 | bytes 3147776 | tf_op jit(solution)/shard_map/dot_general | solution.py:23
  19.8 0.1 slice_reduce_fusion.2
  19.9 0.2 multiply_reduce_fusion.4
  20.1 1.4 %fusion.27 = f32[128,1024]{1,0:T(8,128)S(1)} fusion(f32[512,1024]{1,0:T(8,128)S(1)} %copy-done, f32[1024]{0:T(1024)S(1)} %bitcast.168, f32[128,256]{1,0:T(8,128)S(1)} %get-tuple-element.41, f32[128,256]{1,0:T(8,128)S(1)} %get-tuple-element.42, f32[512]{0:T(512)S(1)} %bitcast.176, f32[128]{0:T(128)S(1)} %add_rsqrt_fusion.4, f32[128]{0:T(128)S(1)} %add_multiply_fusion.6), kind=kOutput, calls=%fused_computation.51 | convolution fusion | flops 806748160 | bytes 2890752 | tf_op jit(solution)/shard_map/dot_general | solution.py:20
  21.5 1.3 %convolution_add_fusion.12 = f32[128,512]{1,0:T(8,128)S(1)} fusion(f32[128,1024]{1,0:T(8,128)S(1)} %fusion.27, f32[1024,512]{1,0:T(8,128)S(1)} %copy-done.2, f32[128,256]{1,0:T(8,128)S(1)} %get-tuple-element.41, f32[128,256]{1,0:T(8,128)S(1)} %get-tuple-element.42, f32[512]{0:T(512)S(1)} %bitcast.184), kind=kOutput, calls=%fused_computation.12 | convolution fusion | flops 805502976 | bytes 3147776 | tf_op jit(solution)/shard_map/dot_general | solution.py:23
  22.9 8.4 %all_to_all.39 = f32[4,64,256]{2,1,0:T(8,128)S(1)} all-to-all(f32[4,64,256]{2,1,0:T(8,128)S(1)} %bitcast.147), channel_id=1, replica_groups=mesh['seqhi'=4,'seqlo'=8] {'seqhi'}, dimensions={0} | all-to-all | bytes 524288 | tf_op jit(solution)/shard_map/all_to_all | solution.py:71
  31.3 14.8 %all_to_all.40 = f32[8,32,256]{2,1,0:T(8,128)S(1)} all-to-all(f32[8,32,256]{2,1,0:T(8,128)S(1)} %bitcast.149), channel_id=1, replica_groups=mesh['seqhi'=4,'seqlo'=8] {'seqlo'}, dimensions={0} | all-to-all | bytes 524288 | tf_op jit(solution)/shard_map/all_to_all | solution.py:73
  46.1 0.1 slice_reduce_fusion.10
  46.2 0.1 div.109
  46.3 0.0 copy-start.3
  46.3 0.2 multiply_reduce_fusion.3
  46.5 1.4 %fusion.34 = f32[128,1024]{1,0:T(8,128)S(1)} fusion(f32[512,1024]{1,0:T(8,128)S(1)} %copy-done, f32[1024]{0:T(1024)S(1)} %bitcast.167, f32[128,256]{1,0:T(8,128)S(1)} %bitcast.129, f32[128,256]{1,0:T(8,128)S(1)} %bitcast.132, f32[512]{0:T(512)S(1)} %bitcast.175, f32[128]{0:T(128)S(1)} %add_rsqrt_fusion.3, f32[128]{0:T(128)S(1)} %div.109), kind=kOutput, calls=%fused_computation.58 | convolution fusion | flops 806748160 | bytes 2890752 | tf_op jit(solution)/shard_map/dot_general | solution.py:20
  47.9 0.0 copy-done.3
  47.9 1.3 %convolution_add_fusion.11 = f32[128,512]{1,0:T(8,128)S(1)} fusion(f32[128,1024]{1,0:T(8,128)S(1)} %fusion.34, f32[1024,512]{1,0:T(8,128)S(1)} %copy-done.3, f32[128,256]{1,0:T(8,128)S(1)} %bitcast.130, f32[128,256]{1,0:T(8,128)S(1)} %bitcast.133, f32[512]{0:T(512)S(1)} %bitcast.183), kind=kOutput, calls=%fused_computation.11 | convolution fusion | flops 805502976 | bytes 3147776 | tf_op jit(solution)/shard_map/dot_general | solution.py:23
  49.3 0.1 slice_reduce_fusion.8
  49.4 0.1 div.112
  49.5 0.0 copy-start.4
  49.5 0.2 multiply_reduce_fusion.2
  49.7 1.4 %fusion.41 = f32[128,1024]{1,0:T(8,128)S(1)} fusion(f32[512,1024]{1,0:T(8,128)S(1)} %copy-done, f32[1024]{0:T(1024)S(1)} %bitcast.166, f32[128,256]{1,0:T(8,128)S(1)} %bitcast.135, f32[128,256]{1,0:T(8,128)S(1)} %bitcast.138, f32[512]{0:T(512)S(1)} %bitcast.174, f32[128]{0:T(128)S(1)} %add_rsqrt_fusion.2, f32[128]{0:T(128)S(1)} %div.112), kind=kOutput, calls=%fused_computation.65 | convolution fusion | flops 806748160 | bytes 2890752 | tf_op jit(solution)/shard_map/dot_general | solution.py:20
  51.1 0.0 copy-done.4
  51.1 1.3 %convolution_add_fusion.10 = f32[128,512]{1,0:T(8,128)S(1)} fusion(f32[128,1024]{1,0:T(8,128)S(1)} %fusion.41, f32[1024,512]{1,0:T(8,128)S(1)} %copy-done.4, f32[128,256]{1,0:T(8,128)S(1)} %bitcast.136, f32[128,256]{1,0:T(8,128)S(1)} %bitcast.139, f32[512]{0:T(512)S(1)} %bitcast.182), kind=kOutput, calls=%fused_computation.10 | convolution fusion | flops 805502976 | bytes 3147776 | tf_op jit(solution)/shard_map/dot_general | solution.py:23
  52.5 0.1 slice_reduce_fusion
  52.6 0.2 multiply_reduce_fusion.1
  52.8 1.4 %fusion.48 = f32[128,1024]{1,0:T(8,128)S(1)} fusion(f32[512,1024]{1,0:T(8,128)S(1)} %copy-done, f32[1024]{0:T(1024)S(1)} %bitcast.165, f32[128,256]{1,0:T(8,128)S(1)} %get-tuple-element.29, f32[128,256]{1,0:T(8,128)S(1)} %get-tuple-element.30, f32[512]{0:T(512)S(1)} %bitcast.173, f32[128]{0:T(128)S(1)} %add_rsqrt_fusion.1, f32[128]{0:T(128)S(1)} %add_multiply_fusion.5), kind=kOutput, calls=%fused_computation.72 | convolution fusion | flops 806748160 | bytes 2890752 | tf_op jit(solution)/shard_map/dot_general | solution.py:20
  54.2 1.3 %convolution_add_fusion.9 = f32[128,512]{1,0:T(8,128)S(1)} fusion(f32[128,1024]{1,0:T(8,128)S(1)} %fusion.48, f32[1024,512]{1,0:T(8,128)S(1)} %copy-done.4, f32[128,256]{1,0:T(8,128)S(1)} %get-tuple-element.29, f32[128,256]{1,0:T(8,128)S(1)} %get-tuple-element.30, f32[512]{0:T(512)S(1)} %bitcast.181), kind=kOutput, calls=%fused_computation.9 | convolution fusion | flops 805502976 | bytes 3147776 | tf_op jit(solution)/shard_map/dot_general | solution.py:23
  55.5 0.1 slice_reduce_fusion.6
  55.7 0.1 div.117
  55.7 0.0 copy-start.5
  55.7 0.2 multiply_reduce_fusion
  55.9 1.4 %fusion.55 = f32[128,1024]{1,0:T(8,128)S(1)} fusion(f32[512,1024]{1,0:T(8,128)S(1)} %copy-done, f32[1024]{0:T(1024)S(1)} %bitcast.164, f32[128,256]{1,0:T(8,128)S(1)} %bitcast.111, f32[128,256]{1,0:T(8,128)S(1)} %bitcast.114, f32[512]{0:T(512)S(1)} %bitcast.172, f32[128]{0:T(128)S(1)} %add_rsqrt_fusion, f32[128]{0:T(128)S(1)} %div.117), kind=kOutput, calls=%fused_computation.79 | convolution fusion | flops 806748160 | bytes 2890752 | tf_op jit(solution)/shard_map/dot_general | solution.py:20
  57.3 0.0 copy-done.5
  57.4 1.3 %convolution_add_fusion.8 = f32[128,512]{1,0:T(8,128)S(1)} fusion(f32[128,1024]{1,0:T(8,128)S(1)} %fusion.55, f32[1024,512]{1,0:T(8,128)S(1)} %copy-done.5, f32[128,256]{1,0:T(8,128)S(1)} %bitcast.112, f32[128,256]{1,0:T(8,128)S(1)} %bitcast.115, f32[512]{0:T(512)S(1)} %bitcast.180), kind=kOutput, calls=%fused_computation.8 | convolution fusion | flops 805502976 | bytes 3147776 | tf_op jit(solution)/shard_map/dot_general | solution.py:23
  58.7 11.9 %all_to_all.41 = f32[8,32,256]{2,1,0:T(8,128)S(1)} all-to-all(f32[8,32,256]{2,1,0:T(8,128)S(1)} %bitcast.148), channel_id=1, replica_groups=mesh['seqhi'=4,'seqlo'=8] {'seqlo'}, dimensions={0} | all-to-all | bytes 524288 | tf_op jit(solution)/shard_map/all_to_all | solution.py:78
  70.6 0.7 copy.18
  (34 shorter events, 0.4 us)
Async XLA Ops:
  0.0 10.8 %copy-start = (f32[512,1024]{1,0:T(8,128)S(1)}, f32[512,1024]{1,0:T(8,128)}, u32[]{:S(2)}) copy-start(f32[512,1024]{1,0:T(8,128)} %param.10) | copy-start | bytes 6291460
  0.0 10.4 %all-to-all-start = ((f32[4,64,256]{2,1,0:T(8,128)}), f32[4,64,256]{2,1,0:T(8,128)S(1)}, u32[]{:S(2)}, u32[]{:S(2)}) async-start(f32[4,64,256]{2,1,0:T(8,128)} %bitcast.163), calls=%async_computation | async-start | bytes 524288 | tf_op jit(solution)/shard_map/all_to_all | solution.py:67
  10.6 1.6 %copy-start.1 = (f32[1024,512]{1,0:T(8,128)S(1)}, f32[1024,512]{1,0:T(8,128)}, u32[]{:S(2)}) copy-start(f32[1024,512]{1,0:T(8,128)} %param.11) | copy-start | bytes 6291460
  16.8 1.6 %copy-start.2 = (f32[1024,512]{1,0:T(8,128)S(1)}, f32[1024,512]{1,0:T(8,128)}, u32[]{:S(2)}) copy-start(f32[1024,512]{1,0:T(8,128)} %param.11) | copy-start | bytes 6291460
  46.3 1.6 %copy-start.3 = (f32[1024,512]{1,0:T(8,128)S(1)}, f32[1024,512]{1,0:T(8,128)}, u32[]{:S(2)}) copy-start(f32[1024,512]{1,0:T(8,128)} %param.11) | copy-start | bytes 6291460
  49.5 1.6 %copy-start.4 = (f32[1024,512]{1,0:T(8,128)S(1)}, f32[1024,512]{1,0:T(8,128)}, u32[]{:S(2)}) copy-start(f32[1024,512]{1,0:T(8,128)} %param.11) | copy-start | bytes 6291460
  55.7 1.6 %copy-start.5 = (f32[1024,512]{1,0:T(8,128)S(1)}, f32[1024,512]{1,0:T(8,128)}, u32[]{:S(2)}) copy-start(f32[1024,512]{1,0:T(8,128)} %param.11) | copy-start | bytes 6291460
where the time goes:
time: 72 us; the launch traced here: 71.3 us
  blocking collectives  35.1 us (49%)
  matrix products  21.4 us (30%)
  starting transfers between devices  4.34 us (6%)
  other arithmetic  3.6 us (5%)
  local copies, waits for them, and re-layouts  3.45 us (5%)
  waiting for transfers between devices  2.87 us (4%)
    all_to_all x1, blocking collectives, body(): lax.all_to_all(low_states, 'seqlo', split_axis=0, concat_axis=0, tiled=True)  14.8 us
    all_to_all x1, blocking collectives, body(): lax.all_to_all(states, 'seqlo', split_axis=0, concat_axis=0, tiled=True)  11.9 us
    dot_general x8, matrix products, switch_unit(): jnp.dot(normed, w_in, precision=lax.Precision.HIGHEST, preferred_element_...  11.1 us
    dot_general x8, matrix products, switch_unit(): jnp.dot(hidden, w_out, precision=lax.Precision.HIGHEST, preferred_element...  10.3 us
    all_to_all x1, blocking collectives, body(): lax.all_to_all(states, 'seqhi', split_axis=0, concat_axis=0, tiled=True)  8.42 us
    all_to_all x1, starting transfers between devices, body(): lax.all_to_all(states, 'seqhi', split_axis=0, concat_axis=0, tiled=True)  4.34 us
    all_to_all x1, waiting for transfers between devices, body(): lax.all_to_all(states, 'seqhi', split_axis=0, concat_axis=0, tiled=True)  2.87 us
  transfers between devices with their start and end apart: 1, of which 1 were waited for; matrix products, arithmetic and copies ran while one was open for 4% of the time, Pallas kernels for 0%

commit v1 on v0

v1 whole, which is shorter than its diff:
```python
import functools

import jax
import jax.numpy as jnp
from jax import lax
from jax.experimental import pallas as pl
from jax.experimental.pallas import tpu as pltpu
from jax.sharding import PartitionSpec as P

HI_LAYERS = 4
NORM_EPS = 1e-05
GELU_SCALE = 0.7978845608028654
GELU_CUBE = 0.044715


def split_high_low(x):
    high = x.astype(jnp.bfloat16)
    return high, (x - high.astype(jnp.float32)).astype(jnp.bfloat16)


def dot(a, b):
    return jnp.dot(a, b, preferred_element_type=jnp.float32)


def dot_split(x, w_high, w_low):
    rows = x.shape[0]
    x_high, x_low = split_high_low(x)
    both = dot(jnp.concatenate([x_high, x_low], axis=0), w_high)
    return both[:rows] + (both[rows:] + dot(x_high, w_low))


def gelu(x):
    return 0.5 * x * (1.0 + jnp.tanh(GELU_SCALE * (x + GELU_CUBE * (x * x * x))))


def switch_unit(lower, upper, gain, bias, gate, w_in, w_out, hidden_block):
    width = lower.shape[-1]
    pair = jnp.concatenate([lower, upper], axis=-1)
    center = pair - jnp.mean(pair, axis=-1, keepdims=True)
    spread = jnp.mean(center * center, axis=-1, keepdims=True)
    normed = center * lax.rsqrt(spread + NORM_EPS) * gain
    out = gate * pair
    in_high, in_low = w_in
    out_high, out_low = w_out
    for start in range(0, in_high.shape[1], hidden_block):
        cols = slice(start, start + hidden_block)
        hidden = gelu(dot_split(normed, in_high[:, cols], in_low[:, cols]) + bias[:, cols])
        out = out + dot_split(hidden, out_high[cols, :], out_low[cols, :])
    return out[:, :width], out[:, width:]


def layers_kernel(
    first, distances, hidden_block,
    x_ref, gain_ref, bias_ref, gate_ref, in_high_ref, in_low_ref, out_high_ref, out_low_ref, y_ref,
):
    rows, width = x_ref.shape
    states = x_ref[...]
    for step, distance in enumerate(distances):
        k = first + step
        groups = rows // (2 * distance)
        grouped = states.reshape(groups, 2, distance, width)
        new_lower, new_upper = switch_unit(
            grouped[:, 0].reshape(-1, width),
            grouped[:, 1].reshape(-1, width),
            gain_ref[k : k + 1, :],
            bias_ref[k : k + 1, :],
            jax.nn.sigmoid(gate_ref[k : k + 1, :]),
            (in_high_ref, in_low_ref),
            (out_high_ref, out_low_ref),
            hidden_block,
        )
        shape = (groups, 1, distance, width)
        states = jnp.concatenate(
            [new_lower.reshape(shape), new_upper.reshape(shape)], axis=1
        ).reshape(rows, width)
    y_ref[...] = states.reshape(y_ref.shape)


def run_layers(states, first, distances, params, name):
    rows, width = states.shape
    hidden = params[1].shape[1]
    kernel = functools.partial(layers_kernel, first, distances, min(hidden, 256))
    return pl.pallas_call(
        kernel,
        out_shape=jax.ShapeDtypeStruct((rows, width), jnp.float32),
        in_specs=[pl.BlockSpec(memory_space=pltpu.VMEM)] * 8,
        out_specs=pl.BlockSpec(memory_space=pltpu.VMEM),
        compiler_params=pltpu.CompilerParams(vmem_limit_bytes=24 * 2**20),
        name=name,
    )(states, *params)


def swap_leading(x, a, b):
    return x.reshape(a, b, -1, x.shape[-1]).swapaxes(0, 1).reshape(x.shape)


def all_to_all(x, axes):
    return lax.all_to_all(x, axes, split_axis=0, concat_axis=0, tiled=True)


def body(features, norm_gain, bias_hidden, gate_logit, w_in, w_out):
    rows = features.shape[0]
    high_count = lax.axis_size("seqhi")
    low_count = lax.axis_size("seqlo")
    high_bits = high_count.bit_length() - 1
    low_bits = low_count.bit_length() - 1
    layer_total = norm_gain.shape[0]

    def parts(w):
        high = lax.reduce_precision(w, exponent_bits=8, mantissa_bits=7)
        return high.astype(jnp.bfloat16), (w - high).astype(jnp.bfloat16)

    params = (norm_gain, bias_hidden, gate_logit, *parts(w_in), *parts(w_out))
    high_distances = [rows // high_count * 2 ** (k % high_bits) for k in range(HI_LAYERS)]
    low_distances = [rows // low_count * 2 ** (j % low_bits) for j in range(layer_total - HI_LAYERS)]

    states = all_to_all(features, "seqhi")
    states = run_layers(states, 0, high_distances, params, "high_layers")
    if rows % (8 * high_count * low_count) == 0:
        states = swap_leading(states, high_count, low_count)
        states = all_to_all(states, "seqlo")
        states = run_layers(states, HI_LAYERS, low_distances, params, "low_layers")
        states = swap_leading(states, low_count, high_count)
        return all_to_all(states, ("seqhi", "seqlo"))
    states = all_to_all(states, "seqhi")
    states = all_to_all(states, "seqlo")
    states = run_layers(states, HI_LAYERS, low_distances, params, "low_layers")
    return all_to_all(states, "seqlo")


def solution(mesh):
    placed = (P(("seqhi", "seqlo"), None), P(), P(), P(), P(), P())
    return jax.shard_map(
        body, mesh=mesh, in_specs=placed, out_specs=P(("seqhi", "seqlo"), None), check_vma=False
    )
```

time: 72 us -> 51.9 us (0.72)
  matrix products: 21.4 us -> 0 us
  Pallas kernels: 0 us -> 11.2 us
  blocking collectives: 35.1 us -> 28.2 us
  local copies, waits for them, and re-layouts: 3.45 us -> 2.02 us
    dot_general x16 -> x0, matrix products: 21.4 us -> none  [the longest x8 11.1 us: switch_unit(): jnp.dot(normed, w_in, precision=lax.Precision.HIGHEST, preferred_element_...]
    pallas_call x0 -> x2, Pallas kernels: none -> 11.2 us  [run_layers(): pl.pallas_call(kernel, out_shape=jax.ShapeDtypeStruct((rows, width), jnp....]
    all_to_all x3 -> x2, blocking collectives: 35.1 us -> 28.2 us  [all_to_all(): return lax.all_to_all(x, axes, split_axis=0, concat_axis=0, tiled=True)]
    convert_element_type x0 -> x2, other arithmetic: none -> 3.48 us  [parts(): return (high.astype(jnp.bfloat16), (w - high).astype(jnp.bfloat16))]
    reduce_sum x16 -> x0, other arithmetic: 2.31 us -> none  [the longest x8 1.41 us: switch_unit(): spread = jnp.mean(center * center, axis=-1, keepdims=True)]
    slice x8 -> x0, local copies, waits for them, and re-layouts: 2.22 us -> none  [the longest x1 1.08 us: params_of(): bias_hidden[layer_index]]
    unnamed x13 -> x11, local copies, waits for them, and re-layouts: 0.73 us -> 1.98 us
    div x9 -> x0, other arithmetic: 1.1 us -> none  [the longest x1 1.06 us: switch_unit(): jax.nn.sigmoid(gate_logit) * paired]
  transfers between devices with their start and end apart: 1 -> 1, of which waited for: 1 -> 1; matrix products, arithmetic and copies ran while one was open for 4% -> 7% of each run, Pallas kernels for 0% -> 0%
where the time goes in v1:
time: 51.9 us; the launch traced here: 51.6 us
  blocking collectives  28.2 us (54%)
  Pallas kernels  11.2 us (22%)
  starting transfers between devices  4.21 us (8%)
  other arithmetic  3.48 us (7%)
  waiting for transfers between devices  2.49 us (5%)
  local copies, waits for them, and re-layouts  2.02 us (4%)
    all_to_all x2, blocking collectives, all_to_all(): return lax.all_to_all(x, axes, split_axis=0, concat_axis=0, tiled=True)  28.2 us
    pallas_call x2, Pallas kernels, run_layers(): pl.pallas_call(kernel, out_shape=jax.ShapeDtypeStruct((rows, width), jnp....  11.2 us
    all_to_all x1, starting transfers between devices, all_to_all(): return lax.all_to_all(x, axes, split_axis=0, concat_axis=0, tiled=True)  4.21 us
    convert_element_type x2, other arithmetic, parts(): return (high.astype(jnp.bfloat16), (w - high).astype(jnp.bfloat16))  3.48 us
    all_to_all x1, waiting for transfers between devices, all_to_all(): return lax.all_to_all(x, axes, split_axis=0, concat_axis=0, tiled=True)  2.49 us
    unnamed x11, local copies, waits for them, and re-layouts  1.98 us
  transfers between devices with their start and end apart: 1, of which 1 were waited for; matrix products, arithmetic and copies ran while one was open for 7% of the time, Pallas kernels for 0%

profile of v1, /device:TPU:0, one launch (start us, length us, event | category | flops | bytes accessed | tf_op | source)
XLA Modules:
  0.0 51.6 jit_solution(7843919003030802813)
XLA Ops:
  0.0 4.2 %all-to-all-start = ((f32[4,64,256]{2,1,0:T(8,128)}), f32[4,64,256]{2,1,0:T(8,128)S(1)}, u32[]{:S(2)}, u32[]{:S(2)}) async-start(f32[4,64,256]{2,1,0:T(8,128)} %bitcast.21), calls=%async_computation | async-start | bytes 524288 | tf_op jit(solution)/shard_map/all_to_all | solution.py:98
  4.2 0.0 copy-start.4
  4.2 2.2 %fusion = (bf16[512,1024]{1,0:T(8,128)(2,1)S(1)}, bf16[512,1024]{1,0:T(8,128)(2,1)S(1)}) fusion(f32[512,1024]{1,0:T(8,128)} %param.10), kind=kLoop, calls=%fused_computation.4 | loop fusion | flops 2097152 | bytes 4194304 | tf_op jit(solution)/shard_map/convert_element_type | solution.py:111
  6.4 0.0 copy-done.4
  6.4 0.0 copy-start.1
  6.4 0.0 copy-start.2
  6.4 0.0 copy-start.3
  6.4 1.3 %fusion.1 = (bf16[1024,512]{1,0:T(8,128)(2,1)S(1)}, bf16[1024,512]{1,0:T(8,128)(2,1)}) fusion(f32[1024,512]{1,0:T(8,128)S(1)} %copy-done.4), kind=kLoop, calls=%fused_computation.5 | loop fusion | flops 2097152 | bytes 4194304 | tf_op jit(solution)/shard_map/convert_element_type | solution.py:111
  7.8 2.5 %all-to-all-done = f32[4,64,256]{2,1,0:T(8,128)S(1)} async-done(((f32[4,64,256]{2,1,0:T(8,128)}), f32[4,64,256]{2,1,0:T(8,128)S(1)}, u32[]{:S(2)}, u32[]{:S(2)}) %all-to-all-start) | async-done | bytes 262176 | tf_op jit(solution)/shard_map/all_to_all | solution.py:98
  10.2 0.0 copy-done.1
  10.2 0.0 copy-done.2
  10.3 0.0 copy-done.3
  10.3 0.0 copy-start
  10.3 1.2 %copy-done = bf16[1024,512]{1,0:T(8,128)(2,1)S(1)} copy-done((bf16[1024,512]{1,0:T(8,128)(2,1)S(1)}, bf16[1024,512]{1,0:T(8,128)(2,1)}, u32[]{:S(2)}) %copy-start) | copy-done | bytes 1048600
  11.5 5.6 %high_layers.1 = f32[256,256]{1,0:T(8,128)S(1)} custom-call(f32[256,256]{1,0:T(8,128)S(1)} %bitcast.14, f32[8,512]{1,0:T(8,128)S(1)} %copy-done.2, f32[8,1024]{1,0:T(8,128)S(1)} %copy-done.1, f32[8,512]{1,0:T(8,128)S(1)} %copy-done.3, bf16[512,1024]{1,0:T(8,128)(2,1)S(1)} %get-tuple-element.8.in_high_ref, bf16[512,1024]{1,0:T(8,128)(2,1)S(1)} %get-tuple-element.7.in_low_ref, ...), custom_call_target="tpu_custom_call" | custom-call | tf_op jit(solution)/shard_map/high_layers/pallas_call | solution.py:83
  17.1 15.0 %all_to_all.34 = f32[8,32,256]{2,1,0:T(8,128)S(1)} all-to-all(f32[8,32,256]{2,1,0:T(8,128)S(1)} %bitcast.18), channel_id=1, replica_groups=mesh['seqhi'=4,'seqlo'=8] {'seqlo'}, dimensions={0} | all-to-all | bytes 524288 | tf_op jit(solution)/shard_map/all_to_all | solution.py:98
  32.1 5.6 %low_layers.1 = f32[256,256]{1,0:T(8,128)S(1)} custom-call(f32[256,256]{1,0:T(8,128)S(1)} %bitcast.15, f32[8,512]{1,0:T(8,128)S(1)} %copy-done.2, f32[8,1024]{1,0:T(8,128)S(1)} %copy-done.1, f32[8,512]{1,0:T(8,128)S(1)} %copy-done.3, bf16[512,1024]{1,0:T(8,128)(2,1)S(1)} %get-tuple-element.8.in_high_ref, bf16[512,1024]{1,0:T(8,128)(2,1)S(1)} %get-tuple-element.7.in_low_ref, ...), custom_call_target="tpu_custom_call" | custom-call | tf_op jit(solution)/shard_map/low_layers/pallas_call | solution.py:83
  37.7 13.2 %all_to_all.35 = f32[32,8,256]{2,1,0:T(8,128)S(1)} all-to-all(f32[32,8,256]{2,1,0:T(8,128)S(1)} %bitcast.19), channel_id=1, replica_groups=mesh['seqhi'=4,'seqlo'=8] {'seqhi','seqlo'}, dimensions={0} | all-to-all | bytes 524288 | tf_op jit(solution)/shard_map/all_to_all | solution.py:98
  50.9 0.7 %copy.13 = f32[256,256]{1,0:T(8,128)} copy(f32[256,256]{1,0:T(8,128)S(1)} %bitcast.20) | data formatting | bytes 524288
  (2 shorter events, 0.0 us)
Async XLA Ops:
  0.0 10.2 %all-to-all-start = ((f32[4,64,256]{2,1,0:T(8,128)}), f32[4,64,256]{2,1,0:T(8,128)S(1)}, u32[]{:S(2)}, u32[]{:S(2)}) async-start(f32[4,64,256]{2,1,0:T(8,128)} %bitcast.21), calls=%async_computation | async-start | bytes 524288 | tf_op jit(solution)/shard_map/all_to_all | solution.py:98
  4.2 2.2 %copy-start.4 = (f32[1024,512]{1,0:T(8,128)S(1)}, f32[1024,512]{1,0:T(8,128)}, u32[]{:S(2)}) copy-start(f32[1024,512]{1,0:T(8,128)} %param.11) | copy-start | bytes 6291460
  6.4 3.8 %copy-start.1 = (f32[8,1024]{1,0:T(8,128)S(1)}, f32[8,1024]{1,0:T(8,128)}, u32[]{:S(2)}) copy-start(f32[8,1024]{1,0:T(8,128)} %bias_ref.3) | copy-start | bytes 98308
  6.4 3.8 %copy-start.2 = (f32[8,512]{1,0:T(8,128)S(1)}, f32[8,512]{1,0:T(8,128)}, u32[]{:S(2)}) copy-start(f32[8,512]{1,0:T(8,128)} %gain_ref.3) | copy-start | bytes 49156
  6.4 3.8 %copy-start.3 = (f32[8,512]{1,0:T(8,128)S(1)}, f32[8,512]{1,0:T(8,128)}, u32[]{:S(2)}) copy-start(f32[8,512]{1,0:T(8,128)} %gate_ref.3) | copy-start | bytes 49156
  10.3 1.2 %copy-start = (bf16[1024,512]{1,0:T(8,128)(2,1)S(1)}, bf16[1024,512]{1,0:T(8,128)(2,1)}, u32[]{:S(2)}) copy-start(bf16[1024,512]{1,0:T(8,128)(2,1)} %get-tuple-element.6.out_high_ref) | copy-start | bytes 3145732

commit v2 on v1

--- a/solution.py
+++ b/solution.py
@@ -11,6 +11,8 @@
 NORM_EPS = 1e-05
 GELU_SCALE = 0.7978845608028654
 GELU_CUBE = 0.044715
+AXES = ("seqhi", "seqlo")
+VMEM = pl.BlockSpec(memory_space=pltpu.VMEM)
 
 
 def split_high_low(x):
@@ -49,12 +51,20 @@
     return out[:, :width], out[:, width:]
 
 
-def layers_kernel(
-    first, distances, hidden_block,
-    x_ref, gain_ref, bias_ref, gate_ref, in_high_ref, in_low_ref, out_high_ref, out_low_ref, y_ref,
-):
-    rows, width = x_ref.shape
-    states = x_ref[...]
+def layers_kernel(first, distances, hidden_block, axis, chunks_out, send_from, *refs):
+    chunks_in = lax.axis_size(axis)
+    x_refs = refs[:chunks_in]
+    gain_ref, bias_ref, gate_ref, in_high_ref, in_low_ref, out_high_ref, out_low_ref = refs[
+        chunks_in : chunks_in + 7
+    ]
+    y_refs = refs[chunks_in + 7 : -2]
+    arrived, leaving = refs[-2:]
+    me = lax.axis_index(axis)
+    for step, x_ref in enumerate(x_refs):
+        arrived[me ^ step] = x_ref[...]
+    count, chunk, width = arrived.shape
+    rows = count * chunk
+    states = arrived[...].reshape(rows, width)
     for step, distance in enumerate(distances):
         k = first + step
         groups = rows // (2 * distance)
@@ -73,29 +83,74 @@
         states = jnp.concatenate(
             [new_lower.reshape(shape), new_upper.reshape(shape)], axis=1
         ).reshape(rows, width)
-    y_ref[...] = states.reshape(y_ref.shape)
-
-
-def run_layers(states, first, distances, params, name):
-    rows, width = states.shape
+    leaving[...] = states.reshape(leaving.shape)
+    first_chunk = send_from()
+    for step, y_ref in enumerate(y_refs):
+        y_ref[...] = leaving[first_chunk ^ step]
+
+
+def run_layers(chunks, first, distances, axis, chunks_out, send_from, params, name):
+    chunk, width = chunks[0].shape
+    rows = chunk * len(chunks)
     hidden = params[1].shape[1]
-    kernel = functools.partial(layers_kernel, first, distances, min(hidden, 256))
+    kernel = functools.partial(
+        layers_kernel, first, distances, min(hidden, 256), axis, chunks_out, send_from
+    )
     return pl.pallas_call(
         kernel,
-        out_shape=jax.ShapeDtypeStruct((rows, width), jnp.float32),
-        in_specs=[pl.BlockSpec(memory_space=pltpu.VMEM)] * 8,
-        out_specs=pl.BlockSpec(memory_space=pltpu.VMEM),
+        out_shape=[jax.ShapeDtypeStruct((rows // chunks_out, width), jnp.float32)] * chunks_out,
+        in_specs=[VMEM] * (len(chunks) + 7),
+        out_specs=[VMEM] * chunks_out,
+        scratch_shapes=[
+            pltpu.VMEM((len(chunks), chunk, width), jnp.float32),
+            pltpu.VMEM((chunks_out, rows // chunks_out, width), jnp.float32),
+        ],
         compiler_params=pltpu.CompilerParams(vmem_limit_bytes=24 * 2**20),
         name=name,
-    )(states, *params)
-
-
-def swap_leading(x, a, b):
-    return x.reshape(a, b, -1, x.shape[-1]).swapaxes(0, 1).reshape(x.shape)
-
-
-def all_to_all(x, axes):
-    return lax.all_to_all(x, axes, split_axis=0, concat_axis=0, tiled=True)
+    )(*chunks, *params)
+
+
+def take_apart_kernel(axis, x_ref, *y_refs):
+    me = lax.axis_index(axis)
+    for step, y_ref in enumerate(y_refs):
+        y_ref[...] = x_ref[me ^ step]
+
+
+def take_apart(x, axis, count):
+    rows, width = x.shape
+    return pl.pallas_call(
+        functools.partial(take_apart_kernel, axis),
+        out_shape=[jax.ShapeDtypeStruct((rows // count, width), jnp.float32)] * count,
+        in_specs=[VMEM],
+        out_specs=[VMEM] * count,
+        name="take_apart",
+    )(x.reshape(count, rows // count, width))
+
+
+def put_together_kernel(axis, *refs):
+    me = lax.axis_index(axis)
+    y_ref = refs[-1]
+    for step, x_ref in enumerate(refs[:-1]):
+        y_ref[me ^ step] = x_ref[...]
+
+
+def put_together(chunks, axis):
+    chunk, width = chunks[0].shape
+    return pl.pallas_call(
+        functools.partial(put_together_kernel, axis),
+        out_shape=jax.ShapeDtypeStruct((len(chunks), chunk, width), jnp.float32),
+        in_specs=[VMEM] * len(chunks),
+        out_specs=VMEM,
+        name="put_together",
+    )(*chunks).reshape(-1, width)
+
+
+def exchange(chunks, axis):
+    count = len(chunks)
+    return [chunks[0]] + [
+        lax.ppermute(chunks[step], axis, [(i, i ^ step) for i in range(count)])
+        for step in range(1, count)
+    ]
 
 
 def body(features, norm_gain, bias_hidden, gate_logit, w_in, w_out):
@@ -105,6 +160,7 @@
     high_bits = high_count.bit_length() - 1
     low_bits = low_count.bit_length() - 1
     layer_total = norm_gain.shape[0]
+    spare = low_count // high_count
 
     def parts(w):
         high = lax.reduce_precision(w, exponent_bits=8, mantissa_bits=7)
@@ -114,22 +170,34 @@
     high_distances = [rows // high_count * 2 ** (k % high_bits) for k in range(HI_LAYERS)]
     low_distances = [rows // low_count * 2 ** (j % low_bits) for j in range(layer_total - HI_LAYERS)]
 
-    states = all_to_all(features, "seqhi")
-    states = run_layers(states, 0, high_distances, params, "high_layers")
-    if rows % (8 * high_count * low_count) == 0:
-        states = swap_leading(states, high_count, low_count)
-        states = all_to_all(states, "seqlo")
-        states = run_layers(states, HI_LAYERS, low_distances, params, "low_layers")
-        states = swap_leading(states, low_count, high_count)
-        return all_to_all(states, ("seqhi", "seqlo"))
-    states = all_to_all(states, "seqhi")
-    states = all_to_all(states, "seqlo")
-    states = run_layers(states, HI_LAYERS, low_distances, params, "low_layers")
-    return all_to_all(states, "seqlo")
+    def low_index():
+        return lax.axis_index("seqlo")
+
+    def row_index():
+        return lax.axis_index("seqhi") * spare + lax.rem(lax.axis_index("seqlo"), spare)
+
+    chunks = exchange(take_apart(features, "seqhi", high_count), "seqhi")
+    chunks = run_layers(
+        chunks, 0, high_distances, "seqhi", low_count, low_index, params, "high_layers"
+    )
+    chunks = exchange(chunks, "seqlo")
+    chunks = run_layers(
+        chunks, HI_LAYERS, low_distances, "seqlo", low_count, row_index, params, "low_layers"
+    )
+    home = []
+    for step in range(low_count):
+        pairs = []
+        for high in range(high_count):
+            for low in range(low_count):
+                block = high * spare + low % spare
+                target = (low // spare) * low_count + (block ^ step)
+                pairs.append((high * low_count + low, target))
+        home.append(lax.ppermute(chunks[step], AXES, pairs))
+    return put_together(home, "seqlo")
 
 
 def solution(mesh):
-    placed = (P(("seqhi", "seqlo"), None), P(), P(), P(), P(), P())
+    placed = (P(AXES, None), P(), P(), P(), P(), P())
     return jax.shard_map(
-        body, mesh=mesh, in_specs=placed, out_specs=P(("seqhi", "seqlo"), None), check_vma=False
-    )
+        body, mesh=mesh, in_specs=placed, out_specs=P(AXES, None), check_vma=False
+    )

time: 51.9 us -> 57.3 us (1.10)
  blocking collectives: 28.2 us -> 0 us
  starting transfers between devices: 4.21 us -> 29.2 us
  waiting for transfers between devices: 2.49 us -> 10 us
  Pallas kernels: 11.2 us -> 14.5 us
  local copies, waits for them, and re-layouts: 2.02 us -> 0.65 us
  other arithmetic: 3.48 us -> 2.5 us
    ppermute x0 -> x18, starting transfers between devices: none -> 29.2 us  [the longest x8 15 us: body(): home.append(lax.ppermute(chunks[step], AXES, pairs))]
    all_to_all x2 -> x0, blocking collectives: 28.2 us -> none  [all_to_all(): return lax.all_to_all(x, axes, split_axis=0, concat_axis=0, tiled=True)]
    ppermute x0 -> x18, waiting for transfers between devices: none -> 10 us  [the longest x10 8.06 us: exchange(): lax.ppermute(chunks[step], axis, [(i, i ^ step) for i in range(count)])]
    all_to_all x1 -> x0, starting transfers between devices: 4.21 us -> none  [all_to_all(): return lax.all_to_all(x, axes, split_axis=0, concat_axis=0, tiled=True)]
    pallas_call x2 -> x4, Pallas kernels: 11.2 us -> 14.5 us  [the longest x2 11.2 us: run_layers(): pl.pallas_call(kernel, out_shape=[jax.ShapeDtypeStruct((rows // chunks_ou...]
    all_to_all x1 -> x0, waiting for transfers between devices: 2.49 us -> none  [all_to_all(): return lax.all_to_all(x, axes, split_axis=0, concat_axis=0, tiled=True)]
    unnamed x11 -> x26, local copies, waits for them, and re-layouts: 1.98 us -> 0.65 us
    convert_element_type x2, other arithmetic: 3.48 us -> 2.5 us  [parts(): return (high.astype(jnp.bfloat16), (w - high).astype(jnp.bfloat16))]
  transfers between devices with their start and end apart: 1 -> 18, of which waited for: 1 -> 6; matrix products, arithmetic and copies ran while one was open for 7% -> 4% of each run, Pallas kernels for 0% -> 0%
where the time goes in v2:
time: 57.3 us; the launch traced here: 57.1 us
  starting transfers between devices  29.2 us (51%)
  Pallas kernels  14.5 us (25%)
  waiting for transfers between devices  10 us (17%)
  other arithmetic  2.5 us (4%)
  local copies, waits for them, and re-layouts  0.65 us (1%)
    ppermute x8, starting transfers between devices, body(): home.append(lax.ppermute(chunks[step], AXES, pairs))  15 us
    ppermute x10, starting transfers between devices, exchange(): lax.ppermute(chunks[step], axis, [(i, i ^ step) for i in range(count)])  14.3 us
    pallas_call x2, Pallas kernels, run_layers(): pl.pallas_call(kernel, out_shape=[jax.ShapeDtypeStruct((rows // chunks_ou...  11.2 us
    ppermute x10, waiting for transfers between devices, exchange(): lax.ppermute(chunks[step], axis, [(i, i ^ step) for i in range(count)])  8.06 us
    convert_element_type x2, other arithmetic, parts(): return (high.astype(jnp.bfloat16), (w - high).astype(jnp.bfloat16))  2.5 us
    ppermute x8, waiting for transfers between devices, body(): home.append(lax.ppermute(chunks[step], AXES, pairs))  1.97 us
    pallas_call x1, Pallas kernels, take_apart(): pl.pallas_call(functools.partial(take_apart_kernel, axis), out_shape=[jax...  1.65 us
    pallas_call x1, Pallas kernels, put_together(): pl.pallas_call(functools.partial(put_together_kernel, axis), out_shape=ja...  1.6 us
  transfers between devices with their start and end apart: 18, of which 6 were waited for; matrix products, arithmetic and copies ran while one was open for 4% of the time, Pallas kernels for 0%

profile of v2, /device:TPU:0, one launch (start us, length us, event | category | flops | bytes accessed | tf_op | source)
XLA Modules:
  0.0 57.1 jit_solution(11918049794425262857)
XLA Ops:
  0.0 1.6 %take_apart.1 = (f32[64,256]{1,0:T(8,128)}, f32[64,256]{1,0:T(8,128)}, f32[64,256]{1,0:T(8,128)}, f32[64,256]{1,0:T(8,128)}) custom-call(f32[4,64,256]{2,1,0:T(8,128)} %bitcast.2), custom_call_target="tpu_custom_call" | custom-call | tf_op jit(solution)/shard_map/take_apart/pallas_call | solution.py:121
  1.6 0.5 collective-permute-start
  2.1 2.5 %collective-permute-start.1 = (f32[64,256]{1,0:T(8,128)}, f32[64,256]{1,0:T(8,128)S(1)}, u32[]{:S(2)}, u32[]{:S(2)}) collective-permute-start(f32[64,256]{1,0:T(8,128)} %get-tuple-element.27), channel_id=1, source_target_pairs={{0,16},{8,24},{16,0},{24,8},{1,17},{9,25},{17,1},{25,9},{2,18},{10... | collective-permute-start | bytes 196616 | tf_op jit(solution)/shard_map/ppermute | solution.py:151
  4.6 0.0 copy-start.4
  4.6 0.1 collective-permute-start.2
  4.7 2.1 %fusion = (bf16[512,1024]{1,0:T(8,128)(2,1)S(1)}, bf16[512,1024]{1,0:T(8,128)(2,1)S(1)}) fusion(f32[512,1024]{1,0:T(8,128)} %param.10), kind=kLoop, calls=%fused_computation.4 | loop fusion | flops 2097152 | bytes 4194304 | tf_op jit(solution)/shard_map/convert_element_type | solution.py:167
  6.9 0.0 copy-done.4
  6.9 0.0 copy-start
  6.9 0.0 copy-start.1
  6.9 0.0 copy-start.2
  6.9 0.0 copy-start.3
  6.9 0.4 fusion.1
  7.3 0.0 collective-permute-done.refs_1_
  7.3 0.2 collective-permute-done.1.refs_2_
  7.6 1.3 %collective-permute-done.2.refs_3_ = f32[64,256]{1,0:T(8,128)S(1)} collective-permute-done((f32[64,256]{1,0:T(8,128)}, f32[64,256]{1,0:T(8,128)S(1)}, u32[]{:S(2)}, u32[]{:S(2)}) %collective-permute-start.2) | collective-permute-done | bytes 65568 | tf_op jit(solution)/shard_map/ppermute | solution.py:151
  8.9 0.0 copy-done
  8.9 0.0 copy-done.1
  8.9 0.0 copy-done.2
  8.9 0.0 copy-done.3
  8.9 5.6 %high_layers.1 = (f32[32,256]{1,0:T(8,128)S(1)}, f32[32,256]{1,0:T(8,128)S(1)}, f32[32,256]{1,0:T(8,128)S(1)}, f32[32,256]{1,0:T(8,128)S(1)}, f32[32,256]{1,0:T(...) custom-call(f32[64,256]{1,0:T(8,128)S(1)} %copy-done.1, ...), custom_call_target="tpu_custom_call" | custom-call | tf_op jit(solution)/shard_map/high_layers/pallas_call | solution.py:99
  14.5 1.7 %collective-permute-start.3 = (f32[32,256]{1,0:T(8,128)S(1)}, f32[32,256]{1,0:T(8,128)S(1)}, u32[]{:S(2)}, u32[]{:S(2)}) collective-permute-start(f32[32,256]{1,0:T(8,128)S(1)} %get-tuple-element.30), channel_id=1, source_target_pairs={{0,1},{1,0},{2,3},{3,2},{4,5},{5,4},{6,7},{7,6},{8,9},{9,8},{10,11... | collective-permute-start | bytes 98312 | tf_op jit(solution)/shard_map/ppermute | solution.py:151
  16.2 1.6 %collective-permute-start.4 = (f32[32,256]{1,0:T(8,128)S(1)}, f32[32,256]{1,0:T(8,128)S(1)}, u32[]{:S(2)}, u32[]{:S(2)}) collective-permute-start(f32[32,256]{1,0:T(8,128)S(1)} %get-tuple-element.31), channel_id=1, source_target_pairs={{0,2},{1,3},{2,0},{3,1},{4,6},{5,7},{6,4},{7,5},{8,10},{9,11},{10,... | collective-permute-start | bytes 98312 | tf_op jit(solution)/shard_map/ppermute | solution.py:151
  17.7 0.3 collective-permute-start.5
  18.1 2.7 %collective-permute-start.6 = (f32[32,256]{1,0:T(8,128)S(1)}, f32[32,256]{1,0:T(8,128)S(1)}, u32[]{:S(2)}, u32[]{:S(2)}) collective-permute-start(f32[32,256]{1,0:T(8,128)S(1)} %get-tuple-element.33), channel_id=1, source_target_pairs={{0,4},{1,5},{2,6},{3,7},{4,0},{5,1},{6,2},{7,3},{8,12},{9,13},{10,... | collective-permute-start | bytes 98312 | tf_op jit(solution)/shard_map/ppermute | solution.py:151
  20.7 1.3 %collective-permute-start.7 = (f32[32,256]{1,0:T(8,128)S(1)}, f32[32,256]{1,0:T(8,128)S(1)}, u32[]{:S(2)}, u32[]{:S(2)}) collective-permute-start(f32[32,256]{1,0:T(8,128)S(1)} %get-tuple-element.34), channel_id=1, source_target_pairs={{0,5},{1,4},{2,7},{3,6},{4,1},{5,0},{6,3},{7,2},{8,13},{9,12},{10,... | collective-permute-start | bytes 98312 | tf_op jit(solution)/shard_map/ppermute | solution.py:151
  22.0 0.0 collective-permute-done.3.refs_1_
  22.0 3.6 %collective-permute-start.8 = (f32[32,256]{1,0:T(8,128)S(1)}, f32[32,256]{1,0:T(8,128)S(1)}, u32[]{:S(2)}, u32[]{:S(2)}) collective-permute-start(f32[32,256]{1,0:T(8,128)S(1)} %get-tuple-element.35), channel_id=1, source_target_pairs={{0,6},{1,7},{2,4},{3,5},{4,2},{5,3},{6,0},{7,1},{8,14},{9,15},{10,... | collective-permute-start | bytes 98312 | tf_op jit(solution)/shard_map/ppermute | solution.py:151
  25.6 0.0 collective-permute-done.4.refs_2_
  25.6 0.1 collective-permute-start.9
  25.7 0.0 collective-permute-done.5.refs_3_
  25.7 0.0 collective-permute-done.6.refs_4_
  25.7 0.7 %collective-permute-done.7.refs_5_ = f32[32,256]{1,0:T(8,128)S(1)} collective-permute-done((f32[32,256]{1,0:T(8,128)S(1)}, f32[32,256]{1,0:T(8,128)S(1)}, u32[]{:S(2)}, u32[]{:S(2)}) %collective-permute-start.7) | collective-permute-done | bytes 32800 | tf_op jit(solution)/shard_map/ppermute | solution.py:151
  26.4 1.4 %collective-permute-done.8.refs_6_ = f32[32,256]{1,0:T(8,128)S(1)} collective-permute-done((f32[32,256]{1,0:T(8,128)S(1)}, f32[32,256]{1,0:T(8,128)S(1)}, u32[]{:S(2)}, u32[]{:S(2)}) %collective-permute-start.8) | collective-permute-done | bytes 32800 | tf_op jit(solution)/shard_map/ppermute | solution.py:151
  27.9 4.4 %collective-permute-done.9.refs_7_ = f32[32,256]{1,0:T(8,128)S(1)} collective-permute-done((f32[32,256]{1,0:T(8,128)S(1)}, f32[32,256]{1,0:T(8,128)S(1)}, u32[]{:S(2)}, u32[]{:S(2)}) %collective-permute-start.9) | collective-permute-done | bytes 32800 | tf_op jit(solution)/shard_map/ppermute | solution.py:151
  32.2 5.6 %low_layers.1 = (f32[32,256]{1,0:T(8,128)S(1)}, f32[32,256]{1,0:T(8,128)S(1)}, f32[32,256]{1,0:T(8,128)S(1)}, f32[32,256]{1,0:T(8,128)S(1)}, f32[32,256]{1,0:T(8...) custom-call(f32[32,256]{1,0:T(8,128)S(1)} %get-tuple-element.29.refs_0_, ...), custom_call_target="tpu_custom_call" | custom-call | tf_op jit(solution)/shard_map/low_layers/pallas_call | solution.py:99
  37.9 0.7 %collective-permute-start.10 = (f32[32,256]{1,0:T(8,128)S(1)}, f32[32,256]{1,0:T(8,128)S(1)}, u32[]{:S(2)}, u32[]{:S(2)}) collective-permute-start(f32[32,256]{1,0:T(8,128)S(1)} %get-tuple-element.37), channel_id=1, source_target_pairs={{0,0},{1,1},{2,8},{3,9},{4,16},{5,17},{6,24},{7,25},{8,2},{9,3},{1... | collective-permute-start | bytes 98312 | tf_op jit(solution)/shard_map/ppermute | solution.py:195
  38.5 0.6 collective-permute-start.11
  39.1 0.2 collective-permute-start.12
  39.3 1.0 %collective-permute-start.13 = (f32[32,256]{1,0:T(8,128)S(1)}, f32[32,256]{1,0:T(8,128)S(1)}, u32[]{:S(2)}, u32[]{:S(2)}) collective-permute-start(f32[32,256]{1,0:T(8,128)S(1)} %get-tuple-element.40), channel_id=1, source_target_pairs={{0,3},{1,2},{2,11},{3,10},{4,19},{5,18},{6,27},{7,26},{8,1},{9,0},... | collective-permute-start | bytes 98312 | tf_op jit(solution)/shard_map/ppermute | solution.py:195
  40.3 3.9 %collective-permute-start.14 = (f32[32,256]{1,0:T(8,128)S(1)}, f32[32,256]{1,0:T(8,128)S(1)}, u32[]{:S(2)}, u32[]{:S(2)}) collective-permute-start(f32[32,256]{1,0:T(8,128)S(1)} %get-tuple-element.41), channel_id=1, source_target_pairs={{0,4},{1,5},{2,12},{3,13},{4,20},{5,21},{6,28},{7,29},{8,6},{9,7},... | collective-permute-start | bytes 98312 | tf_op jit(solution)/shard_map/ppermute | solution.py:195
  44.2 0.0 collective-permute-done.10.refs_0_
  44.2 1.5 %collective-permute-start.15 = (f32[32,256]{1,0:T(8,128)S(1)}, f32[32,256]{1,0:T(8,128)S(1)}, u32[]{:S(2)}, u32[]{:S(2)}) collective-permute-start(f32[32,256]{1,0:T(8,128)S(1)} %get-tuple-element.42), channel_id=1, source_target_pairs={{0,5},{1,4},{2,13},{3,12},{4,21},{5,20},{6,29},{7,28},{8,7},{9,6},... | collective-permute-start | bytes 98312 | tf_op jit(solution)/shard_map/ppermute | solution.py:195
  45.7 0.0 collective-permute-done.11.refs_1_
  45.7 4.9 %collective-permute-start.16 = (f32[32,256]{1,0:T(8,128)S(1)}, f32[32,256]{1,0:T(8,128)S(1)}, u32[]{:S(2)}, u32[]{:S(2)}) collective-permute-start(f32[32,256]{1,0:T(8,128)S(1)} %get-tuple-element.43), channel_id=1, source_target_pairs={{0,6},{1,7},{2,14},{3,15},{4,22},{5,23},{6,30},{7,31},{8,4},{9,5},... | collective-permute-start | bytes 98312 | tf_op jit(solution)/shard_map/ppermute | solution.py:195
  50.6 0.0 collective-permute-done.12.refs_2_
  50.6 2.2 %collective-permute-start.17 = (f32[32,256]{1,0:T(8,128)S(1)}, f32[32,256]{1,0:T(8,128)S(1)}, u32[]{:S(2)}, u32[]{:S(2)}) collective-permute-start(f32[32,256]{1,0:T(8,128)S(1)} %get-tuple-element.44), channel_id=1, source_target_pairs={{0,7},{1,6},{2,15},{3,14},{4,23},{5,22},{6,31},{7,30},{8,5},{9,4},... | collective-permute-start | bytes 98312 | tf_op jit(solution)/shard_map/ppermute | solution.py:195
  52.9 0.0 collective-permute-done.13.refs_3_
  52.9 0.0 collective-permute-done.14.refs_4_
  52.9 0.0 copy-start.9
  52.9 0.0 collective-permute-done.15.refs_5_
  52.9 0.0 copy-start.10
  52.9 0.0 collective-permute-done.16.refs_6_
  52.9 0.0 copy-start.11
  52.9 1.9 %collective-permute-done.17.refs_7_ = f32[32,256]{1,0:T(8,128)S(1)} collective-permute-done((f32[32,256]{1,0:T(8,128)S(1)}, f32[32,256]{1,0:T(8,128)S(1)}, u32[]{:S(2)}, u32[]{:S(2)}) %collective-permute-start.17) | collective-permute-done | bytes 32800 | tf_op jit(solution)/shard_map/ppermute | solution.py:195
  54.9 0.0 copy-done.5
  54.9 0.0 copy-done.6
  54.9 0.0 copy-done.7
  54.9 0.0 copy-done.8
  54.9 0.0 copy-done.9
  54.9 0.0 copy-done.10
  54.9 0.0 copy-done.11
  54.9 0.0 copy-start.12
  54.9 0.6 %copy-done.12 = f32[32,256]{1,0:T(8,128)} copy-done((f32[32,256]{1,0:T(8,128)}, f32[32,256]{1,0:T(8,128)S(1)}, u32[]{:S(2)}) %copy-start.12) | copy-done | bytes 32792
  55.5 1.6 %put_together.1 = f32[8,32,256]{2,1,0:T(8,128)} custom-call(f32[32,256]{1,0:T(8,128)} %copy-done.5, f32[32,256]{1,0:T(8,128)} %copy-done.6, f32[32,256]{1,0:T(8,128)} %copy-done.7, f32[32,256]{1,0:T(8,128)} %copy-done.8, f32[32,256]{1,0:T(8,128)} %copy-done.9, f32[32,256]{1,0:T(8,128)} %copy-done.10, f32[32,256]{1,0:T(8,128)} %copy-done.11, f32[32,256]{1,0:T(8,128)} %copy-done.12), custom_call_target="tpu_custom_call" | custom-call | tf_op jit(solution)/shard_map/put_together/pallas_call | solution.py:139
  (4 shorter events, 0.0 us)
Async XLA Ops:
  1.6 5.7 %collective-permute-start = (f32[64,256]{1,0:T(8,128)}, f32[64,256]{1,0:T(8,128)S(1)}, u32[]{:S(2)}, u32[]{:S(2)}) collective-permute-start(f32[64,256]{1,0:T(8,128)} %get-tuple-element.26), channel_id=1, source_target_pairs={{0,8},{8,0},{16,24},{24,16},{1,9},{9,1},{17,25},{25,17},{2,10},{10... | collective-permute-start | bytes 196616 | tf_op jit(solution)/shard_map/ppermute | solution.py:151
  2.1 5.5 %collective-permute-start.1 = (f32[64,256]{1,0:T(8,128)}, f32[64,256]{1,0:T(8,128)S(1)}, u32[]{:S(2)}, u32[]{:S(2)}) collective-permute-start(f32[64,256]{1,0:T(8,128)} %get-tuple-element.27), channel_id=1, source_target_pairs={{0,16},{8,24},{16,0},{24,8},{1,17},{9,25},{17,1},{25,9},{2,18},{10... | collective-permute-start | bytes 196616 | tf_op jit(solution)/shard_map/ppermute | solution.py:151
  4.6 2.3 %copy-start.4 = (f32[1024,512]{1,0:T(8,128)S(1)}, f32[1024,512]{1,0:T(8,128)}, u32[]{:S(2)}) copy-start(f32[1024,512]{1,0:T(8,128)} %param.11) | copy-start | bytes 6291460
  4.6 4.3 %collective-permute-start.2 = (f32[64,256]{1,0:T(8,128)}, f32[64,256]{1,0:T(8,128)S(1)}, u32[]{:S(2)}, u32[]{:S(2)}) collective-permute-start(f32[64,256]{1,0:T(8,128)} %get-tuple-element.28), channel_id=1, source_target_pairs={{0,24},{8,16},{16,8},{24,0},{1,25},{9,17},{17,9},{25,1},{2,26},{10... | collective-permute-start | bytes 196616 | tf_op jit(solution)/shard_map/ppermute | solution.py:151
  6.9 2.0 %copy-start = (f32[8,1024]{1,0:T(8,128)S(1)}, f32[8,1024]{1,0:T(8,128)}, u32[]{:S(2)}) copy-start(f32[8,1024]{1,0:T(8,128)} %refs_9_.1) | copy-start | bytes 98308
  6.9 2.0 %copy-start.1 = (f32[64,256]{1,0:T(8,128)S(1)}, f32[64,256]{1,0:T(8,128)}, u32[]{:S(2)}) copy-start(f32[64,256]{1,0:T(8,128)} %get-tuple-element.25.refs_0_) | copy-start | bytes 196612
  6.9 1.9 %copy-start.2 = (f32[8,512]{1,0:T(8,128)S(1)}, f32[8,512]{1,0:T(8,128)}, u32[]{:S(2)}) copy-start(f32[8,512]{1,0:T(8,128)} %refs_8_.1) | copy-start | bytes 49156
  6.9 1.9 %copy-start.3 = (f32[8,512]{1,0:T(8,128)S(1)}, f32[8,512]{1,0:T(8,128)}, u32[]{:S(2)}) copy-start(f32[8,512]{1,0:T(8,128)} %refs_10_.1) | copy-start | bytes 49156
  14.5 7.5 %collective-permute-start.3 = (f32[32,256]{1,0:T(8,128)S(1)}, f32[32,256]{1,0:T(8,128)S(1)}, u32[]{:S(2)}, u32[]{:S(2)}) collective-permute-start(f32[32,256]{1,0:T(8,128)S(1)} %get-tuple-element.30), channel_id=1, source_target_pairs={{0,1},{1,0},{2,3},{3,2},{4,5},{5,4},{6,7},{7,6},{8,9},{9,8},{10,11... | collective-permute-start | bytes 98312 | tf_op jit(solution)/shard_map/ppermute | solution.py:151
  16.2 9.5 %collective-permute-start.4 = (f32[32,256]{1,0:T(8,128)S(1)}, f32[32,256]{1,0:T(8,128)S(1)}, u32[]{:S(2)}, u32[]{:S(2)}) collective-permute-start(f32[32,256]{1,0:T(8,128)S(1)} %get-tuple-element.31), channel_id=1, source_target_pairs={{0,2},{1,3},{2,0},{3,1},{4,6},{5,7},{6,4},{7,5},{8,10},{9,11},{10,... | collective-permute-start | bytes 98312 | tf_op jit(solution)/shard_map/ppermute | solution.py:151
  17.7 8.0 %collective-permute-start.5 = (f32[32,256]{1,0:T(8,128)S(1)}, f32[32,256]{1,0:T(8,128)S(1)}, u32[]{:S(2)}, u32[]{:S(2)}) collective-permute-start(f32[32,256]{1,0:T(8,128)S(1)} %get-tuple-element.32), channel_id=1, source_target_pairs={{0,3},{1,2},{2,1},{3,0},{4,7},{5,6},{6,5},{7,4},{8,11},{9,10},{10,... | collective-permute-start | bytes 98312 | tf_op jit(solution)/shard_map/ppermute | solution.py:151
  18.1 7.7 %collective-permute-start.6 = (f32[32,256]{1,0:T(8,128)S(1)}, f32[32,256]{1,0:T(8,128)S(1)}, u32[]{:S(2)}, u32[]{:S(2)}) collective-permute-start(f32[32,256]{1,0:T(8,128)S(1)} %get-tuple-element.33), channel_id=1, source_target_pairs={{0,4},{1,5},{2,6},{3,7},{4,0},{5,1},{6,2},{7,3},{8,12},{9,13},{10,... | collective-permute-start | bytes 98312 | tf_op jit(solution)/shard_map/ppermute | solution.py:151
  20.7 5.7 %collective-permute-start.7 = (f32[32,256]{1,0:T(8,128)S(1)}, f32[32,256]{1,0:T(8,128)S(1)}, u32[]{:S(2)}, u32[]{:S(2)}) collective-permute-start(f32[32,256]{1,0:T(8,128)S(1)} %get-tuple-element.34), channel_id=1, source_target_pairs={{0,5},{1,4},{2,7},{3,6},{4,1},{5,0},{6,3},{7,2},{8,13},{9,12},{10,... | collective-permute-start | bytes 98312 | tf_op jit(solution)/shard_map/ppermute | solution.py:151
  22.0 5.8 %collective-permute-start.8 = (f32[32,256]{1,0:T(8,128)S(1)}, f32[32,256]{1,0:T(8,128)S(1)}, u32[]{:S(2)}, u32[]{:S(2)}) collective-permute-start(f32[32,256]{1,0:T(8,128)S(1)} %get-tuple-element.35), channel_id=1, source_target_pairs={{0,6},{1,7},{2,4},{3,5},{4,2},{5,3},{6,0},{7,1},{8,14},{9,15},{10,... | collective-permute-start | bytes 98312 | tf_op jit(solution)/shard_map/ppermute | solution.py:151
  25.6 6.6 %collective-permute-start.9 = (f32[32,256]{1,0:T(8,128)S(1)}, f32[32,256]{1,0:T(8,128)S(1)}, u32[]{:S(2)}, u32[]{:S(2)}) collective-permute-start(f32[32,256]{1,0:T(8,128)S(1)} %get-tuple-element.36), channel_id=1, source_target_pairs={{0,7},{1,6},{2,5},{3,4},{4,3},{5,2},{6,1},{7,0},{8,15},{9,14},{10,... | collective-permute-start | bytes 98312 | tf_op jit(solution)/shard_map/ppermute | solution.py:151
  37.9 6.3 %collective-permute-start.10 = (f32[32,256]{1,0:T(8,128)S(1)}, f32[32,256]{1,0:T(8,128)S(1)}, u32[]{:S(2)}, u32[]{:S(2)}) collective-permute-start(f32[32,256]{1,0:T(8,128)S(1)} %get-tuple-element.37), channel_id=1, source_target_pairs={{0,0},{1,1},{2,8},{3,9},{4,16},{5,17},{6,24},{7,25},{8,2},{9,3},{1... | collective-permute-start | bytes 98312 | tf_op jit(solution)/shard_map/ppermute | solution.py:195
  38.5 7.1 %collective-permute-start.11 = (f32[32,256]{1,0:T(8,128)S(1)}, f32[32,256]{1,0:T(8,128)S(1)}, u32[]{:S(2)}, u32[]{:S(2)}) collective-permute-start(f32[32,256]{1,0:T(8,128)S(1)} %get-tuple-element.38), channel_id=1, source_target_pairs={{0,1},{1,0},{2,9},{3,8},{4,17},{5,16},{6,25},{7,24},{8,3},{9,2},{1... | collective-permute-start | bytes 98312 | tf_op jit(solution)/shard_map/ppermute | solution.py:195
  39.1 11.5 %collective-permute-start.12 = (f32[32,256]{1,0:T(8,128)S(1)}, f32[32,256]{1,0:T(8,128)S(1)}, u32[]{:S(2)}, u32[]{:S(2)}) collective-permute-start(f32[32,256]{1,0:T(8,128)S(1)} %get-tuple-element.39), channel_id=1, source_target_pairs={{0,2},{1,3},{2,10},{3,11},{4,18},{5,19},{6,26},{7,27},{8,0},{9,1},... | collective-permute-start | bytes 98312 | tf_op jit(solution)/shard_map/ppermute | solution.py:195
  39.3 13.6 %collective-permute-start.13 = (f32[32,256]{1,0:T(8,128)S(1)}, f32[32,256]{1,0:T(8,128)S(1)}, u32[]{:S(2)}, u32[]{:S(2)}) collective-permute-start(f32[32,256]{1,0:T(8,128)S(1)} %get-tuple-element.40), channel_id=1, source_target_pairs={{0,3},{1,2},{2,11},{3,10},{4,19},{5,18},{6,27},{7,26},{8,1},{9,0},... | collective-permute-start | bytes 98312 | tf_op jit(solution)/shard_map/ppermute | solution.py:195
  40.3 12.6 %collective-permute-start.14 = (f32[32,256]{1,0:T(8,128)S(1)}, f32[32,256]{1,0:T(8,128)S(1)}, u32[]{:S(2)}, u32[]{:S(2)}) collective-permute-start(f32[32,256]{1,0:T(8,128)S(1)} %get-tuple-element.41), channel_id=1, source_target_pairs={{0,4},{1,5},{2,12},{3,13},{4,20},{5,21},{6,28},{7,29},{8,6},{9,7},... | collective-permute-start | bytes 98312 | tf_op jit(solution)/shard_map/ppermute | solution.py:195
  44.2 10.7 %copy-start.5 = (f32[32,256]{1,0:T(8,128)}, f32[32,256]{1,0:T(8,128)S(1)}, u32[]{:S(2)}) copy-start(f32[32,256]{1,0:T(8,128)S(1)} %collective-permute-done.10.refs_0_) | copy-start | bytes 98308
  44.2 8.7 %collective-permute-start.15 = (f32[32,256]{1,0:T(8,128)S(1)}, f32[32,256]{1,0:T(8,128)S(1)}, u32[]{:S(2)}, u32[]{:S(2)}) collective-permute-start(f32[32,256]{1,0:T(8,128)S(1)} %get-tuple-element.42), channel_id=1, source_target_pairs={{0,5},{1,4},{2,13},{3,12},{4,21},{5,20},{6,29},{7,28},{8,7},{9,6},... | collective-permute-start | bytes 98312 | tf_op jit(solution)/shard_map/ppermute | solution.py:195
  45.7 9.2 %copy-start.6 = (f32[32,256]{1,0:T(8,128)}, f32[32,256]{1,0:T(8,128)S(1)}, u32[]{:S(2)}) copy-start(f32[32,256]{1,0:T(8,128)S(1)} %collective-permute-done.11.refs_1_) | copy-start | bytes 98308
  45.7 7.2 %collective-permute-start.16 = (f32[32,256]{1,0:T(8,128)S(1)}, f32[32,256]{1,0:T(8,128)S(1)}, u32[]{:S(2)}, u32[]{:S(2)}) collective-permute-start(f32[32,256]{1,0:T(8,128)S(1)} %get-tuple-element.43), channel_id=1, source_target_pairs={{0,6},{1,7},{2,14},{3,15},{4,22},{5,23},{6,30},{7,31},{8,4},{9,5},... | collective-permute-start | bytes 98312 | tf_op jit(solution)/shard_map/ppermute | solution.py:195
  50.6 4.2 %copy-start.7 = (f32[32,256]{1,0:T(8,128)}, f32[32,256]{1,0:T(8,128)S(1)}, u32[]{:S(2)}) copy-start(f32[32,256]{1,0:T(8,128)S(1)} %collective-permute-done.12.refs_2_) | copy-start | bytes 98308
  50.6 4.2 %collective-permute-start.17 = (f32[32,256]{1,0:T(8,128)S(1)}, f32[32,256]{1,0:T(8,128)S(1)}, u32[]{:S(2)}, u32[]{:S(2)}) collective-permute-start(f32[32,256]{1,0:T(8,128)S(1)} %get-tuple-element.44), channel_id=1, source_target_pairs={{0,7},{1,6},{2,15},{3,14},{4,23},{5,22},{6,31},{7,30},{8,5},{9,4},... | collective-permute-start | bytes 98312 | tf_op jit(solution)/shard_map/ppermute | solution.py:195
  52.9 2.0 %copy-start.8 = (f32[32,256]{1,0:T(8,128)}, f32[32,256]{1,0:T(8,128)S(1)}, u32[]{:S(2)}) copy-start(f32[32,256]{1,0:T(8,128)S(1)} %collective-permute-done.13.refs_3_) | copy-start | bytes 98308
  52.9 2.0 %copy-start.9 = (f32[32,256]{1,0:T(8,128)}, f32[32,256]{1,0:T(8,128)S(1)}, u32[]{:S(2)}) copy-start(f32[32,256]{1,0:T(8,128)S(1)} %collective-permute-done.14.refs_4_) | copy-start | bytes 98308
  52.9 2.0 %copy-start.10 = (f32[32,256]{1,0:T(8,128)}, f32[32,256]{1,0:T(8,128)S(1)}, u32[]{:S(2)}) copy-start(f32[32,256]{1,0:T(8,128)S(1)} %collective-permute-done.15.refs_5_) | copy-start | bytes 98308
  52.9 2.0 %copy-start.11 = (f32[32,256]{1,0:T(8,128)}, f32[32,256]{1,0:T(8,128)S(1)}, u32[]{:S(2)}) copy-start(f32[32,256]{1,0:T(8,128)S(1)} %collective-permute-done.16.refs_6_) | copy-start | bytes 98308
  54.9 0.6 %copy-start.12 = (f32[32,256]{1,0:T(8,128)}, f32[32,256]{1,0:T(8,128)S(1)}, u32[]{:S(2)}) copy-start(f32[32,256]{1,0:T(8,128)S(1)} %collective-permute-done.17.refs_7_) | copy-start | bytes 98308

commit v3 on v1

--- a/solution.py
+++ b/solution.py
@@ -73,7 +73,7 @@
         states = jnp.concatenate(
             [new_lower.reshape(shape), new_upper.reshape(shape)], axis=1
         ).reshape(rows, width)
-    y_ref[...] = states.reshape(y_ref.shape)
+    y_ref[...] = states
 
 
 def run_layers(states, first, distances, params, name):
@@ -88,10 +88,6 @@
         compiler_params=pltpu.CompilerParams(vmem_limit_bytes=24 * 2**20),
         name=name,
     )(states, *params)
-
-
-def swap_leading(x, a, b):
-    return x.reshape(a, b, -1, x.shape[-1]).swapaxes(0, 1).reshape(x.shape)
 
 
 def all_to_all(x, axes):
@@ -111,17 +107,19 @@
         return high.astype(jnp.bfloat16), (w - high).astype(jnp.bfloat16)
 
     params = (norm_gain, bias_hidden, gate_logit, *parts(w_in), *parts(w_out))
+    if rows % (8 * high_count * low_count) == 0:
+        states = all_to_all(features, ("seqhi", "seqlo"))
+        distances = [rows // high_count * 2 ** (k % high_bits) for k in range(HI_LAYERS)]
+        distances += [
+            rows // (high_count * low_count) * 2 ** (j % low_bits)
+            for j in range(layer_total - HI_LAYERS)
+        ]
+        states = run_layers(states, 0, distances, params, "all_layers")
+        return all_to_all(states, ("seqhi", "seqlo"))
     high_distances = [rows // high_count * 2 ** (k % high_bits) for k in range(HI_LAYERS)]
     low_distances = [rows // low_count * 2 ** (j % low_bits) for j in range(layer_total - HI_LAYERS)]
-
     states = all_to_all(features, "seqhi")
     states = run_layers(states, 0, high_distances, params, "high_layers")
-    if rows % (8 * high_count * low_count) == 0:
-        states = swap_leading(states, high_count, low_count)
-        states = all_to_all(states, "seqlo")
-        states = run_layers(states, HI_LAYERS, low_distances, params, "low_layers")
-        states = swap_leading(states, low_count, high_count)
-        return all_to_all(states, ("seqhi", "seqlo"))
     states = all_to_all(states, "seqhi")
     states = all_to_all(states, "seqlo")
     states = run_layers(states, HI_LAYERS, low_distances, params, "low_layers")

time: 51.9 us -> 44.1 us (0.85)
  blocking collectives: 28.2 us -> 12.8 us
  waiting for transfers between devices: 2.49 us -> 7.09 us
  starting transfers between devices: 4.21 us -> 7.3 us
    all_to_all x2 -> x1, blocking collectives: 28.2 us -> 12.8 us  [all_to_all(): return lax.all_to_all(x, axes, split_axis=0, concat_axis=0, tiled=True)]
    all_to_all x1, waiting for transfers between devices: 2.49 us -> 7.09 us  [all_to_all(): return lax.all_to_all(x, axes, split_axis=0, concat_axis=0, tiled=True)]
    all_to_all x1, starting transfers between devices: 4.21 us -> 7.3 us  [all_to_all(): return lax.all_to_all(x, axes, split_axis=0, concat_axis=0, tiled=True)]
    pallas_call x2 -> x1, Pallas kernels: 11.2 us -> 11.1 us  [run_layers(): pl.pallas_call(kernel, out_shape=jax.ShapeDtypeStruct((rows, width), jnp....]
  transfers between devices with their start and end apart: 1 -> 1, of which waited for: 1 -> 1; matrix products, arithmetic and copies ran while one was open for 7% -> 8% of each run, Pallas kernels for 0% -> 0%
where the time goes in v3:
time: 44.1 us; the launch traced here: 43.8 us
  blocking collectives  12.8 us (29%)
  Pallas kernels  11.1 us (25%)
  starting transfers between devices  7.3 us (17%)
  waiting for transfers between devices  7.09 us (16%)
  other arithmetic  3.49 us (8%)
  local copies, waits for them, and re-layouts  1.97 us (4%)
    all_to_all x1, blocking collectives, all_to_all(): return lax.all_to_all(x, axes, split_axis=0, concat_axis=0, tiled=True)  12.8 us
    pallas_call x1, Pallas kernels, run_layers(): pl.pallas_call(kernel, out_shape=jax.ShapeDtypeStruct((rows, width), jnp....  11.1 us
    all_to_all x1, starting transfers between devices, all_to_all(): return lax.all_to_all(x, axes, split_axis=0, concat_axis=0, tiled=True)  7.3 us
    all_to_all x1, waiting for transfers between devices, all_to_all(): return lax.all_to_all(x, axes, split_axis=0, concat_axis=0, tiled=True)  7.09 us
    convert_element_type x2, other arithmetic, parts(): return (high.astype(jnp.bfloat16), (w - high).astype(jnp.bfloat16))  3.49 us
    unnamed x11, local copies, waits for them, and re-layouts  1.97 us
  transfers between devices with their start and end apart: 1, of which 1 were waited for; matrix products, arithmetic and copies ran while one was open for 8% of the time, Pallas kernels for 0%

profile of v3, /device:TPU:0, one launch (start us, length us, event | category | flops | bytes accessed | tf_op | source)
XLA Modules:
  0.0 43.8 jit_solution(16845926211458512807)
XLA Ops:
  0.0 7.3 %all-to-all-start = ((f32[32,8,256]{2,1,0:T(8,128)}), f32[32,8,256]{2,1,0:T(8,128)S(1)}, u32[]{:S(2)}, u32[]{:S(2)}) async-start(f32[32,8,256]{2,1,0:T(8,128)} %bitcast.7), calls=%async_computation | async-start | bytes 524288 | tf_op jit(solution)/shard_map/all_to_all | solution.py:94
  7.3 0.0 copy-start.4
  7.3 2.2 %fusion = (bf16[512,1024]{1,0:T(8,128)(2,1)S(1)}, bf16[512,1024]{1,0:T(8,128)(2,1)S(1)}) fusion(f32[512,1024]{1,0:T(8,128)} %param.10), kind=kLoop, calls=%fused_computation.4 | loop fusion | flops 2097152 | bytes 4194304 | tf_op jit(solution)/shard_map/convert_element_type | solution.py:107
  9.5 0.0 copy-done.4
  9.5 0.0 copy-start.1
  9.5 0.0 copy-start.2
  9.5 0.0 copy-start.3
  9.5 1.3 %fusion.1 = (bf16[1024,512]{1,0:T(8,128)(2,1)S(1)}, bf16[1024,512]{1,0:T(8,128)(2,1)}) fusion(f32[1024,512]{1,0:T(8,128)S(1)} %copy-done.4), kind=kLoop, calls=%fused_computation.5 | loop fusion | flops 2097152 | bytes 4194304 | tf_op jit(solution)/shard_map/convert_element_type | solution.py:107
  10.9 7.1 %all-to-all-done = f32[32,8,256]{2,1,0:T(8,128)S(1)} async-done(((f32[32,8,256]{2,1,0:T(8,128)}), f32[32,8,256]{2,1,0:T(8,128)S(1)}, u32[]{:S(2)}, u32[]{:S(2)}) %all-to-all-start) | async-done | bytes 262176 | tf_op jit(solution)/shard_map/all_to_all | solution.py:94
  18.0 0.0 copy-done.1
  18.0 0.0 copy-done.2
  18.0 0.0 copy-done.3
  18.0 0.0 copy-start
  18.0 1.2 %copy-done = bf16[1024,512]{1,0:T(8,128)(2,1)S(1)} copy-done((bf16[1024,512]{1,0:T(8,128)(2,1)S(1)}, bf16[1024,512]{1,0:T(8,128)(2,1)}, u32[]{:S(2)}) %copy-start) | copy-done | bytes 1048600
  19.2 11.1 %all_layers.1 = f32[256,256]{1,0:T(8,128)S(1)} custom-call(f32[256,256]{1,0:T(8,128)S(1)} %bitcast.4, f32[8,512]{1,0:T(8,128)S(1)} %copy-done.2, f32[8,1024]{1,0:T(8,128)S(1)} %copy-done.1, f32[8,512]{1,0:T(8,128)S(1)} %copy-done.3, bf16[512,1024]{1,0:T(8,128)(2,1)S(1)} %get-tuple-element.8.in_high_ref, bf16[512,1024]{1,0:T(8,128)(2,1)S(1)} %get-tuple-element.7.in_low_ref, ...), custom_call_target="tpu_custom_call" | custom-call | tf_op jit(solution)/shard_map/all_layers/pallas_call | solution.py:83
  30.3 12.8 %all_to_all.23 = f32[32,8,256]{2,1,0:T(8,128)S(1)} all-to-all(f32[32,8,256]{2,1,0:T(8,128)S(1)} %bitcast.5), channel_id=1, replica_groups=mesh['seqhi'=4,'seqlo'=8] {'seqhi','seqlo'}, dimensions={0} | all-to-all | bytes 524288 | tf_op jit(solution)/shard_map/all_to_all | solution.py:94
  43.1 0.7 %copy.8 = f32[256,256]{1,0:T(8,128)} copy(f32[256,256]{1,0:T(8,128)S(1)} %bitcast.6) | data formatting | bytes 524288
Async XLA Ops:
  0.0 18.0 %all-to-all-start = ((f32[32,8,256]{2,1,0:T(8,128)}), f32[32,8,256]{2,1,0:T(8,128)S(1)}, u32[]{:S(2)}, u32[]{:S(2)}) async-start(f32[32,8,256]{2,1,0:T(8,128)} %bitcast.7), calls=%async_computation | async-start | bytes 524288 | tf_op jit(solution)/shard_map/all_to_all | solution.py:94
  7.3 2.2 %copy-start.4 = (f32[1024,512]{1,0:T(8,128)S(1)}, f32[1024,512]{1,0:T(8,128)}, u32[]{:S(2)}) copy-start(f32[1024,512]{1,0:T(8,128)} %param.11) | copy-start | bytes 6291460
  9.5 8.4 %copy-start.1 = (f32[8,1024]{1,0:T(8,128)S(1)}, f32[8,1024]{1,0:T(8,128)}, u32[]{:S(2)}) copy-start(f32[8,1024]{1,0:T(8,128)} %bias_ref.1) | copy-start | bytes 98308
  9.5 8.4 %copy-start.2 = (f32[8,512]{1,0:T(8,128)S(1)}, f32[8,512]{1,0:T(8,128)}, u32[]{:S(2)}) copy-start(f32[8,512]{1,0:T(8,128)} %gain_ref.1) | copy-start | bytes 49156
  9.5 8.4 %copy-start.3 = (f32[8,512]{1,0:T(8,128)S(1)}, f32[8,512]{1,0:T(8,128)}, u32[]{:S(2)}) copy-start(f32[8,512]{1,0:T(8,128)} %gate_ref.1) | copy-start | bytes 49156
  18.0 1.2 %copy-start = (bf16[1024,512]{1,0:T(8,128)(2,1)S(1)}, bf16[1024,512]{1,0:T(8,128)(2,1)}, u32[]{:S(2)}) copy-start(bf16[1024,512]{1,0:T(8,128)(2,1)} %get-tuple-element.6.out_high_ref) | copy-start | bytes 3145732

commit v4 on v3

--- a/solution.py
+++ b/solution.py
@@ -18,15 +18,13 @@
     return high, (x - high.astype(jnp.float32)).astype(jnp.bfloat16)
 
 
-def dot(a, b):
-    return jnp.dot(a, b, preferred_element_type=jnp.float32)
-
-
 def dot_split(x, w_high, w_low):
-    rows = x.shape[0]
     x_high, x_low = split_high_low(x)
-    both = dot(jnp.concatenate([x_high, x_low], axis=0), w_high)
-    return both[:rows] + (both[rows:] + dot(x_high, w_low))
+    return jnp.dot(
+        jnp.concatenate([x_high, x_high, x_low], axis=1),
+        jnp.concatenate([w_high, w_low, w_high], axis=0),
+        preferred_element_type=jnp.float32,
+    )
 
 
 def gelu(x):
@@ -85,7 +83,7 @@
         out_shape=jax.ShapeDtypeStruct((rows, width), jnp.float32),
         in_specs=[pl.BlockSpec(memory_space=pltpu.VMEM)] * 8,
         out_specs=pl.BlockSpec(memory_space=pltpu.VMEM),
-        compiler_params=pltpu.CompilerParams(vmem_limit_bytes=24 * 2**20),
+        compiler_params=pltpu.CompilerParams(vmem_limit_bytes=12 * 2**20),
         name=name,
     )(states, *params)
 

time: 44.1 us -> 44.1 us (level)
  no operation moved by 1% of the time
where the time goes in v4:
time: 44.1 us; the launch traced here: 43.9 us
  blocking collectives  12.8 us (29%)
  Pallas kernels  11.2 us (25%)
  starting transfers between devices  7.3 us (17%)
  waiting for transfers between devices  7.09 us (16%)
  other arithmetic  3.49 us (8%)
  local copies, waits for them, and re-layouts  1.97 us (4%)
    all_to_all x1, blocking collectives, all_to_all(): return lax.all_to_all(x, axes, split_axis=0, concat_axis=0, tiled=True)  12.8 us
    pallas_call x1, Pallas kernels, run_layers(): pl.pallas_call(kernel, out_shape=jax.ShapeDtypeStruct((rows, width), jnp....  11.2 us
    all_to_all x1, starting transfers between devices, all_to_all(): return lax.all_to_all(x, axes, split_axis=0, concat_axis=0, tiled=True)  7.3 us
    all_to_all x1, waiting for transfers between devices, all_to_all(): return lax.all_to_all(x, axes, split_axis=0, concat_axis=0, tiled=True)  7.09 us
    convert_element_type x2, other arithmetic, parts(): return (high.astype(jnp.bfloat16), (w - high).astype(jnp.bfloat16))  3.49 us
    unnamed x11, local copies, waits for them, and re-layouts  1.97 us
  transfers between devices with their start and end apart: 1, of which 1 were waited for; matrix products, arithmetic and copies ran while one was open for 8% of the time, Pallas kernels for 0%

profile of v4, /device:TPU:0, one launch (start us, length us, event | category | flops | bytes accessed | tf_op | source)
XLA Modules:
  0.0 43.9 jit_solution(16860965343348197203)
XLA Ops:
  0.0 7.3 %all-to-all-start = ((f32[32,8,256]{2,1,0:T(8,128)}), f32[32,8,256]{2,1,0:T(8,128)S(1)}, u32[]{:S(2)}, u32[]{:S(2)}) async-start(f32[32,8,256]{2,1,0:T(8,128)} %bitcast.7), calls=%async_computation | async-start | bytes 524288 | tf_op jit(solution)/shard_map/all_to_all | solution.py:92
  7.3 0.0 copy-start.4
  7.3 2.2 %fusion = (bf16[512,1024]{1,0:T(8,128)(2,1)S(1)}, bf16[512,1024]{1,0:T(8,128)(2,1)S(1)}) fusion(f32[512,1024]{1,0:T(8,128)} %param.10), kind=kLoop, calls=%fused_computation.4 | loop fusion | flops 2097152 | bytes 4194304 | tf_op jit(solution)/shard_map/convert_element_type | solution.py:105
  9.5 0.0 copy-done.4
  9.5 0.0 copy-start.1
  9.5 0.0 copy-start.2
  9.5 0.0 copy-start.3
  9.5 1.3 %fusion.1 = (bf16[1024,512]{1,0:T(8,128)(2,1)S(1)}, bf16[1024,512]{1,0:T(8,128)(2,1)}) fusion(f32[1024,512]{1,0:T(8,128)S(1)} %copy-done.4), kind=kLoop, calls=%fused_computation.5 | loop fusion | flops 2097152 | bytes 4194304 | tf_op jit(solution)/shard_map/convert_element_type | solution.py:105
  10.9 7.1 %all-to-all-done = f32[32,8,256]{2,1,0:T(8,128)S(1)} async-done(((f32[32,8,256]{2,1,0:T(8,128)}), f32[32,8,256]{2,1,0:T(8,128)S(1)}, u32[]{:S(2)}, u32[]{:S(2)}) %all-to-all-start) | async-done | bytes 262176 | tf_op jit(solution)/shard_map/all_to_all | solution.py:92
  18.0 0.0 copy-done.1
  18.0 0.0 copy-done.2
  18.0 0.0 copy-done.3
  18.0 0.0 copy-start
  18.0 1.2 %copy-done = bf16[1024,512]{1,0:T(8,128)(2,1)S(1)} copy-done((bf16[1024,512]{1,0:T(8,128)(2,1)S(1)}, bf16[1024,512]{1,0:T(8,128)(2,1)}, u32[]{:S(2)}) %copy-start) | copy-done | bytes 1048600
  19.2 11.2 %all_layers.1 = f32[256,256]{1,0:T(8,128)S(1)} custom-call(f32[256,256]{1,0:T(8,128)S(1)} %bitcast.4, f32[8,512]{1,0:T(8,128)S(1)} %copy-done.2, f32[8,1024]{1,0:T(8,128)S(1)} %copy-done.1, f32[8,512]{1,0:T(8,128)S(1)} %copy-done.3, bf16[512,1024]{1,0:T(8,128)(2,1)S(1)} %get-tuple-element.8.in_high_ref, bf16[512,1024]{1,0:T(8,128)(2,1)S(1)} %get-tuple-element.7.in_low_ref, ...), custom_call_target="tpu_custom_call" | custom-call | tf_op jit(solution)/shard_map/all_layers/pallas_call | solution.py:81
  30.4 12.8 %all_to_all.23 = f32[32,8,256]{2,1,0:T(8,128)S(1)} all-to-all(f32[32,8,256]{2,1,0:T(8,128)S(1)} %bitcast.5), channel_id=1, replica_groups=mesh['seqhi'=4,'seqlo'=8] {'seqhi','seqlo'}, dimensions={0} | all-to-all | bytes 524288 | tf_op jit(solution)/shard_map/all_to_all | solution.py:92
  43.2 0.7 %copy.8 = f32[256,256]{1,0:T(8,128)} copy(f32[256,256]{1,0:T(8,128)S(1)} %bitcast.6) | data formatting | bytes 524288
Async XLA Ops:
  0.0 18.0 %all-to-all-start = ((f32[32,8,256]{2,1,0:T(8,128)}), f32[32,8,256]{2,1,0:T(8,128)S(1)}, u32[]{:S(2)}, u32[]{:S(2)}) async-start(f32[32,8,256]{2,1,0:T(8,128)} %bitcast.7), calls=%async_computation | async-start | bytes 524288 | tf_op jit(solution)/shard_map/all_to_all | solution.py:92
  7.3 2.2 %copy-start.4 = (f32[1024,512]{1,0:T(8,128)S(1)}, f32[1024,512]{1,0:T(8,128)}, u32[]{:S(2)}) copy-start(f32[1024,512]{1,0:T(8,128)} %param.11) | copy-start | bytes 6291460
  9.5 8.4 %copy-start.1 = (f32[8,1024]{1,0:T(8,128)S(1)}, f32[8,1024]{1,0:T(8,128)}, u32[]{:S(2)}) copy-start(f32[8,1024]{1,0:T(8,128)} %bias_ref.1) | copy-start | bytes 98308
  9.5 8.4 %copy-start.2 = (f32[8,512]{1,0:T(8,128)S(1)}, f32[8,512]{1,0:T(8,128)}, u32[]{:S(2)}) copy-start(f32[8,512]{1,0:T(8,128)} %gain_ref.1) | copy-start | bytes 49156
  9.5 8.4 %copy-start.3 = (f32[8,512]{1,0:T(8,128)S(1)}, f32[8,512]{1,0:T(8,128)}, u32[]{:S(2)}) copy-start(f32[8,512]{1,0:T(8,128)} %gate_ref.1) | copy-start | bytes 49156
  18.0 1.2 %copy-start = (bf16[1024,512]{1,0:T(8,128)(2,1)S(1)}, bf16[1024,512]{1,0:T(8,128)(2,1)}, u32[]{:S(2)}) copy-start(bf16[1024,512]{1,0:T(8,128)(2,1)} %get-tuple-element.6.out_high_ref) | copy-start | bytes 3145732

commit v5 on v3

--- a/solution.py
+++ b/solution.py
@@ -33,59 +33,118 @@
     return 0.5 * x * (1.0 + jnp.tanh(GELU_SCALE * (x + GELU_CUBE * (x * x * x))))
 
 
-def switch_unit(lower, upper, gain, bias, gate, w_in, w_out, hidden_block):
-    width = lower.shape[-1]
-    pair = jnp.concatenate([lower, upper], axis=-1)
-    center = pair - jnp.mean(pair, axis=-1, keepdims=True)
-    spread = jnp.mean(center * center, axis=-1, keepdims=True)
-    normed = center * lax.rsqrt(spread + NORM_EPS) * gain
-    out = gate * pair
-    in_high, in_low = w_in
-    out_high, out_low = w_out
-    for start in range(0, in_high.shape[1], hidden_block):
-        cols = slice(start, start + hidden_block)
-        hidden = gelu(dot_split(normed, in_high[:, cols], in_low[:, cols]) + bias[:, cols])
-        out = out + dot_split(hidden, out_high[cols, :], out_low[cols, :])
-    return out[:, :width], out[:, width:]
+def split_rows(distances, rows):
+    strides = [8 * 2**i for i in range((rows // 16).bit_length())]
+    runs, start = [], 0
+    while start < len(distances):
+        end, stride = start, None
+        while end < len(distances):
+            free = [s for s in strides if s not in distances[start : end + 1]]
+            if not free:
+                break
+            end, stride = end + 1, free[-1]
+        end = max(end, start + 1)
+        runs.append((start, end, stride))
+        start = end
+    return runs
+
+
+def layer_chain(states, layers, hidden_block, weights):
+    rows, width = states.shape
+    gain_ref, bias_ref, gate_ref, in_high, in_low, out_high, out_low, ready = weights
+    hidden_count = in_high.shape[1]
+    for k, distance in layers:
+        groups = rows // (2 * distance)
+        grouped = states.reshape(groups, 2, distance, width)
+        pair = jnp.concatenate(
+            [grouped[:, 0].reshape(-1, width), grouped[:, 1].reshape(-1, width)], axis=-1
+        )
+        center = pair - jnp.mean(pair, axis=-1, keepdims=True)
+        spread = jnp.mean(center * center, axis=-1, keepdims=True)
+        normed = center * lax.rsqrt(spread + NORM_EPS) * gain_ref[k : k + 1, :]
+        out = jax.nn.sigmoid(gate_ref[k : k + 1, :]) * pair
+        yield None
+        blocks = [slice(c, c + hidden_block) for c in range(0, hidden_count, hidden_block)]
+        for cols in blocks:
+            mixed = dot_split(normed, in_high[:, cols], in_low[:, cols])
+            hidden = gelu(mixed + bias_ref[k : k + 1, cols])
+            yield None
+            ready()
+            out = out + dot_split(hidden, out_high[cols, :], out_low[cols, :])
+            yield None
+        shape = (groups, 1, distance, width)
+        states = jnp.concatenate(
+            [out[:, :width].reshape(shape), out[:, width:].reshape(shape)], axis=1
+        ).reshape(rows, width)
+    yield states
+
+
+def interleave(chains, lag):
+    results = [None] * len(chains)
+    active = list(range(len(chains)))
+    turn = 0
+    while active:
+        for i in list(active):
+            if turn < i * lag:
+                continue
+            value = next(chains[i])
+            if value is not None:
+                results[i] = value
+                active.remove(i)
+        turn += 1
+    return results
 
 
 def layers_kernel(
     first, distances, hidden_block,
-    x_ref, gain_ref, bias_ref, gate_ref, in_high_ref, in_low_ref, out_high_ref, out_low_ref, y_ref,
+    x_ref, gain_ref, bias_ref, gate_ref, in_high_ref, in_low_ref, out_low_ref, out_high_hbm,
+    y_ref, out_high_ref, copied,
 ):
+    copy = pltpu.make_async_copy(out_high_hbm, out_high_ref, copied)
+    copy.start()
+    waited = []
+
+    def ready():
+        if not waited:
+            copy.wait()
+            waited.append(True)
+
+    weights = (gain_ref, bias_ref, gate_ref, in_high_ref, in_low_ref, out_high_ref, out_low_ref, ready)
     rows, width = x_ref.shape
     states = x_ref[...]
-    for step, distance in enumerate(distances):
-        k = first + step
-        groups = rows // (2 * distance)
-        grouped = states.reshape(groups, 2, distance, width)
-        new_lower, new_upper = switch_unit(
-            grouped[:, 0].reshape(-1, width),
-            grouped[:, 1].reshape(-1, width),
-            gain_ref[k : k + 1, :],
-            bias_ref[k : k + 1, :],
-            jax.nn.sigmoid(gate_ref[k : k + 1, :]),
-            (in_high_ref, in_low_ref),
-            (out_high_ref, out_low_ref),
-            hidden_block,
+    for start, end, stride in split_rows(distances, rows):
+        ks = range(first + start, first + end)
+        if stride is None:
+            layers = list(zip(ks, distances[start:end]))
+            (states,) = interleave([layer_chain(states, layers, hidden_block, weights)], 0)
+            continue
+        parted = states.reshape(rows // (2 * stride), 2, stride, width)
+        layers = [(k, d if d < stride else d // 2) for k, d in zip(ks, distances[start:end])]
+        halves = interleave(
+            [
+                layer_chain(parted[:, i].reshape(rows // 2, width), layers, hidden_block, weights)
+                for i in range(2)
+            ],
+            2,
         )
-        shape = (groups, 1, distance, width)
-        states = jnp.concatenate(
-            [new_lower.reshape(shape), new_upper.reshape(shape)], axis=1
-        ).reshape(rows, width)
+        shape = (rows // (2 * stride), 1, stride, width)
+        states = jnp.concatenate([half.reshape(shape) for half in halves], axis=1)
+        states = states.reshape(rows, width)
     y_ref[...] = states
 
 
 def run_layers(states, first, distances, params, name):
     rows, width = states.shape
     hidden = params[1].shape[1]
-    kernel = functools.partial(layers_kernel, first, distances, min(hidden, 256))
+    kernel = functools.partial(layers_kernel, first, distances, min(hidden, 512))
+    vmem = pl.BlockSpec(memory_space=pltpu.VMEM)
     return pl.pallas_call(
         kernel,
         out_shape=jax.ShapeDtypeStruct((rows, width), jnp.float32),
-        in_specs=[pl.BlockSpec(memory_space=pltpu.VMEM)] * 8,
-        out_specs=pl.BlockSpec(memory_space=pltpu.VMEM),
-        compiler_params=pltpu.CompilerParams(vmem_limit_bytes=24 * 2**20),
+        in_specs=[vmem] * 7 + [pl.BlockSpec(memory_space=pltpu.HBM)],
+        out_specs=vmem,
+        scratch_shapes=[pltpu.VMEM(params[-1].shape, params[-1].dtype), pltpu.SemaphoreType.DMA],
+        compiler_params=pltpu.CompilerParams(vmem_limit_bytes=16 * 2**20),
         name=name,
     )(states, *params)
 
@@ -106,7 +165,8 @@
         high = lax.reduce_precision(w, exponent_bits=8, mantissa_bits=7)
         return high.astype(jnp.bfloat16), (w - high).astype(jnp.bfloat16)
 
-    params = (norm_gain, bias_hidden, gate_logit, *parts(w_in), *parts(w_out))
+    out_high, out_low = parts(w_out)
+    params = (norm_gain, bias_hidden, gate_logit, *parts(w_in), out_low, out_high)
     if rows % (8 * high_count * low_count) == 0:
         states = all_to_all(features, ("seqhi", "seqlo"))
         distances = [rows // high_count * 2 ** (k % high_bits) for k in range(HI_LAYERS)]

time: 44.1 us -> 45.5 us (1.032)
  Pallas kernels: 11.1 us -> 12.5 us
    pallas_call x1, Pallas kernels: 11.1 us -> 12.5 us  [run_layers(): pl.pallas_call(kernel, out_shape=jax.ShapeDtypeStruct((rows, width), jnp....]
where the time goes in v5:
time: 45.5 us; the launch traced here: 45.2 us
  blocking collectives  12.8 us (28%)
  Pallas kernels  12.5 us (27%)
  starting transfers between devices  7.3 us (16%)
  waiting for transfers between devices  7.09 us (16%)
  other arithmetic  3.49 us (8%)
  local copies, waits for them, and re-layouts  1.97 us (4%)
    all_to_all x1, blocking collectives, all_to_all(): return lax.all_to_all(x, axes, split_axis=0, concat_axis=0, tiled=True)  12.8 us
    pallas_call x1, Pallas kernels, run_layers(): pl.pallas_call(kernel, out_shape=jax.ShapeDtypeStruct((rows, width), jnp....  12.5 us
    all_to_all x1, starting transfers between devices, all_to_all(): return lax.all_to_all(x, axes, split_axis=0, concat_axis=0, tiled=True)  7.3 us
    all_to_all x1, waiting for transfers between devices, all_to_all(): return lax.all_to_all(x, axes, split_axis=0, concat_axis=0, tiled=True)  7.09 us
    convert_element_type x2, other arithmetic, parts(): return (high.astype(jnp.bfloat16), (w - high).astype(jnp.bfloat16))  3.49 us
    unnamed x11, local copies, waits for them, and re-layouts  1.97 us
  transfers between devices with their start and end apart: 1, of which 1 were waited for; matrix products, arithmetic and copies ran while one was open for 8% of the time, Pallas kernels for 0%

profile of v5, /device:TPU:0, one launch (start us, length us, event | category | flops | bytes accessed | tf_op | source)
XLA Modules:
  0.0 45.2 jit_solution(15982468747057599367)
XLA Ops:
  0.0 7.3 %all-to-all-start = ((f32[32,8,256]{2,1,0:T(8,128)}), f32[32,8,256]{2,1,0:T(8,128)S(1)}, u32[]{:S(2)}, u32[]{:S(2)}) async-start(f32[32,8,256]{2,1,0:T(8,128)} %bitcast.7), calls=%async_computation | async-start | bytes 524288 | tf_op jit(solution)/shard_map/all_to_all | solution.py:153
  7.3 0.0 copy-start.4
  7.3 2.2 %fusion = (bf16[512,1024]{1,0:T(8,128)(2,1)S(1)}, bf16[512,1024]{1,0:T(8,128)(2,1)S(1)}) fusion(f32[512,1024]{1,0:T(8,128)} %param.10), kind=kLoop, calls=%fused_computation.4 | loop fusion | flops 2097152 | bytes 4194304 | tf_op jit(solution)/shard_map/convert_element_type | solution.py:166
  9.5 0.0 copy-done.4
  9.5 0.0 copy-start.1
  9.5 0.0 copy-start.2
  9.5 0.0 copy-start.3
  9.5 1.3 %reduce-precision_convert_fusion = (bf16[1024,512]{1,0:T(8,128)(2,1)S(1)}, bf16[1024,512]{1,0:T(8,128)(2,1)}) fusion(f32[1024,512]{1,0:T(8,128)S(1)} %copy-done.4), kind=kLoop, calls=%fused_computation | loop fusion | flops 2097152 | bytes 4194304 | tf_op jit(solution)/shard_map/convert_element_type | solution.py:166
  10.9 7.1 %all-to-all-done = f32[32,8,256]{2,1,0:T(8,128)S(1)} async-done(((f32[32,8,256]{2,1,0:T(8,128)}), f32[32,8,256]{2,1,0:T(8,128)S(1)}, u32[]{:S(2)}, u32[]{:S(2)}) %all-to-all-start) | async-done | bytes 262176 | tf_op jit(solution)/shard_map/all_to_all | solution.py:153
  18.0 0.0 copy-done.1
  18.0 0.0 copy-done.2
  18.0 0.0 copy-done.3
  18.0 0.0 copy-start
  18.0 1.2 %copy-done = bf16[1024,512]{1,0:T(8,128)(2,1)S(1)} copy-done((bf16[1024,512]{1,0:T(8,128)(2,1)S(1)}, bf16[1024,512]{1,0:T(8,128)(2,1)}, u32[]{:S(2)}) %copy-start) | copy-done | bytes 1048600
  19.2 12.5 %all_layers.1 = f32[256,256]{1,0:T(8,128)S(1)} custom-call(f32[256,256]{1,0:T(8,128)S(1)} %bitcast.4, f32[8,512]{1,0:T(8,128)S(1)} %copy-done.2, f32[8,1024]{1,0:T(8,128)S(1)} %copy-done.1, f32[8,512]{1,0:T(8,128)S(1)} %copy-done.3, bf16[512,1024]{1,0:T(8,128)(2,1)S(1)} %get-tuple-element.8.in_high_ref, bf16[512,1024]{1,0:T(8,128)(2,1)S(1)} %get-tuple-element.7.in_low_ref, ...), custom_call_target="tpu_custom_call" | custom-call | tf_op jit(solution)/shard_map/all_layers/pallas_call | solution.py:141
  31.7 12.8 %all_to_all.23 = f32[32,8,256]{2,1,0:T(8,128)S(1)} all-to-all(f32[32,8,256]{2,1,0:T(8,128)S(1)} %bitcast.5), channel_id=1, replica_groups=mesh['seqhi'=4,'seqlo'=8] {'seqhi','seqlo'}, dimensions={0} | all-to-all | bytes 524288 | tf_op jit(solution)/shard_map/all_to_all | solution.py:153
  44.5 0.7 %copy.8 = f32[256,256]{1,0:T(8,128)} copy(f32[256,256]{1,0:T(8,128)S(1)} %bitcast.6) | data formatting | bytes 524288
Async XLA Ops:
  0.0 18.0 %all-to-all-start = ((f32[32,8,256]{2,1,0:T(8,128)}), f32[32,8,256]{2,1,0:T(8,128)S(1)}, u32[]{:S(2)}, u32[]{:S(2)}) async-start(f32[32,8,256]{2,1,0:T(8,128)} %bitcast.7), calls=%async_computation | async-start | bytes 524288 | tf_op jit(solution)/shard_map/all_to_all | solution.py:153
  7.3 2.2 %copy-start.4 = (f32[1024,512]{1,0:T(8,128)S(1)}, f32[1024,512]{1,0:T(8,128)}, u32[]{:S(2)}) copy-start(f32[1024,512]{1,0:T(8,128)} %param.11) | copy-start | bytes 6291460
  9.5 8.4 %copy-start.1 = (f32[8,1024]{1,0:T(8,128)S(1)}, f32[8,1024]{1,0:T(8,128)}, u32[]{:S(2)}) copy-start(f32[8,1024]{1,0:T(8,128)} %bias_ref.1) | copy-start | bytes 98308
  9.5 8.4 %copy-start.2 = (f32[8,512]{1,0:T(8,128)S(1)}, f32[8,512]{1,0:T(8,128)}, u32[]{:S(2)}) copy-start(f32[8,512]{1,0:T(8,128)} %gain_ref.1) | copy-start | bytes 49156
  9.5 8.4 %copy-start.3 = (f32[8,512]{1,0:T(8,128)S(1)}, f32[8,512]{1,0:T(8,128)}, u32[]{:S(2)}) copy-start(f32[8,512]{1,0:T(8,128)} %gate_ref.1) | copy-start | bytes 49156
  18.0 1.2 %copy-start = (bf16[1024,512]{1,0:T(8,128)(2,1)S(1)}, bf16[1024,512]{1,0:T(8,128)(2,1)}, u32[]{:S(2)}) copy-start(bf16[1024,512]{1,0:T(8,128)(2,1)} %get-tuple-element.6.out_low_ref) | copy-start | bytes 3145732

commit v6 on v3

--- a/solution.py
+++ b/solution.py
@@ -30,48 +30,73 @@
 
 
 def gelu(x):
-    return 0.5 * x * (1.0 + jnp.tanh(GELU_SCALE * (x + GELU_CUBE * (x * x * x))))
+    half = 0.5 * x
+    return half + half * jnp.tanh(x * (GELU_SCALE + (GELU_SCALE * GELU_CUBE) * (x * x)))
 
 
-def switch_unit(lower, upper, gain, bias, gate, w_in, w_out, hidden_block):
-    width = lower.shape[-1]
-    pair = jnp.concatenate([lower, upper], axis=-1)
+def switch_unit(pair, gain, bias, gate, w_in, w_out, hidden_block, out_ready):
     center = pair - jnp.mean(pair, axis=-1, keepdims=True)
     spread = jnp.mean(center * center, axis=-1, keepdims=True)
     normed = center * lax.rsqrt(spread + NORM_EPS) * gain
     out = gate * pair
     in_high, in_low = w_in
     out_high, out_low = w_out
-    for start in range(0, in_high.shape[1], hidden_block):
-        cols = slice(start, start + hidden_block)
-        hidden = gelu(dot_split(normed, in_high[:, cols], in_low[:, cols]) + bias[:, cols])
+    hidden_count = in_high.shape[1]
+    blocks = [slice(c, c + hidden_block) for c in range(0, hidden_count, hidden_block)]
+
+    def enter(cols):
+        return dot_split(normed, in_high[:, cols], in_low[:, cols]) + bias[:, cols]
+
+    ahead = enter(blocks[0])
+    for number, cols in enumerate(blocks):
+        entered = ahead
+        if number + 1 < len(blocks):
+            ahead = enter(blocks[number + 1])
+        hidden = gelu(entered)
+        if number == 0:
+            out_ready()
         out = out + dot_split(hidden, out_high[cols, :], out_low[cols, :])
-    return out[:, :width], out[:, width:]
+    return out
 
 
 def layers_kernel(
     first, distances, hidden_block,
-    x_ref, gain_ref, bias_ref, gate_ref, in_high_ref, in_low_ref, out_high_ref, out_low_ref, y_ref,
+    x_ref, gain_ref, bias_ref, gate_ref, in_high_ref, in_low_ref, out_high_hbm, out_low_hbm,
+    y_ref, out_high_ref, out_low_ref, copied,
 ):
+    copies = [
+        pltpu.make_async_copy(out_high_hbm, out_high_ref, copied.at[0]),
+        pltpu.make_async_copy(out_low_hbm, out_low_ref, copied.at[1]),
+    ]
+    for copy in copies:
+        copy.start()
+
+    def wait_copies():
+        for copy in copies:
+            copy.wait()
+
     rows, width = x_ref.shape
     states = x_ref[...]
     for step, distance in enumerate(distances):
         k = first + step
         groups = rows // (2 * distance)
         grouped = states.reshape(groups, 2, distance, width)
-        new_lower, new_upper = switch_unit(
-            grouped[:, 0].reshape(-1, width),
-            grouped[:, 1].reshape(-1, width),
+        pair = jnp.concatenate(
+            [grouped[:, 0].reshape(-1, width), grouped[:, 1].reshape(-1, width)], axis=-1
+        )
+        out = switch_unit(
+            pair,
             gain_ref[k : k + 1, :],
             bias_ref[k : k + 1, :],
             jax.nn.sigmoid(gate_ref[k : k + 1, :]),
             (in_high_ref, in_low_ref),
             (out_high_ref, out_low_ref),
             hidden_block,
+            wait_copies if step == 0 else lambda: None,
         )
         shape = (groups, 1, distance, width)
         states = jnp.concatenate(
-            [new_lower.reshape(shape), new_upper.reshape(shape)], axis=1
+            [out[:, :width].reshape(shape), out[:, width:].reshape(shape)], axis=1
         ).reshape(rows, width)
     y_ref[...] = states
 
@@ -80,12 +105,18 @@
     rows, width = states.shape
     hidden = params[1].shape[1]
     kernel = functools.partial(layers_kernel, first, distances, min(hidden, 256))
+    vmem = pl.BlockSpec(memory_space=pltpu.VMEM)
     return pl.pallas_call(
         kernel,
         out_shape=jax.ShapeDtypeStruct((rows, width), jnp.float32),
-        in_specs=[pl.BlockSpec(memory_space=pltpu.VMEM)] * 8,
-        out_specs=pl.BlockSpec(memory_space=pltpu.VMEM),
-        compiler_params=pltpu.CompilerParams(vmem_limit_bytes=24 * 2**20),
+        in_specs=[vmem] * 6 + [pl.BlockSpec(memory_space=pl.ANY)] * 2,
+        out_specs=vmem,
+        scratch_shapes=[
+            pltpu.VMEM(params[-2].shape, params[-2].dtype),
+            pltpu.VMEM(params[-1].shape, params[-1].dtype),
+            pltpu.SemaphoreType.DMA((2,)),
+        ],
+        compiler_params=pltpu.CompilerParams(vmem_limit_bytes=60 * 2**20),
         name=name,
     )(states, *params)
 
@@ -108,14 +139,14 @@
 
     params = (norm_gain, bias_hidden, gate_logit, *parts(w_in), *parts(w_out))
     if rows % (8 * high_count * low_count) == 0:
-        states = all_to_all(features, ("seqhi", "seqlo"))
-        distances = [rows // high_count * 2 ** (k % high_bits) for k in range(HI_LAYERS)]
+        block = rows // (high_count * low_count)
+        distances = [block * 2 ** (k % high_bits) for k in range(HI_LAYERS)]
         distances += [
-            rows // (high_count * low_count) * 2 ** (j % low_bits)
-            for j in range(layer_total - HI_LAYERS)
+            block * high_count * 2 ** (j % low_bits) for j in range(layer_total - HI_LAYERS)
         ]
+        states = all_to_all(features, ("seqlo", "seqhi"))
         states = run_layers(states, 0, distances, params, "all_layers")
-        return all_to_all(states, ("seqhi", "seqlo"))
+        return all_to_all(states, ("seqlo", "seqhi"))
     high_distances = [rows // high_count * 2 ** (k % high_bits) for k in range(HI_LAYERS)]
     low_distances = [rows // low_count * 2 ** (j % low_bits) for j in range(layer_total - HI_LAYERS)]
     states = all_to_all(features, "seqhi")

time: 44.1 us -> 46.4 us (1.052)
  Pallas kernels: 11.1 us -> 13.6 us
  other arithmetic: 3.49 us -> 5.16 us
  waiting for transfers between devices: 7.09 us -> 5.42 us
  local copies, waits for them, and re-layouts: 1.97 us -> 1.41 us
    pallas_call x1, Pallas kernels: 11.1 us -> 13.6 us  [run_layers(): pl.pallas_call(kernel, out_shape=jax.ShapeDtypeStruct((rows, width), jnp....]
    convert_element_type x2, other arithmetic: 3.49 us -> 5.16 us  [parts(): return (high.astype(jnp.bfloat16), (w - high).astype(jnp.bfloat16))]
    all_to_all x1, waiting for transfers between devices: 7.09 us -> 5.42 us  [all_to_all(): return lax.all_to_all(x, axes, split_axis=0, concat_axis=0, tiled=True)]
    unnamed x11 -> x5, local copies, waits for them, and re-layouts: 1.97 us -> 1.41 us
  transfers between devices with their start and end apart: 1 -> 1, of which waited for: 1 -> 1; matrix products, arithmetic and copies ran while one was open for 8% -> 11% of each run, Pallas kernels for 0% -> 0%
where the time goes in v6:
time: 46.4 us; the launch traced here: 46.1 us
  Pallas kernels  13.6 us (29%)
  blocking collectives  13.2 us (28%)
  starting transfers between devices  7.3 us (16%)
  waiting for transfers between devices  5.42 us (12%)
  other arithmetic  5.16 us (11%)
  local copies, waits for them, and re-layouts  1.41 us (3%)
    pallas_call x1, Pallas kernels, run_layers(): pl.pallas_call(kernel, out_shape=jax.ShapeDtypeStruct((rows, width), jnp....  13.6 us
    all_to_all x1, blocking collectives, all_to_all(): return lax.all_to_all(x, axes, split_axis=0, concat_axis=0, tiled=True)  13.2 us
    all_to_all x1, starting transfers between devices, all_to_all(): return lax.all_to_all(x, axes, split_axis=0, concat_axis=0, tiled=True)  7.3 us
    all_to_all x1, waiting for transfers between devices, all_to_all(): return lax.all_to_all(x, axes, split_axis=0, concat_axis=0, tiled=True)  5.42 us
    convert_element_type x2, other arithmetic, parts(): return (high.astype(jnp.bfloat16), (w - high).astype(jnp.bfloat16))  5.16 us
    unnamed x5, local copies, waits for them, and re-layouts  1.41 us
  transfers between devices with their start and end apart: 1, of which 1 were waited for; matrix products, arithmetic and copies ran while one was open for 11% of the time, Pallas kernels for 0%

profile of v6, /device:TPU:0, one launch (start us, length us, event | category | flops | bytes accessed | tf_op | source)
XLA Modules:
  0.0 46.1 jit_solution(7843914851883677927)
XLA Ops:
  0.0 7.3 %all-to-all-start = ((f32[32,8,256]{2,1,0:T(8,128)}), f32[32,8,256]{2,1,0:T(8,128)S(1)}, u32[]{:S(2)}, u32[]{:S(2)}) async-start(f32[32,8,256]{2,1,0:T(8,128)} %bitcast.7), calls=%async_computation | async-start | bytes 524288 | tf_op jit(solution)/shard_map/all_to_all | solution.py:125
  7.3 0.0 copy-start
  7.3 3.5 %fusion = (bf16[512,1024]{1,0:T(8,128)(2,1)}, bf16[512,1024]{1,0:T(8,128)(2,1)}) fusion(f32[512,1024]{1,0:T(8,128)} %param.10), kind=kLoop, calls=%fused_computation.4 | loop fusion | flops 2097152 | bytes 4194304 | tf_op jit(solution)/shard_map/convert_element_type | solution.py:138
  10.8 0.0 copy-done
  10.8 1.7 %fusion.1 = (bf16[1024,512]{1,0:T(8,128)(2,1)}, bf16[1024,512]{1,0:T(8,128)(2,1)}) fusion(f32[1024,512]{1,0:T(8,128)S(1)} %copy-done), kind=kLoop, calls=%fused_computation.5 | loop fusion | flops 2097152 | bytes 4194304 | tf_op jit(solution)/shard_map/convert_element_type | solution.py:138
  12.5 5.4 %all-to-all-done = f32[32,8,256]{2,1,0:T(8,128)S(1)} async-done(((f32[32,8,256]{2,1,0:T(8,128)}), f32[32,8,256]{2,1,0:T(8,128)S(1)}, u32[]{:S(2)}, u32[]{:S(2)}) %all-to-all-start) | async-done | bytes 262176 | tf_op jit(solution)/shard_map/all_to_all | solution.py:125
  17.9 0.0 copy-start.1
  17.9 0.7 %copy-done.1 = f32[32,8,256]{2,1,0:T(8,128)} copy-done((f32[32,8,256]{2,1,0:T(8,128)}, f32[32,8,256]{2,1,0:T(8,128)S(1)}, u32[]{:S(2)}) %copy-start.1) | copy-done | bytes 262168
  18.6 13.6 %all_layers.1 = f32[256,256]{1,0:T(8,128)} custom-call(f32[256,256]{1,0:T(8,128)} %bitcast.4, f32[8,512]{1,0:T(8,128)} %gain_ref.1, f32[8,1024]{1,0:T(8,128)} %bias_ref.1, f32[8,512]{1,0:T(8,128)} %gate_ref.1, bf16[512,1024]{1,0:T(8,128)(2,1)} %get-tuple-element.8.in_high_ref, bf16[512,1024]{1,0:T(8,128)(2,1)} %get-tuple-element.7.in_low_ref, ...), custom_call_target="tpu_custom_call" | custom-call | tf_op jit(solution)/shard_map/all_layers/pallas_call | solution.py:109
  32.2 13.2 %all_to_all.23 = f32[32,8,256]{2,1,0:T(8,128)S(1)} all-to-all(f32[32,8,256]{2,1,0:T(8,128)} %bitcast.5), channel_id=1, replica_groups=mesh['seqhi'=4,'seqlo'=8] {'seqlo','seqhi'}, dimensions={0} | all-to-all | bytes 524288 | tf_op jit(solution)/shard_map/all_to_all | solution.py:125
  45.4 0.7 %copy.8 = f32[256,256]{1,0:T(8,128)} copy(f32[256,256]{1,0:T(8,128)S(1)} %bitcast.6) | data formatting | bytes 524288
Async XLA Ops:
  0.0 17.9 %all-to-all-start = ((f32[32,8,256]{2,1,0:T(8,128)}), f32[32,8,256]{2,1,0:T(8,128)S(1)}, u32[]{:S(2)}, u32[]{:S(2)}) async-start(f32[32,8,256]{2,1,0:T(8,128)} %bitcast.7), calls=%async_computation | async-start | bytes 524288 | tf_op jit(solution)/shard_map/all_to_all | solution.py:125
  7.3 3.5 %copy-start = (f32[1024,512]{1,0:T(8,128)S(1)}, f32[1024,512]{1,0:T(8,128)}, u32[]{:S(2)}) copy-start(f32[1024,512]{1,0:T(8,128)} %param.11) | copy-start | bytes 6291460
  17.9 0.7 %copy-start.1 = (f32[32,8,256]{2,1,0:T(8,128)}, f32[32,8,256]{2,1,0:T(8,128)S(1)}, u32[]{:S(2)}) copy-start(f32[32,8,256]{2,1,0:T(8,128)S(1)} %all-to-all-done) | copy-start | bytes 786436

commit v7 on v6

--- a/solution.py
+++ b/solution.py
@@ -22,11 +22,14 @@
     return jnp.dot(a, b, preferred_element_type=jnp.float32)
 
 
-def dot_split(x, w_high, w_low):
-    rows = x.shape[0]
-    x_high, x_low = split_high_low(x)
+def dot_parts(x_high, x_low, w_high, w_low):
+    rows = x_high.shape[0]
     both = dot(jnp.concatenate([x_high, x_low], axis=0), w_high)
     return both[:rows] + (both[rows:] + dot(x_high, w_low))
+
+
+def dot_split(x, w_high, w_low):
+    return dot_parts(*split_high_low(x), w_high, w_low)
 
 
 def gelu(x):
@@ -44,29 +47,24 @@
     hidden_count = in_high.shape[1]
     blocks = [slice(c, c + hidden_block) for c in range(0, hidden_count, hidden_block)]
 
-    def enter(cols):
-        return dot_split(normed, in_high[:, cols], in_low[:, cols]) + bias[:, cols]
-
-    ahead = enter(blocks[0])
-    for number, cols in enumerate(blocks):
-        entered = ahead
-        if number + 1 < len(blocks):
-            ahead = enter(blocks[number + 1])
-        hidden = gelu(entered)
-        if number == 0:
-            out_ready()
-        out = out + dot_split(hidden, out_high[cols, :], out_low[cols, :])
-    return out
+    parts = []
+    for cols in blocks:
+        entered = dot_split(normed, in_high[:, cols], in_low[:, cols]) + bias[:, cols]
+        parts.append(split_high_low(gelu(entered)))
+    high = jnp.concatenate([part[0] for part in parts], axis=1)
+    low = jnp.concatenate([part[1] for part in parts], axis=1)
+    out_ready()
+    return out + dot_parts(high, low, out_high[...], out_low[...])
 
 
 def layers_kernel(
     first, distances, hidden_block,
-    x_ref, gain_ref, bias_ref, gate_ref, in_high_ref, in_low_ref, out_high_hbm, out_low_hbm,
+    x_ref, gain_ref, bias_ref, gate_ref, in_high_ref, in_low_ref, out_high_any, out_low_any,
     y_ref, out_high_ref, out_low_ref, copied,
 ):
     copies = [
-        pltpu.make_async_copy(out_high_hbm, out_high_ref, copied.at[0]),
-        pltpu.make_async_copy(out_low_hbm, out_low_ref, copied.at[1]),
+        pltpu.make_async_copy(out_high_any, out_high_ref, copied.at[0]),
+        pltpu.make_async_copy(out_low_any, out_low_ref, copied.at[1]),
     ]
     for copy in copies:
         copy.start()
@@ -116,7 +114,7 @@
             pltpu.VMEM(params[-1].shape, params[-1].dtype),
             pltpu.SemaphoreType.DMA((2,)),
         ],
-        compiler_params=pltpu.CompilerParams(vmem_limit_bytes=60 * 2**20),
+        compiler_params=pltpu.CompilerParams(vmem_limit_bytes=51 * 2**20),
         name=name,
     )(states, *params)
 
@@ -140,13 +138,11 @@
     params = (norm_gain, bias_hidden, gate_logit, *parts(w_in), *parts(w_out))
     if rows % (8 * high_count * low_count) == 0:
         block = rows // (high_count * low_count)
-        distances = [block * 2 ** (k % high_bits) for k in range(HI_LAYERS)]
-        distances += [
-            block * high_count * 2 ** (j % low_bits) for j in range(layer_total - HI_LAYERS)
-        ]
-        states = all_to_all(features, ("seqlo", "seqhi"))
+        distances = [block * low_count * 2 ** (k % high_bits) for k in range(HI_LAYERS)]
+        distances += [block * 2 ** (j % low_bits) for j in range(layer_total - HI_LAYERS)]
+        states = all_to_all(features, ("seqhi", "seqlo"))
         states = run_layers(states, 0, distances, params, "all_layers")
-        return all_to_all(states, ("seqlo", "seqhi"))
+        return all_to_all(states, ("seqhi", "seqlo"))
     high_distances = [rows // high_count * 2 ** (k % high_bits) for k in range(HI_LAYERS)]
     low_distances = [rows // low_count * 2 ** (j % low_bits) for j in range(layer_total - HI_LAYERS)]
     states = all_to_all(features, "seqhi")

time: 46.4 us -> 41.8 us (0.901)
  Pallas kernels: 13.6 us -> 10.1 us
  waiting for transfers between devices: 5.42 us -> 6.73 us
  other arithmetic: 5.16 us -> 3.85 us
  local copies, waits for them, and re-layouts: 1.41 us -> 0.76 us
    pallas_call x1, Pallas kernels: 13.6 us -> 10.1 us  [run_layers(): pl.pallas_call(kernel, out_shape=jax.ShapeDtypeStruct((rows, width), jnp....]
    convert_element_type x2, other arithmetic: 5.16 us -> 3.85 us  [parts(): return (high.astype(jnp.bfloat16), (w - high).astype(jnp.bfloat16))]
    all_to_all x1, waiting for transfers between devices: 5.42 us -> 6.73 us  [all_to_all(): return lax.all_to_all(x, axes, split_axis=0, concat_axis=0, tiled=True)]
    unnamed x5 -> x9, local copies, waits for them, and re-layouts: 1.41 us -> 0.76 us
  transfers between devices with their start and end apart: 1 -> 1, of which waited for: 1 -> 1; matrix products, arithmetic and copies ran while one was open for 11% -> 9% of each run, Pallas kernels for 0% -> 0%
where the time goes in v7:
time: 41.8 us; the launch traced here: 41.5 us
  blocking collectives  12.8 us (31%)
  Pallas kernels  10.1 us (24%)
  starting transfers between devices  7.3 us (17%)
  waiting for transfers between devices  6.73 us (16%)
  other arithmetic  3.85 us (9%)
  local copies, waits for them, and re-layouts  0.76 us (2%)
    all_to_all x1, blocking collectives, all_to_all(): return lax.all_to_all(x, axes, split_axis=0, concat_axis=0, tiled=True)  12.8 us
    pallas_call x1, Pallas kernels, run_layers(): pl.pallas_call(kernel, out_shape=jax.ShapeDtypeStruct((rows, width), jnp....  10.1 us
    all_to_all x1, starting transfers between devices, all_to_all(): return lax.all_to_all(x, axes, split_axis=0, concat_axis=0, tiled=True)  7.3 us
    all_to_all x1, waiting for transfers between devices, all_to_all(): return lax.all_to_all(x, axes, split_axis=0, concat_axis=0, tiled=True)  6.73 us
    convert_element_type x2, other arithmetic, parts(): return (high.astype(jnp.bfloat16), (w - high).astype(jnp.bfloat16))  3.85 us
  transfers between devices with their start and end apart: 1, of which 1 were waited for; matrix products, arithmetic and copies ran while one was open for 9% of the time, Pallas kernels for 0%

profile of v7, /device:TPU:0, one launch (start us, length us, event | category | flops | bytes accessed | tf_op | source)
XLA Modules:
  0.0 41.5 jit_solution(795075557768301465)
XLA Ops:
  0.0 7.3 %all-to-all-start = ((f32[32,8,256]{2,1,0:T(8,128)}), f32[32,8,256]{2,1,0:T(8,128)S(1)}, u32[]{:S(2)}, u32[]{:S(2)}) async-start(f32[32,8,256]{2,1,0:T(8,128)} %bitcast.7), calls=%async_computation | async-start | bytes 524288 | tf_op jit(solution)/shard_map/all_to_all | solution.py:123
  7.3 0.0 copy-start.3
  7.3 2.2 %fusion = (bf16[512,1024]{1,0:T(8,128)(2,1)S(1)}, bf16[512,1024]{1,0:T(8,128)(2,1)S(1)}) fusion(f32[512,1024]{1,0:T(8,128)} %param.10), kind=kLoop, calls=%fused_computation.4 | loop fusion | flops 2097152 | bytes 4194304 | tf_op jit(solution)/shard_map/convert_element_type | solution.py:136
  9.5 0.0 copy-done.3
  9.5 0.0 copy-start
  9.5 0.0 copy-start.1
  9.5 0.0 copy-start.2
  9.5 1.7 %fusion.1 = (bf16[1024,512]{1,0:T(8,128)(2,1)}, bf16[1024,512]{1,0:T(8,128)(2,1)}) fusion(f32[1024,512]{1,0:T(8,128)S(1)} %copy-done.3), kind=kLoop, calls=%fused_computation.5 | loop fusion | flops 2097152 | bytes 4194304 | tf_op jit(solution)/shard_map/convert_element_type | solution.py:136
  11.2 6.7 %all-to-all-done = f32[32,8,256]{2,1,0:T(8,128)S(1)} async-done(((f32[32,8,256]{2,1,0:T(8,128)}), f32[32,8,256]{2,1,0:T(8,128)S(1)}, u32[]{:S(2)}, u32[]{:S(2)}) %all-to-all-start) | async-done | bytes 262176 | tf_op jit(solution)/shard_map/all_to_all | solution.py:123
  18.0 0.0 copy-done
  18.0 0.0 copy-done.1
  18.0 0.0 copy-done.2
  18.0 10.1 %all_layers.1 = f32[256,256]{1,0:T(8,128)S(1)} custom-call(f32[256,256]{1,0:T(8,128)S(1)} %bitcast.4, f32[8,512]{1,0:T(8,128)S(1)} %copy-done.1, f32[8,1024]{1,0:T(8,128)S(1)} %copy-done, f32[8,512]{1,0:T(8,128)S(1)} %copy-done.2, bf16[512,1024]{1,0:T(8,128)(2,1)S(1)} %get-tuple-element.8.in_high_ref, bf16[512,1024]{1,0:T(8,128)(2,1)S(1)} %get-tuple-element.7.in_low_ref, ...), custom_call_target="tpu_custom_call" | custom-call | tf_op jit(solution)/shard_map/all_layers/pallas_call | solution.py:107
  28.0 12.8 %all_to_all.23 = f32[32,8,256]{2,1,0:T(8,128)S(1)} all-to-all(f32[32,8,256]{2,1,0:T(8,128)S(1)} %bitcast.5), channel_id=1, replica_groups=mesh['seqhi'=4,'seqlo'=8] {'seqhi','seqlo'}, dimensions={0} | all-to-all | bytes 524288 | tf_op jit(solution)/shard_map/all_to_all | solution.py:123
  40.8 0.7 %copy.8 = f32[256,256]{1,0:T(8,128)} copy(f32[256,256]{1,0:T(8,128)S(1)} %bitcast.6) | data formatting | bytes 524288
Async XLA Ops:
  0.0 18.0 %all-to-all-start = ((f32[32,8,256]{2,1,0:T(8,128)}), f32[32,8,256]{2,1,0:T(8,128)S(1)}, u32[]{:S(2)}, u32[]{:S(2)}) async-start(f32[32,8,256]{2,1,0:T(8,128)} %bitcast.7), calls=%async_computation | async-start | bytes 524288 | tf_op jit(solution)/shard_map/all_to_all | solution.py:123
  7.3 2.2 %copy-start.3 = (f32[1024,512]{1,0:T(8,128)S(1)}, f32[1024,512]{1,0:T(8,128)}, u32[]{:S(2)}) copy-start(f32[1024,512]{1,0:T(8,128)} %param.11) | copy-start | bytes 6291460
  9.5 8.4 %copy-start = (f32[8,1024]{1,0:T(8,128)S(1)}, f32[8,1024]{1,0:T(8,128)}, u32[]{:S(2)}) copy-start(f32[8,1024]{1,0:T(8,128)} %bias_ref.1) | copy-start | bytes 98308
  9.5 8.4 %copy-start.1 = (f32[8,512]{1,0:T(8,128)S(1)}, f32[8,512]{1,0:T(8,128)}, u32[]{:S(2)}) copy-start(f32[8,512]{1,0:T(8,128)} %gain_ref.1) | copy-start | bytes 49156
  9.5 8.4 %copy-start.2 = (f32[8,512]{1,0:T(8,128)S(1)}, f32[8,512]{1,0:T(8,128)}, u32[]{:S(2)}) copy-start(f32[8,512]{1,0:T(8,128)} %gate_ref.1) | copy-start | bytes 49156

commit v8 on v7

--- a/solution.py
+++ b/solution.py
@@ -18,49 +18,50 @@
     return high, (x - high.astype(jnp.float32)).astype(jnp.bfloat16)
 
 
-def dot(a, b):
-    return jnp.dot(a, b, preferred_element_type=jnp.float32)
-
-
-def dot_parts(x_high, x_low, w_high, w_low):
-    rows = x_high.shape[0]
-    both = dot(jnp.concatenate([x_high, x_low], axis=0), w_high)
-    return both[:rows] + (both[rows:] + dot(x_high, w_low))
-
-
-def dot_split(x, w_high, w_low):
-    return dot_parts(*split_high_low(x), w_high, w_low)
-
-
 def gelu(x):
     half = 0.5 * x
     return half + half * jnp.tanh(x * (GELU_SCALE + (GELU_SCALE * GELU_CUBE) * (x * x)))
 
 
-def switch_unit(pair, gain, bias, gate, w_in, w_out, hidden_block, out_ready):
-    center = pair - jnp.mean(pair, axis=-1, keepdims=True)
-    spread = jnp.mean(center * center, axis=-1, keepdims=True)
-    normed = center * lax.rsqrt(spread + NORM_EPS) * gain
-    out = gate * pair
-    in_high, in_low = w_in
-    out_high, out_low = w_out
-    hidden_count = in_high.shape[1]
-    blocks = [slice(c, c + hidden_block) for c in range(0, hidden_count, hidden_block)]
-
-    parts = []
-    for cols in blocks:
-        entered = dot_split(normed, in_high[:, cols], in_low[:, cols]) + bias[:, cols]
-        parts.append(split_high_low(gelu(entered)))
-    high = jnp.concatenate([part[0] for part in parts], axis=1)
-    low = jnp.concatenate([part[1] for part in parts], axis=1)
-    out_ready()
-    return out + dot_parts(high, low, out_high[...], out_low[...])
+class Units:
+    def __init__(self, sequences):
+        self.sequences = [iter(sequence) for sequence in sequences]
+        self.register = [0] * len(sequences)
+        for unit in range(len(sequences)):
+            self.push(unit, 0)
+
+    def push(self, unit, register):
+        tile = next(self.sequences[unit], None)
+        if tile is not None:
+            pltpu.matmul_push_rhs(tile(), register, unit)
+
+    def multiply(self, unit, acc, operands):
+        register = self.register[unit]
+        self.register[unit] = 1 - register
+        self.push(unit, 1 - register)
+        for number, operand in enumerate(operands):
+            pltpu.matmul_acc_lhs(acc, operand, load_staged_rhs=register if number == 0 else None)
 
 
 def layers_kernel(
-    first, distances, hidden_block,
+    first, distances, units_count, tile, acc_types,
     x_ref, gain_ref, bias_ref, gate_ref, in_high_ref, in_low_ref, out_high_any, out_low_any,
     y_ref, out_high_ref, out_low_ref, copied,
+):
+    pl.run_scoped(
+        functools.partial(
+            layers_body, first, distances, units_count, tile,
+            x_ref, gain_ref, bias_ref, gate_ref, in_high_ref, in_low_ref, out_high_any, out_low_any,
+            y_ref, out_high_ref, out_low_ref, copied,
+        ),
+        *acc_types,
+    )
+
+
+def layers_body(
+    first, distances, units_count, tile,
+    x_ref, gain_ref, bias_ref, gate_ref, in_high_ref, in_low_ref, out_high_any, out_low_any,
+    y_ref, out_high_ref, out_low_ref, copied, *accs,
 ):
     copies = [
         pltpu.make_async_copy(out_high_any, out_high_ref, copied.at[0]),
@@ -68,12 +69,35 @@
     ]
     for copy in copies:
         copy.start()
-
-    def wait_copies():
-        for copy in copies:
-            copy.wait()
+    pending = list(copies)
 
     rows, width = x_ref.shape
+    pair_width, hidden_count = in_high_ref.shape
+    in_tiles, hidden_tiles, out_tiles = pair_width // tile, hidden_count // tile, pair_width // tile
+    hidden_accs, out_accs = accs[:hidden_tiles], accs[hidden_tiles:]
+
+    def span(index):
+        return slice(index * tile, (index + 1) * tile)
+
+    def loader(ref, row, col, late):
+        def load():
+            while late and pending:
+                pending.pop().wait()
+            return ref[span(row), span(col)]
+        return load
+
+    def sequence(unit):
+        for _ in distances:
+            for col in range(unit, hidden_tiles, units_count):
+                for row in range(in_tiles):
+                    yield loader(in_high_ref, row, col, False)
+                    yield loader(in_low_ref, row, col, False)
+            for row in range(hidden_tiles):
+                for col in range(unit, out_tiles, units_count):
+                    yield loader(out_high_ref, row, col, True)
+                    yield loader(out_low_ref, row, col, True)
+
+    units = Units([sequence(unit) for unit in range(units_count)])
     states = x_ref[...]
     for step, distance in enumerate(distances):
         k = first + step
@@ -82,16 +106,25 @@
         pair = jnp.concatenate(
             [grouped[:, 0].reshape(-1, width), grouped[:, 1].reshape(-1, width)], axis=-1
         )
-        out = switch_unit(
-            pair,
-            gain_ref[k : k + 1, :],
-            bias_ref[k : k + 1, :],
-            jax.nn.sigmoid(gate_ref[k : k + 1, :]),
-            (in_high_ref, in_low_ref),
-            (out_high_ref, out_low_ref),
-            hidden_block,
-            wait_copies if step == 0 else lambda: None,
-        )
+        center = pair - jnp.mean(pair, axis=-1, keepdims=True)
+        spread = jnp.mean(center * center, axis=-1, keepdims=True)
+        normed = center * lax.rsqrt(spread + NORM_EPS) * gain_ref[k : k + 1, :]
+        high, low = split_high_low(normed)
+        for start in range(0, hidden_tiles, units_count):
+            for row in range(in_tiles):
+                x_high, x_low = high[:, span(row)], low[:, span(row)]
+                for operands in ((x_high, x_low), (x_high,)):
+                    for unit in range(units_count):
+                        units.multiply(unit, hidden_accs[start + unit], operands)
+        for row in range(hidden_tiles):
+            entered = pltpu.matmul_pop(hidden_accs[row]) + bias_ref[k : k + 1, span(row)]
+            h_high, h_low = split_high_low(gelu(entered))
+            for start in range(0, out_tiles, units_count):
+                for operands in ((h_high, h_low), (h_high,)):
+                    for unit in range(units_count):
+                        units.multiply(unit, out_accs[start + unit], operands)
+        mixed = jnp.concatenate([pltpu.matmul_pop(acc) for acc in out_accs], axis=1)
+        out = jax.nn.sigmoid(gate_ref[k : k + 1, :]) * pair + mixed
         shape = (groups, 1, distance, width)
         states = jnp.concatenate(
             [out[:, :width].reshape(shape), out[:, width:].reshape(shape)], axis=1
@@ -101,8 +134,15 @@
 
 def run_layers(states, first, distances, params, name):
     rows, width = states.shape
-    hidden = params[1].shape[1]
-    kernel = functools.partial(layers_kernel, first, distances, min(hidden, 256))
+    pair_width, hidden = params[3].shape
+    info = pltpu.get_tpu_info()
+    units, tile = info.num_mxus, info.mxu_column_size
+    acc_types = [
+        pltpu.ACC(i % units)((rows // 2, tile), jnp.float32)
+        for count in (hidden // tile, pair_width // tile)
+        for i in range(count)
+    ]
+    kernel = functools.partial(layers_kernel, first, distances, units, tile, acc_types)
     vmem = pl.BlockSpec(memory_space=pltpu.VMEM)
     return pl.pallas_call(
         kernel,

time: 41.8 us -> 42 us (level)
  no operation moved by 1% of the time
where the time goes in v8:
time: 42 us; the launch traced here: 41.8 us
  blocking collectives  12.8 us (30%)
  Pallas kernels  10.3 us (25%)
  starting transfers between devices  7.3 us (17%)
  waiting for transfers between devices  6.73 us (16%)
  other arithmetic  3.85 us (9%)
  local copies, waits for them, and re-layouts  0.76 us (2%)
    all_to_all x1, blocking collectives, all_to_all(): return lax.all_to_all(x, axes, split_axis=0, concat_axis=0, tiled=True)  12.8 us
    pallas_call x1, Pallas kernels, run_layers(): pl.pallas_call(kernel, out_shape=jax.ShapeDtypeStruct((rows, width), jnp....  10.3 us
    all_to_all x1, starting transfers between devices, all_to_all(): return lax.all_to_all(x, axes, split_axis=0, concat_axis=0, tiled=True)  7.3 us
    all_to_all x1, waiting for transfers between devices, all_to_all(): return lax.all_to_all(x, axes, split_axis=0, concat_axis=0, tiled=True)  6.73 us
    convert_element_type x2, other arithmetic, parts(): return (high.astype(jnp.bfloat16), (w - high).astype(jnp.bfloat16))  3.85 us
  transfers between devices with their start and end apart: 1, of which 1 were waited for; matrix products, arithmetic and copies ran while one was open for 9% of the time, Pallas kernels for 0%

profile of v8, /device:TPU:0, one launch (start us, length us, event | category | flops | bytes accessed | tf_op | source)
XLA Modules:
  0.0 41.8 jit_solution(13312322684379403846)
XLA Ops:
  0.0 7.3 %all-to-all-start = ((f32[32,8,256]{2,1,0:T(8,128)}), f32[32,8,256]{2,1,0:T(8,128)S(1)}, u32[]{:S(2)}, u32[]{:S(2)}) async-start(f32[32,8,256]{2,1,0:T(8,128)} %bitcast.7), calls=%async_computation | async-start | bytes 524288 | tf_op jit(solution)/shard_map/all_to_all | solution.py:163
  7.3 0.0 copy-start.3
  7.3 2.2 %fusion = (bf16[512,1024]{1,0:T(8,128)(2,1)S(1)}, bf16[512,1024]{1,0:T(8,128)(2,1)S(1)}) fusion(f32[512,1024]{1,0:T(8,128)} %param.10), kind=kLoop, calls=%fused_computation.4 | loop fusion | flops 2097152 | bytes 4194304 | tf_op jit(solution)/shard_map/convert_element_type | solution.py:176
  9.5 0.0 copy-done.3
  9.5 0.0 copy-start
  9.5 0.0 copy-start.1
  9.5 0.0 copy-start.2
  9.5 1.7 %fusion.1 = (bf16[1024,512]{1,0:T(8,128)(2,1)}, bf16[1024,512]{1,0:T(8,128)(2,1)}) fusion(f32[1024,512]{1,0:T(8,128)S(1)} %copy-done.3), kind=kLoop, calls=%fused_computation.5 | loop fusion | flops 2097152 | bytes 4194304 | tf_op jit(solution)/shard_map/convert_element_type | solution.py:176
  11.2 6.7 %all-to-all-done = f32[32,8,256]{2,1,0:T(8,128)S(1)} async-done(((f32[32,8,256]{2,1,0:T(8,128)}), f32[32,8,256]{2,1,0:T(8,128)S(1)}, u32[]{:S(2)}, u32[]{:S(2)}) %all-to-all-start) | async-done | bytes 262176 | tf_op jit(solution)/shard_map/all_to_all | solution.py:163
  18.0 0.0 copy-done
  18.0 0.0 copy-done.1
  18.0 0.0 copy-done.2
  18.0 10.3 %all_layers.1 = f32[256,256]{1,0:T(8,128)S(1)} custom-call(f32[256,256]{1,0:T(8,128)S(1)} %bitcast.4, f32[8,512]{1,0:T(8,128)S(1)} %copy-done.1, f32[8,1024]{1,0:T(8,128)S(1)} %copy-done, f32[8,512]{1,0:T(8,128)S(1)} %copy-done.2, bf16[512,1024]{1,0:T(8,128)(2,1)S(1)} %get-tuple-element.8.in_high_ref, bf16[512,1024]{1,0:T(8,128)(2,1)S(1)} %get-tuple-element.7.in_low_ref, ...), custom_call_target="tpu_custom_call" | custom-call | tf_op jit(solution)/shard_map/all_layers/pallas_call | solution.py:147
  28.3 12.8 %all_to_all.23 = f32[32,8,256]{2,1,0:T(8,128)S(1)} all-to-all(f32[32,8,256]{2,1,0:T(8,128)S(1)} %bitcast.5), channel_id=1, replica_groups=mesh['seqhi'=4,'seqlo'=8] {'seqhi','seqlo'}, dimensions={0} | all-to-all | bytes 524288 | tf_op jit(solution)/shard_map/all_to_all | solution.py:163
  41.1 0.7 %copy.8 = f32[256,256]{1,0:T(8,128)} copy(f32[256,256]{1,0:T(8,128)S(1)} %bitcast.6) | data formatting | bytes 524288
Async XLA Ops:
  0.0 18.0 %all-to-all-start = ((f32[32,8,256]{2,1,0:T(8,128)}), f32[32,8,256]{2,1,0:T(8,128)S(1)}, u32[]{:S(2)}, u32[]{:S(2)}) async-start(f32[32,8,256]{2,1,0:T(8,128)} %bitcast.7), calls=%async_computation | async-start | bytes 524288 | tf_op jit(solution)/shard_map/all_to_all | solution.py:163
  7.3 2.2 %copy-start.3 = (f32[1024,512]{1,0:T(8,128)S(1)}, f32[1024,512]{1,0:T(8,128)}, u32[]{:S(2)}) copy-start(f32[1024,512]{1,0:T(8,128)} %param.11) | copy-start | bytes 6291460
  9.5 8.4 %copy-start = (f32[8,1024]{1,0:T(8,128)S(1)}, f32[8,1024]{1,0:T(8,128)}, u32[]{:S(2)}) copy-start(f32[8,1024]{1,0:T(8,128)} %bias_ref.1) | copy-start | bytes 98308
  9.5 8.4 %copy-start.1 = (f32[8,512]{1,0:T(8,128)S(1)}, f32[8,512]{1,0:T(8,128)}, u32[]{:S(2)}) copy-start(f32[8,512]{1,0:T(8,128)} %gain_ref.1) | copy-start | bytes 49156
  9.5 8.4 %copy-start.2 = (f32[8,512]{1,0:T(8,128)S(1)}, f32[8,512]{1,0:T(8,128)}, u32[]{:S(2)}) copy-start(f32[8,512]{1,0:T(8,128)} %gate_ref.1) | copy-start | bytes 49156

commit v9 on v8

--- a/solution.py
+++ b/solution.py
@@ -9,6 +9,7 @@
 
 HI_LAYERS = 4
 NORM_EPS = 1e-05
+CHUNK_ROWS = 32
 GELU_SCALE = 0.7978845608028654
 GELU_CUBE = 0.044715
 
@@ -26,21 +27,23 @@
 class Units:
     def __init__(self, sequences):
         self.sequences = [iter(sequence) for sequence in sequences]
-        self.register = [0] * len(sequences)
-        for unit in range(len(sequences)):
-            self.push(unit, 0)
-
-    def push(self, unit, register):
-        tile = next(self.sequences[unit], None)
-        if tile is not None:
-            pltpu.matmul_push_rhs(tile(), register, unit)
-
-    def multiply(self, unit, acc, operands):
-        register = self.register[unit]
-        self.register[unit] = 1 - register
-        self.push(unit, 1 - register)
-        for number, operand in enumerate(operands):
-            pltpu.matmul_acc_lhs(acc, operand, load_staged_rhs=register if number == 0 else None)
+        self.register = 0
+        self.push(0)
+
+    def push(self, register):
+        for unit, sequence in enumerate(self.sequences):
+            tile = next(sequence, None)
+            if tile is not None:
+                pltpu.matmul_push_rhs(tile(), register, unit)
+
+    def multiply(self, feed):
+        register = self.register
+        self.register = 1 - register
+        self.push(1 - register)
+        fresh = [True] * len(self.sequences)
+        for unit, acc, operand in feed:
+            pltpu.matmul_acc_lhs(acc, operand, load_staged_rhs=register if fresh[unit] else None)
+            fresh[unit] = False
 
 
 def layers_kernel(
@@ -98,38 +101,84 @@
                     yield loader(out_low_ref, row, col, True)
 
     units = Units([sequence(unit) for unit in range(units_count)])
-    states = x_ref[...]
+    chunks = len(hidden_accs[0])
+    chunk = rows // 2 // chunks
+    hidden_groups = [
+        range(start, start + units_count) for start in range(0, hidden_tiles, units_count)
+    ]
+    out_groups = [range(start, start + units_count) for start in range(0, out_tiles, units_count)]
+
+    def pair_spans(number, distance):
+        piece = min(chunk, distance)
+        for index in range(number * chunk, (number + 1) * chunk, piece):
+            start = index // distance * 2 * distance + index % distance
+            yield start, piece
+
+    def pair_rows(ref, number, distance):
+        spans = list(pair_spans(number, distance))
+        sides = [
+            jnp.concatenate([ref[s + side : s + side + n, :] for s, n in spans], axis=0)
+            for side in (0, distance)
+        ]
+        return jnp.concatenate(sides, axis=1)
+
+    def layer(k, distance, source):
+        normed, hidden = {}, {}
+
+        def norm(number):
+            if number not in normed:
+                pair = pair_rows(source, number, distance)
+                center = pair - jnp.mean(pair, axis=-1, keepdims=True)
+                spread = jnp.mean(center * center, axis=-1, keepdims=True)
+                normed[number] = split_high_low(
+                    center * lax.rsqrt(spread + NORM_EPS) * gain_ref[k : k + 1, :]
+                )
+            return normed[number]
+
+        def activate(row, number):
+            if (row, number) not in hidden:
+                entered = pltpu.matmul_pop(hidden_accs[row][number])
+                hidden[row, number] = split_high_low(gelu(entered + bias_ref[k : k + 1, span(row)]))
+            return hidden[row, number]
+
+        def feed(group, accs, operand_of, low_too, tasks):
+            for number in range(chunks):
+                operands = operand_of(number)
+                for operand in operands if low_too else operands[:1]:
+                    for unit, col in enumerate(group):
+                        yield unit, accs[col][number], operand
+                if number % 2 and tasks:
+                    activate(*tasks.pop(0))
+
+        def normed_part(row):
+            return lambda number: [part[:, span(row)] for part in norm(number)]
+
+        tasks = []
+        for group in hidden_groups:
+            for row in range(in_tiles):
+                for low_too in (True, False):
+                    units.multiply(feed(group, hidden_accs, normed_part(row), low_too, tasks))
+            tasks += [(row, number) for row in group for number in range(chunks)]
+        for row in range(hidden_tiles):
+            tasks = [task for task in tasks if task[0] > row or task not in hidden]
+            for group in out_groups:
+                for low_too in (True, False):
+                    units.multiply(
+                        feed(group, out_accs, functools.partial(activate, row), low_too, tasks)
+                    )
+        gate = jax.nn.sigmoid(gate_ref[k : k + 1, :])
+        for number in range(chunks):
+            mixed = jnp.concatenate([pltpu.matmul_pop(accs[number]) for accs in out_accs], axis=1)
+            out = gate * pair_rows(source, number, distance) + mixed
+            done = 0
+            for start, piece in pair_spans(number, distance):
+                block = out[done : done + piece]
+                y_ref[start : start + piece, :] = block[:, :width]
+                y_ref[start + distance : start + distance + piece, :] = block[:, width:]
+                done += piece
+
     for step, distance in enumerate(distances):
-        k = first + step
-        groups = rows // (2 * distance)
-        grouped = states.reshape(groups, 2, distance, width)
-        pair = jnp.concatenate(
-            [grouped[:, 0].reshape(-1, width), grouped[:, 1].reshape(-1, width)], axis=-1
-        )
-        center = pair - jnp.mean(pair, axis=-1, keepdims=True)
-        spread = jnp.mean(center * center, axis=-1, keepdims=True)
-        normed = center * lax.rsqrt(spread + NORM_EPS) * gain_ref[k : k + 1, :]
-        high, low = split_high_low(normed)
-        for start in range(0, hidden_tiles, units_count):
-            for row in range(in_tiles):
-                x_high, x_low = high[:, span(row)], low[:, span(row)]
-                for operands in ((x_high, x_low), (x_high,)):
-                    for unit in range(units_count):
-                        units.multiply(unit, hidden_accs[start + unit], operands)
-        for row in range(hidden_tiles):
-            entered = pltpu.matmul_pop(hidden_accs[row]) + bias_ref[k : k + 1, span(row)]
-            h_high, h_low = split_high_low(gelu(entered))
-            for start in range(0, out_tiles, units_count):
-                for operands in ((h_high, h_low), (h_high,)):
-                    for unit in range(units_count):
-                        units.multiply(unit, out_accs[start + unit], operands)
-        mixed = jnp.concatenate([pltpu.matmul_pop(acc) for acc in out_accs], axis=1)
-        out = jax.nn.sigmoid(gate_ref[k : k + 1, :]) * pair + mixed
-        shape = (groups, 1, distance, width)
-        states = jnp.concatenate(
-            [out[:, :width].reshape(shape), out[:, width:].reshape(shape)], axis=1
-        ).reshape(rows, width)
-    y_ref[...] = states
+        layer(first + step, distance, x_ref if step == 0 else y_ref)
 
 
 def run_layers(states, first, distances, params, name):
@@ -137,8 +186,12 @@
     pair_width, hidden = params[3].shape
     info = pltpu.get_tpu_info()
     units, tile = info.num_mxus, info.mxu_column_size
+    chunk = min(rows // 2, CHUNK_ROWS)
     acc_types = [
-        pltpu.ACC(i % units)((rows // 2, tile), jnp.float32)
+        [
+            pltpu.ACC(i % units)((chunk, tile), jnp.float32)
+            for _ in range(rows // 2 // chunk)
+        ]
         for count in (hidden // tile, pair_width // tile)
         for i in range(count)
     ]

time: 42 us -> 42.3 us (level)
  no operation moved by 1% of the time
where the time goes in v9:
time: 42.3 us; the launch traced here: 42.1 us
  blocking collectives  12.8 us (30%)
  Pallas kernels  10.6 us (25%)
  starting transfers between devices  7.3 us (17%)
  waiting for transfers between devices  6.73 us (16%)
  other arithmetic  3.85 us (9%)
  local copies, waits for them, and re-layouts  0.76 us (2%)
    all_to_all x1, blocking collectives, all_to_all(): return lax.all_to_all(x, axes, split_axis=0, concat_axis=0, tiled=True)  12.8 us
    pallas_call x1, Pallas kernels, run_layers(): pl.pallas_call(kernel, out_shape=jax.ShapeDtypeStruct((rows, width), jnp....  10.6 us
    all_to_all x1, starting transfers between devices, all_to_all(): return lax.all_to_all(x, axes, split_axis=0, concat_axis=0, tiled=True)  7.3 us
    all_to_all x1, waiting for transfers between devices, all_to_all(): return lax.all_to_all(x, axes, split_axis=0, concat_axis=0, tiled=True)  6.73 us
    convert_element_type x2, other arithmetic, parts(): return (high.astype(jnp.bfloat16), (w - high).astype(jnp.bfloat16))  3.85 us
  transfers between devices with their start and end apart: 1, of which 1 were waited for; matrix products, arithmetic and copies ran while one was open for 9% of the time, Pallas kernels for 0%

profile of v9, /device:TPU:0, one launch (start us, length us, event | category | flops | bytes accessed | tf_op | source)
XLA Modules:
  0.0 42.1 jit_solution(4753438198116076514)
XLA Ops:
  0.0 7.3 %all-to-all-start = ((f32[32,8,256]{2,1,0:T(8,128)}), f32[32,8,256]{2,1,0:T(8,128)S(1)}, u32[]{:S(2)}, u32[]{:S(2)}) async-start(f32[32,8,256]{2,1,0:T(8,128)} %bitcast.7), calls=%async_computation | async-start | bytes 524288 | tf_op jit(solution)/shard_map/all_to_all | solution.py:216
  7.3 0.0 copy-start.3
  7.3 2.2 %fusion = (bf16[512,1024]{1,0:T(8,128)(2,1)S(1)}, bf16[512,1024]{1,0:T(8,128)(2,1)S(1)}) fusion(f32[512,1024]{1,0:T(8,128)} %param.10), kind=kLoop, calls=%fused_computation.4 | loop fusion | flops 2097152 | bytes 4194304 | tf_op jit(solution)/shard_map/convert_element_type | solution.py:229
  9.5 0.0 copy-done.3
  9.5 0.0 copy-start
  9.5 0.0 copy-start.1
  9.5 0.0 copy-start.2
  9.5 1.7 %fusion.1 = (bf16[1024,512]{1,0:T(8,128)(2,1)}, bf16[1024,512]{1,0:T(8,128)(2,1)}) fusion(f32[1024,512]{1,0:T(8,128)S(1)} %copy-done.3), kind=kLoop, calls=%fused_computation.5 | loop fusion | flops 2097152 | bytes 4194304 | tf_op jit(solution)/shard_map/convert_element_type | solution.py:229
  11.2 6.7 %all-to-all-done = f32[32,8,256]{2,1,0:T(8,128)S(1)} async-done(((f32[32,8,256]{2,1,0:T(8,128)}), f32[32,8,256]{2,1,0:T(8,128)S(1)}, u32[]{:S(2)}, u32[]{:S(2)}) %all-to-all-start) | async-done | bytes 262176 | tf_op jit(solution)/shard_map/all_to_all | solution.py:216
  18.0 0.0 copy-done
  18.0 0.0 copy-done.1
  18.0 0.0 copy-done.2
  18.0 10.6 %all_layers.1 = f32[256,256]{1,0:T(8,128)S(1)} custom-call(f32[256,256]{1,0:T(8,128)S(1)} %bitcast.4, f32[8,512]{1,0:T(8,128)S(1)} %copy-done.1, f32[8,1024]{1,0:T(8,128)S(1)} %copy-done, f32[8,512]{1,0:T(8,128)S(1)} %copy-done.2, bf16[512,1024]{1,0:T(8,128)(2,1)S(1)} %get-tuple-element.8.in_high_ref, bf16[512,1024]{1,0:T(8,128)(2,1)S(1)} %get-tuple-element.7.in_low_ref, ...), custom_call_target="tpu_custom_call" | custom-call | tf_op jit(solution)/shard_map/all_layers/pallas_call | solution.py:200
  28.6 12.8 %all_to_all.23 = f32[32,8,256]{2,1,0:T(8,128)S(1)} all-to-all(f32[32,8,256]{2,1,0:T(8,128)S(1)} %bitcast.5), channel_id=1, replica_groups=mesh['seqhi'=4,'seqlo'=8] {'seqhi','seqlo'}, dimensions={0} | all-to-all | bytes 524288 | tf_op jit(solution)/shard_map/all_to_all | solution.py:216
  41.4 0.7 %copy.8 = f32[256,256]{1,0:T(8,128)} copy(f32[256,256]{1,0:T(8,128)S(1)} %bitcast.6) | data formatting | bytes 524288
Async XLA Ops:
  0.0 18.0 %all-to-all-start = ((f32[32,8,256]{2,1,0:T(8,128)}), f32[32,8,256]{2,1,0:T(8,128)S(1)}, u32[]{:S(2)}, u32[]{:S(2)}) async-start(f32[32,8,256]{2,1,0:T(8,128)} %bitcast.7), calls=%async_computation | async-start | bytes 524288 | tf_op jit(solution)/shard_map/all_to_all | solution.py:216
  7.3 2.2 %copy-start.3 = (f32[1024,512]{1,0:T(8,128)S(1)}, f32[1024,512]{1,0:T(8,128)}, u32[]{:S(2)}) copy-start(f32[1024,512]{1,0:T(8,128)} %param.11) | copy-start | bytes 6291460
  9.5 8.4 %copy-start = (f32[8,1024]{1,0:T(8,128)S(1)}, f32[8,1024]{1,0:T(8,128)}, u32[]{:S(2)}) copy-start(f32[8,1024]{1,0:T(8,128)} %bias_ref.1) | copy-start | bytes 98308
  9.5 8.4 %copy-start.1 = (f32[8,512]{1,0:T(8,128)S(1)}, f32[8,512]{1,0:T(8,128)}, u32[]{:S(2)}) copy-start(f32[8,512]{1,0:T(8,128)} %gain_ref.1) | copy-start | bytes 49156
  9.5 8.4 %copy-start.2 = (f32[8,512]{1,0:T(8,128)S(1)}, f32[8,512]{1,0:T(8,128)}, u32[]{:S(2)}) copy-start(f32[8,512]{1,0:T(8,128)} %gate_ref.1) | copy-start | bytes 49156

commit v10 on v7

--- a/solution.py
+++ b/solution.py
@@ -102,7 +102,7 @@
 def run_layers(states, first, distances, params, name):
     rows, width = states.shape
     hidden = params[1].shape[1]
-    kernel = functools.partial(layers_kernel, first, distances, min(hidden, 256))
+    kernel = functools.partial(layers_kernel, first, distances, min(hidden, 512))
     vmem = pl.BlockSpec(memory_space=pltpu.VMEM)
     return pl.pallas_call(
         kernel,

time: 41.8 us -> 41.8 us (level)
  no operation moved by 1% of the time
where the time goes in v10:
time: 41.8 us; the launch traced here: 41.5 us
  blocking collectives  12.8 us (31%)
  Pallas kernels  10.1 us (24%)
  starting transfers between devices  7.3 us (17%)
  waiting for transfers between devices  6.73 us (16%)
  other arithmetic  3.85 us (9%)
  local copies, waits for them, and re-layouts  0.76 us (2%)
    all_to_all x1, blocking collectives, all_to_all(): return lax.all_to_all(x, axes, split_axis=0, concat_axis=0, tiled=True)  12.8 us
    pallas_call x1, Pallas kernels, run_layers(): pl.pallas_call(kernel, out_shape=jax.ShapeDtypeStruct((rows, width), jnp....  10.1 us
    all_to_all x1, starting transfers between devices, all_to_all(): return lax.all_to_all(x, axes, split_axis=0, concat_axis=0, tiled=True)  7.3 us
    all_to_all x1, waiting for transfers between devices, all_to_all(): return lax.all_to_all(x, axes, split_axis=0, concat_axis=0, tiled=True)  6.73 us
    convert_element_type x2, other arithmetic, parts(): return (high.astype(jnp.bfloat16), (w - high).astype(jnp.bfloat16))  3.85 us
  transfers between devices with their start and end apart: 1, of which 1 were waited for; matrix products, arithmetic and copies ran while one was open for 9% of the time, Pallas kernels for 0%

profile of v10, /device:TPU:0, one launch (start us, length us, event | category | flops | bytes accessed | tf_op | source)
XLA Modules:
  0.0 41.5 jit_solution(17995443418950986509)
XLA Ops:
  0.0 7.3 %all-to-all-start = ((f32[32,8,256]{2,1,0:T(8,128)}), f32[32,8,256]{2,1,0:T(8,128)S(1)}, u32[]{:S(2)}, u32[]{:S(2)}) async-start(f32[32,8,256]{2,1,0:T(8,128)} %bitcast.7), calls=%async_computation | async-start | bytes 524288 | tf_op jit(solution)/shard_map/all_to_all | solution.py:123
  7.3 0.0 copy-start.3
  7.3 2.2 %fusion = (bf16[512,1024]{1,0:T(8,128)(2,1)S(1)}, bf16[512,1024]{1,0:T(8,128)(2,1)S(1)}) fusion(f32[512,1024]{1,0:T(8,128)} %param.10), kind=kLoop, calls=%fused_computation.4 | loop fusion | flops 2097152 | bytes 4194304 | tf_op jit(solution)/shard_map/convert_element_type | solution.py:136
  9.5 0.0 copy-done.3
  9.5 0.0 copy-start
  9.5 0.0 copy-start.1
  9.5 0.0 copy-start.2
  9.5 1.7 %fusion.1 = (bf16[1024,512]{1,0:T(8,128)(2,1)}, bf16[1024,512]{1,0:T(8,128)(2,1)}) fusion(f32[1024,512]{1,0:T(8,128)S(1)} %copy-done.3), kind=kLoop, calls=%fused_computation.5 | loop fusion | flops 2097152 | bytes 4194304 | tf_op jit(solution)/shard_map/convert_element_type | solution.py:136
  11.2 6.7 %all-to-all-done = f32[32,8,256]{2,1,0:T(8,128)S(1)} async-done(((f32[32,8,256]{2,1,0:T(8,128)}), f32[32,8,256]{2,1,0:T(8,128)S(1)}, u32[]{:S(2)}, u32[]{:S(2)}) %all-to-all-start) | async-done | bytes 262176 | tf_op jit(solution)/shard_map/all_to_all | solution.py:123
  18.0 0.0 copy-done
  18.0 0.0 copy-done.1
  18.0 0.0 copy-done.2
  18.0 10.1 %all_layers.1 = f32[256,256]{1,0:T(8,128)S(1)} custom-call(f32[256,256]{1,0:T(8,128)S(1)} %bitcast.4, f32[8,512]{1,0:T(8,128)S(1)} %copy-done.1, f32[8,1024]{1,0:T(8,128)S(1)} %copy-done, f32[8,512]{1,0:T(8,128)S(1)} %copy-done.2, bf16[512,1024]{1,0:T(8,128)(2,1)S(1)} %get-tuple-element.8.in_high_ref, bf16[512,1024]{1,0:T(8,128)(2,1)S(1)} %get-tuple-element.7.in_low_ref, ...), custom_call_target="tpu_custom_call" | custom-call | tf_op jit(solution)/shard_map/all_layers/pallas_call | solution.py:107
  28.0 12.8 %all_to_all.23 = f32[32,8,256]{2,1,0:T(8,128)S(1)} all-to-all(f32[32,8,256]{2,1,0:T(8,128)S(1)} %bitcast.5), channel_id=1, replica_groups=mesh['seqhi'=4,'seqlo'=8] {'seqhi','seqlo'}, dimensions={0} | all-to-all | bytes 524288 | tf_op jit(solution)/shard_map/all_to_all | solution.py:123
  40.8 0.7 %copy.8 = f32[256,256]{1,0:T(8,128)} copy(f32[256,256]{1,0:T(8,128)S(1)} %bitcast.6) | data formatting | bytes 524288
Async XLA Ops:
  0.0 18.0 %all-to-all-start = ((f32[32,8,256]{2,1,0:T(8,128)}), f32[32,8,256]{2,1,0:T(8,128)S(1)}, u32[]{:S(2)}, u32[]{:S(2)}) async-start(f32[32,8,256]{2,1,0:T(8,128)} %bitcast.7), calls=%async_computation | async-start | bytes 524288 | tf_op jit(solution)/shard_map/all_to_all | solution.py:123
  7.3 2.2 %copy-start.3 = (f32[1024,512]{1,0:T(8,128)S(1)}, f32[1024,512]{1,0:T(8,128)}, u32[]{:S(2)}) copy-start(f32[1024,512]{1,0:T(8,128)} %param.11) | copy-start | bytes 6291460
  9.5 8.4 %copy-start = (f32[8,1024]{1,0:T(8,128)S(1)}, f32[8,1024]{1,0:T(8,128)}, u32[]{:S(2)}) copy-start(f32[8,1024]{1,0:T(8,128)} %bias_ref.1) | copy-start | bytes 98308
  9.5 8.4 %copy-start.1 = (f32[8,512]{1,0:T(8,128)S(1)}, f32[8,512]{1,0:T(8,128)}, u32[]{:S(2)}) copy-start(f32[8,512]{1,0:T(8,128)} %gain_ref.1) | copy-start | bytes 49156
  9.5 8.4 %copy-start.2 = (f32[8,512]{1,0:T(8,128)S(1)}, f32[8,512]{1,0:T(8,128)}, u32[]{:S(2)}) copy-start(f32[8,512]{1,0:T(8,128)} %gate_ref.1) | copy-start | bytes 49156

commit v11 on v10

--- a/solution.py
+++ b/solution.py
@@ -28,10 +28,6 @@
     return both[:rows] + (both[rows:] + dot(x_high, w_low))
 
 
-def dot_split(x, w_high, w_low):
-    return dot_parts(*split_high_low(x), w_high, w_low)
-
-
 def gelu(x):
     half = 0.5 * x
     return half + half * jnp.tanh(x * (GELU_SCALE + (GELU_SCALE * GELU_CUBE) * (x * x)))
@@ -40,7 +36,8 @@
 def switch_unit(pair, gain, bias, gate, w_in, w_out, hidden_block, out_ready):
     center = pair - jnp.mean(pair, axis=-1, keepdims=True)
     spread = jnp.mean(center * center, axis=-1, keepdims=True)
-    normed = center * lax.rsqrt(spread + NORM_EPS) * gain
+    scale = lax.rsqrt(spread + NORM_EPS)
+    scaled = split_high_low(center * gain)
     out = gate * pair
     in_high, in_low = w_in
     out_high, out_low = w_out
@@ -49,7 +46,8 @@
 
     parts = []
     for cols in blocks:
-        entered = dot_split(normed, in_high[:, cols], in_low[:, cols]) + bias[:, cols]
+        product = dot_parts(*scaled, in_high[:, cols], in_low[:, cols])
+        entered = product * scale + bias[:, cols]
         parts.append(split_high_low(gelu(entered)))
     high = jnp.concatenate([part[0] for part in parts], axis=1)
     low = jnp.concatenate([part[1] for part in parts], axis=1)

time: 41.8 us -> 41.2 us (0.986)
  Pallas kernels: 10.1 us -> 9.53 us
    pallas_call x1, Pallas kernels: 10.1 us -> 9.53 us  [run_layers(): pl.pallas_call(kernel, out_shape=jax.ShapeDtypeStruct((rows, width), jnp....]
where the time goes in v11:
time: 41.2 us; the launch traced here: 41 us
  blocking collectives  12.8 us (31%)
  Pallas kernels  9.53 us (23%)
  starting transfers between devices  7.3 us (18%)
  waiting for transfers between devices  6.73 us (16%)
  other arithmetic  3.85 us (9%)
  local copies, waits for them, and re-layouts  0.76 us (2%)
    all_to_all x1, blocking collectives, all_to_all(): return lax.all_to_all(x, axes, split_axis=0, concat_axis=0, tiled=True)  12.8 us
    pallas_call x1, Pallas kernels, run_layers(): pl.pallas_call(kernel, out_shape=jax.ShapeDtypeStruct((rows, width), jnp....  9.53 us
    all_to_all x1, starting transfers between devices, all_to_all(): return lax.all_to_all(x, axes, split_axis=0, concat_axis=0, tiled=True)  7.3 us
    all_to_all x1, waiting for transfers between devices, all_to_all(): return lax.all_to_all(x, axes, split_axis=0, concat_axis=0, tiled=True)  6.73 us
    convert_element_type x2, other arithmetic, parts(): return (high.astype(jnp.bfloat16), (w - high).astype(jnp.bfloat16))  3.85 us
  transfers between devices with their start and end apart: 1, of which 1 were waited for; matrix products, arithmetic and copies ran while one was open for 9% of the time, Pallas kernels for 0%

profile of v11, /device:TPU:0, one launch (start us, length us, event | category | flops | bytes accessed | tf_op | source)
XLA Modules:
  0.0 41.0 jit_solution(14909840065600411090)
XLA Ops:
  0.0 7.3 %all-to-all-start = ((f32[32,8,256]{2,1,0:T(8,128)}), f32[32,8,256]{2,1,0:T(8,128)S(1)}, u32[]{:S(2)}, u32[]{:S(2)}) async-start(f32[32,8,256]{2,1,0:T(8,128)} %bitcast.7), calls=%async_computation | async-start | bytes 524288 | tf_op jit(solution)/shard_map/all_to_all | solution.py:121
  7.3 0.0 copy-start.3
  7.3 2.2 %fusion = (bf16[512,1024]{1,0:T(8,128)(2,1)S(1)}, bf16[512,1024]{1,0:T(8,128)(2,1)S(1)}) fusion(f32[512,1024]{1,0:T(8,128)} %param.10), kind=kLoop, calls=%fused_computation.4 | loop fusion | flops 2097152 | bytes 4194304 | tf_op jit(solution)/shard_map/convert_element_type | solution.py:134
  9.5 0.0 copy-done.3
  9.5 0.0 copy-start
  9.5 0.0 copy-start.1
  9.5 0.0 copy-start.2
  9.5 1.7 %fusion.1 = (bf16[1024,512]{1,0:T(8,128)(2,1)}, bf16[1024,512]{1,0:T(8,128)(2,1)}) fusion(f32[1024,512]{1,0:T(8,128)S(1)} %copy-done.3), kind=kLoop, calls=%fused_computation.5 | loop fusion | flops 2097152 | bytes 4194304 | tf_op jit(solution)/shard_map/convert_element_type | solution.py:134
  11.2 6.7 %all-to-all-done = f32[32,8,256]{2,1,0:T(8,128)S(1)} async-done(((f32[32,8,256]{2,1,0:T(8,128)}), f32[32,8,256]{2,1,0:T(8,128)S(1)}, u32[]{:S(2)}, u32[]{:S(2)}) %all-to-all-start) | async-done | bytes 262176 | tf_op jit(solution)/shard_map/all_to_all | solution.py:121
  18.0 0.0 copy-done
  18.0 0.0 copy-done.1
  18.0 0.0 copy-done.2
  18.0 9.5 %all_layers.1 = f32[256,256]{1,0:T(8,128)S(1)} custom-call(f32[256,256]{1,0:T(8,128)S(1)} %bitcast.4, f32[8,512]{1,0:T(8,128)S(1)} %copy-done.1, f32[8,1024]{1,0:T(8,128)S(1)} %copy-done, f32[8,512]{1,0:T(8,128)S(1)} %copy-done.2, bf16[512,1024]{1,0:T(8,128)(2,1)S(1)} %get-tuple-element.8.in_high_ref, bf16[512,1024]{1,0:T(8,128)(2,1)S(1)} %get-tuple-element.7.in_low_ref, ...), custom_call_target="tpu_custom_call" | custom-call | tf_op jit(solution)/shard_map/all_layers/pallas_call | solution.py:105
  27.5 12.8 %all_to_all.23 = f32[32,8,256]{2,1,0:T(8,128)S(1)} all-to-all(f32[32,8,256]{2,1,0:T(8,128)S(1)} %bitcast.5), channel_id=1, replica_groups=mesh['seqhi'=4,'seqlo'=8] {'seqhi','seqlo'}, dimensions={0} | all-to-all | bytes 524288 | tf_op jit(solution)/shard_map/all_to_all | solution.py:121
  40.3 0.7 %copy.8 = f32[256,256]{1,0:T(8,128)} copy(f32[256,256]{1,0:T(8,128)S(1)} %bitcast.6) | data formatting | bytes 524288
Async XLA Ops:
  0.0 18.0 %all-to-all-start = ((f32[32,8,256]{2,1,0:T(8,128)}), f32[32,8,256]{2,1,0:T(8,128)S(1)}, u32[]{:S(2)}, u32[]{:S(2)}) async-start(f32[32,8,256]{2,1,0:T(8,128)} %bitcast.7), calls=%async_computation | async-start | bytes 524288 | tf_op jit(solution)/shard_map/all_to_all | solution.py:121
  7.3 2.2 %copy-start.3 = (f32[1024,512]{1,0:T(8,128)S(1)}, f32[1024,512]{1,0:T(8,128)}, u32[]{:S(2)}) copy-start(f32[1024,512]{1,0:T(8,128)} %param.11) | copy-start | bytes 6291460
  9.5 8.4 %copy-start = (f32[8,1024]{1,0:T(8,128)S(1)}, f32[8,1024]{1,0:T(8,128)}, u32[]{:S(2)}) copy-start(f32[8,1024]{1,0:T(8,128)} %bias_ref.1) | copy-start | bytes 98308
  9.5 8.4 %copy-start.1 = (f32[8,512]{1,0:T(8,128)S(1)}, f32[8,512]{1,0:T(8,128)}, u32[]{:S(2)}) copy-start(f32[8,512]{1,0:T(8,128)} %gain_ref.1) | copy-start | bytes 49156
  9.5 8.4 %copy-start.2 = (f32[8,512]{1,0:T(8,128)S(1)}, f32[8,512]{1,0:T(8,128)}, u32[]{:S(2)}) copy-start(f32[8,512]{1,0:T(8,128)} %gate_ref.1) | copy-start | bytes 49156

commit v12 on v8

--- a/solution.py
+++ b/solution.py
@@ -108,23 +108,36 @@
         )
         center = pair - jnp.mean(pair, axis=-1, keepdims=True)
         spread = jnp.mean(center * center, axis=-1, keepdims=True)
-        normed = center * lax.rsqrt(spread + NORM_EPS) * gain_ref[k : k + 1, :]
-        high, low = split_high_low(normed)
+        scale = lax.rsqrt(spread + NORM_EPS)
+        residual = jax.nn.sigmoid(gate_ref[k : k + 1, :]) * pair
+        high, low = split_high_low(center * gain_ref[k : k + 1, :])
+        hidden = []
+
+        def activate():
+            row = len(hidden)
+            if row < hidden_tiles:
+                product = pltpu.matmul_pop(hidden_accs[row])
+                entered = product * scale + bias_ref[k : k + 1, span(row)]
+                hidden.append(split_high_low(gelu(entered)))
+
         for start in range(0, hidden_tiles, units_count):
             for row in range(in_tiles):
                 x_high, x_low = high[:, span(row)], low[:, span(row)]
                 for operands in ((x_high, x_low), (x_high,)):
                     for unit in range(units_count):
                         units.multiply(unit, hidden_accs[start + unit], operands)
+                if start > 0 and start + units_count >= hidden_tiles and row == 0:
+                    activate()
         for row in range(hidden_tiles):
-            entered = pltpu.matmul_pop(hidden_accs[row]) + bias_ref[k : k + 1, span(row)]
-            h_high, h_low = split_high_low(gelu(entered))
+            while len(hidden) < min(row + 2, hidden_tiles):
+                activate()
+            h_high, h_low = hidden[row]
             for start in range(0, out_tiles, units_count):
                 for operands in ((h_high, h_low), (h_high,)):
                     for unit in range(units_count):
                         units.multiply(unit, out_accs[start + unit], operands)
         mixed = jnp.concatenate([pltpu.matmul_pop(acc) for acc in out_accs], axis=1)
-        out = jax.nn.sigmoid(gate_ref[k : k + 1, :]) * pair + mixed
+        out = residual + mixed
         shape = (groups, 1, distance, width)
         states = jnp.concatenate(
             [out[:, :width].reshape(shape), out[:, width:].reshape(shape)], axis=1

time: 42 us -> 41.5 us (0.988)
  Pallas kernels: 10.3 us -> 9.81 us
    pallas_call x1, Pallas kernels: 10.3 us -> 9.81 us  [run_layers(): pl.pallas_call(kernel, out_shape=jax.ShapeDtypeStruct((rows, width), jnp....]
where the time goes in v12:
time: 41.5 us; the launch traced here: 41.3 us
  blocking collectives  12.8 us (31%)
  Pallas kernels  9.81 us (24%)
  starting transfers between devices  7.3 us (18%)
  waiting for transfers between devices  6.73 us (16%)
  other arithmetic  3.85 us (9%)
  local copies, waits for them, and re-layouts  0.76 us (2%)
    all_to_all x1, blocking collectives, all_to_all(): return lax.all_to_all(x, axes, split_axis=0, concat_axis=0, tiled=True)  12.8 us
    pallas_call x1, Pallas kernels, run_layers(): pl.pallas_call(kernel, out_shape=jax.ShapeDtypeStruct((rows, width), jnp....  9.81 us
    all_to_all x1, starting transfers between devices, all_to_all(): return lax.all_to_all(x, axes, split_axis=0, concat_axis=0, tiled=True)  7.3 us
    all_to_all x1, waiting for transfers between devices, all_to_all(): return lax.all_to_all(x, axes, split_axis=0, concat_axis=0, tiled=True)  6.73 us
    convert_element_type x2, other arithmetic, parts(): return (high.astype(jnp.bfloat16), (w - high).astype(jnp.bfloat16))  3.85 us
  transfers between devices with their start and end apart: 1, of which 1 were waited for; matrix products, arithmetic and copies ran while one was open for 9% of the time, Pallas kernels for 0%

profile of v12, /device:TPU:0, one launch (start us, length us, event | category | flops | bytes accessed | tf_op | source)
XLA Modules:
  0.0 41.3 jit_solution(15827814996637174458)
XLA Ops:
  0.0 7.3 %all-to-all-start = ((f32[32,8,256]{2,1,0:T(8,128)}), f32[32,8,256]{2,1,0:T(8,128)S(1)}, u32[]{:S(2)}, u32[]{:S(2)}) async-start(f32[32,8,256]{2,1,0:T(8,128)} %bitcast.7), calls=%async_computation | async-start | bytes 524288 | tf_op jit(solution)/shard_map/all_to_all | solution.py:176
  7.3 0.0 copy-start.3
  7.3 2.2 %fusion = (bf16[512,1024]{1,0:T(8,128)(2,1)S(1)}, bf16[512,1024]{1,0:T(8,128)(2,1)S(1)}) fusion(f32[512,1024]{1,0:T(8,128)} %param.10), kind=kLoop, calls=%fused_computation.4 | loop fusion | flops 2097152 | bytes 4194304 | tf_op jit(solution)/shard_map/convert_element_type | solution.py:189
  9.5 0.0 copy-done.3
  9.5 0.0 copy-start
  9.5 0.0 copy-start.1
  9.5 0.0 copy-start.2
  9.5 1.7 %fusion.1 = (bf16[1024,512]{1,0:T(8,128)(2,1)}, bf16[1024,512]{1,0:T(8,128)(2,1)}) fusion(f32[1024,512]{1,0:T(8,128)S(1)} %copy-done.3), kind=kLoop, calls=%fused_computation.5 | loop fusion | flops 2097152 | bytes 4194304 | tf_op jit(solution)/shard_map/convert_element_type | solution.py:189
  11.2 6.7 %all-to-all-done = f32[32,8,256]{2,1,0:T(8,128)S(1)} async-done(((f32[32,8,256]{2,1,0:T(8,128)}), f32[32,8,256]{2,1,0:T(8,128)S(1)}, u32[]{:S(2)}, u32[]{:S(2)}) %all-to-all-start) | async-done | bytes 262176 | tf_op jit(solution)/shard_map/all_to_all | solution.py:176
  18.0 0.0 copy-done
  18.0 0.0 copy-done.1
  18.0 0.0 copy-done.2
  18.0 9.8 %all_layers.1 = f32[256,256]{1,0:T(8,128)S(1)} custom-call(f32[256,256]{1,0:T(8,128)S(1)} %bitcast.4, f32[8,512]{1,0:T(8,128)S(1)} %copy-done.1, f32[8,1024]{1,0:T(8,128)S(1)} %copy-done, f32[8,512]{1,0:T(8,128)S(1)} %copy-done.2, bf16[512,1024]{1,0:T(8,128)(2,1)S(1)} %get-tuple-element.8.in_high_ref, bf16[512,1024]{1,0:T(8,128)(2,1)S(1)} %get-tuple-element.7.in_low_ref, ...), custom_call_target="tpu_custom_call" | custom-call | tf_op jit(solution)/shard_map/all_layers/pallas_call | solution.py:160
  27.8 12.8 %all_to_all.23 = f32[32,8,256]{2,1,0:T(8,128)S(1)} all-to-all(f32[32,8,256]{2,1,0:T(8,128)S(1)} %bitcast.5), channel_id=1, replica_groups=mesh['seqhi'=4,'seqlo'=8] {'seqhi','seqlo'}, dimensions={0} | all-to-all | bytes 524288 | tf_op jit(solution)/shard_map/all_to_all | solution.py:176
  40.6 0.7 %copy.8 = f32[256,256]{1,0:T(8,128)} copy(f32[256,256]{1,0:T(8,128)S(1)} %bitcast.6) | data formatting | bytes 524288
Async XLA Ops:
  0.0 18.0 %all-to-all-start = ((f32[32,8,256]{2,1,0:T(8,128)}), f32[32,8,256]{2,1,0:T(8,128)S(1)}, u32[]{:S(2)}, u32[]{:S(2)}) async-start(f32[32,8,256]{2,1,0:T(8,128)} %bitcast.7), calls=%async_computation | async-start | bytes 524288 | tf_op jit(solution)/shard_map/all_to_all | solution.py:176
  7.3 2.2 %copy-start.3 = (f32[1024,512]{1,0:T(8,128)S(1)}, f32[1024,512]{1,0:T(8,128)}, u32[]{:S(2)}) copy-start(f32[1024,512]{1,0:T(8,128)} %param.11) | copy-start | bytes 6291460
  9.5 8.4 %copy-start = (f32[8,1024]{1,0:T(8,128)S(1)}, f32[8,1024]{1,0:T(8,128)}, u32[]{:S(2)}) copy-start(f32[8,1024]{1,0:T(8,128)} %bias_ref.1) | copy-start | bytes 98308
  9.5 8.4 %copy-start.1 = (f32[8,512]{1,0:T(8,128)S(1)}, f32[8,512]{1,0:T(8,128)}, u32[]{:S(2)}) copy-start(f32[8,512]{1,0:T(8,128)} %gain_ref.1) | copy-start | bytes 49156
  9.5 8.4 %copy-start.2 = (f32[8,512]{1,0:T(8,128)S(1)}, f32[8,512]{1,0:T(8,128)}, u32[]{:S(2)}) copy-start(f32[8,512]{1,0:T(8,128)} %gate_ref.1) | copy-start | bytes 49156

commit v13 on v11

--- a/solution.py
+++ b/solution.py
@@ -33,7 +33,7 @@
     return half + half * jnp.tanh(x * (GELU_SCALE + (GELU_SCALE * GELU_CUBE) * (x * x)))
 
 
-def switch_unit(pair, gain, bias, gate, w_in, w_out, hidden_block, out_ready):
+def switch_unit(pair, gain, bias, gate, w_in, w_out, hidden_block, ready):
     center = pair - jnp.mean(pair, axis=-1, keepdims=True)
     spread = jnp.mean(center * center, axis=-1, keepdims=True)
     scale = lax.rsqrt(spread + NORM_EPS)
@@ -44,15 +44,14 @@
     hidden_count = in_high.shape[1]
     blocks = [slice(c, c + hidden_block) for c in range(0, hidden_count, hidden_block)]
 
-    parts = []
     for cols in blocks:
         product = dot_parts(*scaled, in_high[:, cols], in_low[:, cols])
-        entered = product * scale + bias[:, cols]
-        parts.append(split_high_low(gelu(entered)))
-    high = jnp.concatenate([part[0] for part in parts], axis=1)
-    low = jnp.concatenate([part[1] for part in parts], axis=1)
-    out_ready()
-    return out + dot_parts(high, low, out_high[...], out_low[...])
+        h_high, h_low = split_high_low(gelu(product * scale + bias[:, cols]))
+        ready(out_high)
+        both = dot(jnp.concatenate([h_high, h_low], axis=0), out_high[cols, :])
+        ready(out_low)
+        out = out + (both[: h_high.shape[0]] + (both[h_high.shape[0] :] + dot(h_high, out_low[cols, :])))
+    return out
 
 
 def layers_kernel(
@@ -60,16 +59,19 @@
     x_ref, gain_ref, bias_ref, gate_ref, in_high_ref, in_low_ref, out_high_any, out_low_any,
     y_ref, out_high_ref, out_low_ref, copied,
 ):
-    copies = [
-        pltpu.make_async_copy(out_high_any, out_high_ref, copied.at[0]),
-        pltpu.make_async_copy(out_low_any, out_low_ref, copied.at[1]),
-    ]
-    for copy in copies:
+    pending = []
+    for number, (source, target) in enumerate(
+        [(out_high_any, out_high_ref), (out_low_any, out_low_ref)]
+    ):
+        copy = pltpu.make_async_copy(source, target, copied.at[number])
         copy.start()
+        pending.append((target, copy))
 
-    def wait_copies():
-        for copy in copies:
-            copy.wait()
+    def ready(ref):
+        for target, copy in list(pending):
+            if target is ref:
+                copy.wait()
+                pending.remove((target, copy))
 
     rows, width = x_ref.shape
     states = x_ref[...]
@@ -88,7 +90,7 @@
             (in_high_ref, in_low_ref),
             (out_high_ref, out_low_ref),
             hidden_block,
-            wait_copies if step == 0 else lambda: None,
+            ready,
         )
         shape = (groups, 1, distance, width)
         states = jnp.concatenate(

time: 41.2 us -> 43.7 us (1.061)
  Pallas kernels: 9.53 us -> 11.9 us
    pallas_call x1, Pallas kernels: 9.53 us -> 11.9 us  [run_layers(): pl.pallas_call(kernel, out_shape=jax.ShapeDtypeStruct((rows, width), jnp....]
where the time goes in v13:
time: 43.7 us; the launch traced here: 43.5 us
  blocking collectives  12.8 us (29%)
  Pallas kernels  11.9 us (27%)
  starting transfers between devices  7.3 us (17%)
  waiting for transfers between devices  6.73 us (15%)
  other arithmetic  3.85 us (9%)
  local copies, waits for them, and re-layouts  0.76 us (2%)
    all_to_all x1, blocking collectives, all_to_all(): return lax.all_to_all(x, axes, split_axis=0, concat_axis=0, tiled=True)  12.8 us
    pallas_call x1, Pallas kernels, run_layers(): pl.pallas_call(kernel, out_shape=jax.ShapeDtypeStruct((rows, width), jnp....  11.9 us
    all_to_all x1, starting transfers between devices, all_to_all(): return lax.all_to_all(x, axes, split_axis=0, concat_axis=0, tiled=True)  7.3 us
    all_to_all x1, waiting for transfers between devices, all_to_all(): return lax.all_to_all(x, axes, split_axis=0, concat_axis=0, tiled=True)  6.73 us
    convert_element_type x2, other arithmetic, parts(): return (high.astype(jnp.bfloat16), (w - high).astype(jnp.bfloat16))  3.85 us
  transfers between devices with their start and end apart: 1, of which 1 were waited for; matrix products, arithmetic and copies ran while one was open for 9% of the time, Pallas kernels for 0%

profile of v13, /device:TPU:0, one launch (start us, length us, event | category | flops | bytes accessed | tf_op | source)
XLA Modules:
  0.0 43.5 jit_solution(5155551113306824292)
XLA Ops:
  0.0 7.3 %all-to-all-start = ((f32[32,8,256]{2,1,0:T(8,128)}), f32[32,8,256]{2,1,0:T(8,128)S(1)}, u32[]{:S(2)}, u32[]{:S(2)}) async-start(f32[32,8,256]{2,1,0:T(8,128)} %bitcast.7), calls=%async_computation | async-start | bytes 524288 | tf_op jit(solution)/shard_map/all_to_all | solution.py:123
  7.3 0.0 copy-start.3
  7.3 2.2 %fusion = (bf16[512,1024]{1,0:T(8,128)(2,1)S(1)}, bf16[512,1024]{1,0:T(8,128)(2,1)S(1)}) fusion(f32[512,1024]{1,0:T(8,128)} %param.10), kind=kLoop, calls=%fused_computation.4 | loop fusion | flops 2097152 | bytes 4194304 | tf_op jit(solution)/shard_map/convert_element_type | solution.py:136
  9.5 0.0 copy-done.3
  9.5 0.0 copy-start
  9.5 0.0 copy-start.1
  9.5 0.0 copy-start.2
  9.5 1.7 %fusion.1 = (bf16[1024,512]{1,0:T(8,128)(2,1)}, bf16[1024,512]{1,0:T(8,128)(2,1)}) fusion(f32[1024,512]{1,0:T(8,128)S(1)} %copy-done.3), kind=kLoop, calls=%fused_computation.5 | loop fusion | flops 2097152 | bytes 4194304 | tf_op jit(solution)/shard_map/convert_element_type | solution.py:136
  11.2 6.7 %all-to-all-done = f32[32,8,256]{2,1,0:T(8,128)S(1)} async-done(((f32[32,8,256]{2,1,0:T(8,128)}), f32[32,8,256]{2,1,0:T(8,128)S(1)}, u32[]{:S(2)}, u32[]{:S(2)}) %all-to-all-start) | async-done | bytes 262176 | tf_op jit(solution)/shard_map/all_to_all | solution.py:123
  18.0 0.0 copy-done
  18.0 0.0 copy-done.1
  18.0 0.0 copy-done.2
  18.0 11.9 %all_layers.1 = f32[256,256]{1,0:T(8,128)S(1)} custom-call(f32[256,256]{1,0:T(8,128)S(1)} %bitcast.4, f32[8,512]{1,0:T(8,128)S(1)} %copy-done.1, f32[8,1024]{1,0:T(8,128)S(1)} %copy-done, f32[8,512]{1,0:T(8,128)S(1)} %copy-done.2, bf16[512,1024]{1,0:T(8,128)(2,1)S(1)} %get-tuple-element.8.in_high_ref, bf16[512,1024]{1,0:T(8,128)(2,1)S(1)} %get-tuple-element.7.in_low_ref, ...), custom_call_target="tpu_custom_call" | custom-call | tf_op jit(solution)/shard_map/all_layers/pallas_call | solution.py:107
  29.9 12.8 %all_to_all.23 = f32[32,8,256]{2,1,0:T(8,128)S(1)} all-to-all(f32[32,8,256]{2,1,0:T(8,128)S(1)} %bitcast.5), channel_id=1, replica_groups=mesh['seqhi'=4,'seqlo'=8] {'seqhi','seqlo'}, dimensions={0} | all-to-all | bytes 524288 | tf_op jit(solution)/shard_map/all_to_all | solution.py:123
  42.7 0.7 %copy.8 = f32[256,256]{1,0:T(8,128)} copy(f32[256,256]{1,0:T(8,128)S(1)} %bitcast.6) | data formatting | bytes 524288
Async XLA Ops:
  0.0 18.0 %all-to-all-start = ((f32[32,8,256]{2,1,0:T(8,128)}), f32[32,8,256]{2,1,0:T(8,128)S(1)}, u32[]{:S(2)}, u32[]{:S(2)}) async-start(f32[32,8,256]{2,1,0:T(8,128)} %bitcast.7), calls=%async_computation | async-start | bytes 524288 | tf_op jit(solution)/shard_map/all_to_all | solution.py:123
  7.3 2.2 %copy-start.3 = (f32[1024,512]{1,0:T(8,128)S(1)}, f32[1024,512]{1,0:T(8,128)}, u32[]{:S(2)}) copy-start(f32[1024,512]{1,0:T(8,128)} %param.11) | copy-start | bytes 6291460
  9.5 8.4 %copy-start = (f32[8,1024]{1,0:T(8,128)S(1)}, f32[8,1024]{1,0:T(8,128)}, u32[]{:S(2)}) copy-start(f32[8,1024]{1,0:T(8,128)} %bias_ref.1) | copy-start | bytes 98308
  9.5 8.4 %copy-start.1 = (f32[8,512]{1,0:T(8,128)S(1)}, f32[8,512]{1,0:T(8,128)}, u32[]{:S(2)}) copy-start(f32[8,512]{1,0:T(8,128)} %gain_ref.1) | copy-start | bytes 49156
  9.5 8.4 %copy-start.2 = (f32[8,512]{1,0:T(8,128)S(1)}, f32[8,512]{1,0:T(8,128)}, u32[]{:S(2)}) copy-start(f32[8,512]{1,0:T(8,128)} %gate_ref.1) | copy-start | bytes 49156

commit v14 on v13

--- a/solution.py
+++ b/solution.py
@@ -22,10 +22,11 @@
     return jnp.dot(a, b, preferred_element_type=jnp.float32)
 
 
-def dot_parts(x_high, x_low, w_high, w_low):
+def dot_parts(x_high, x_low, w_high, w_low, base=None):
     rows = x_high.shape[0]
-    both = dot(jnp.concatenate([x_high, x_low], axis=0), w_high)
-    return both[:rows] + (both[rows:] + dot(x_high, w_low))
+    both = dot(jnp.concatenate([x_high, x_low], axis=0), w_high())
+    first = both[:rows] if base is None else base + both[:rows]
+    return (first + both[rows:]) + dot(x_high, w_low())
 
 
 def gelu(x):
@@ -33,25 +34,24 @@
     return half + half * jnp.tanh(x * (GELU_SCALE + (GELU_SCALE * GELU_CUBE) * (x * x)))
 
 
-def switch_unit(pair, gain, bias, gate, w_in, w_out, hidden_block, ready):
+def switch_unit(pair, gain, bias, gate, w_in, w_out, hidden_block, load):
     center = pair - jnp.mean(pair, axis=-1, keepdims=True)
     spread = jnp.mean(center * center, axis=-1, keepdims=True)
     scale = lax.rsqrt(spread + NORM_EPS)
     scaled = split_high_low(center * gain)
-    out = gate * pair
     in_high, in_low = w_in
     out_high, out_low = w_out
     hidden_count = in_high.shape[1]
     blocks = [slice(c, c + hidden_block) for c in range(0, hidden_count, hidden_block)]
 
+    parts = []
     for cols in blocks:
-        product = dot_parts(*scaled, in_high[:, cols], in_low[:, cols])
-        h_high, h_low = split_high_low(gelu(product * scale + bias[:, cols]))
-        ready(out_high)
-        both = dot(jnp.concatenate([h_high, h_low], axis=0), out_high[cols, :])
-        ready(out_low)
-        out = out + (both[: h_high.shape[0]] + (both[h_high.shape[0] :] + dot(h_high, out_low[cols, :])))
-    return out
+        product = dot_parts(*scaled, lambda: in_high[:, cols], lambda: in_low[:, cols])
+        entered = product * scale + bias[:, cols]
+        parts.append(split_high_low(gelu(entered)))
+    high = jnp.concatenate([part[0] for part in parts], axis=1)
+    low = jnp.concatenate([part[1] for part in parts], axis=1)
+    return dot_parts(high, low, lambda: load(out_high), lambda: load(out_low), gate * pair)
 
 
 def layers_kernel(
@@ -67,11 +67,12 @@
         copy.start()
         pending.append((target, copy))
 
-    def ready(ref):
+    def load(ref):
         for target, copy in list(pending):
             if target is ref:
                 copy.wait()
                 pending.remove((target, copy))
+        return ref[...]
 
     rows, width = x_ref.shape
     states = x_ref[...]
@@ -90,7 +91,7 @@
             (in_high_ref, in_low_ref),
             (out_high_ref, out_low_ref),
             hidden_block,
-            ready,
+            load,
         )
         shape = (groups, 1, distance, width)
         states = jnp.concatenate(

time: 43.7 us -> 41 us (0.938)
  Pallas kernels: 11.9 us -> 9.27 us
    pallas_call x1, Pallas kernels: 11.9 us -> 9.27 us  [run_layers(): pl.pallas_call(kernel, out_shape=jax.ShapeDtypeStruct((rows, width), jnp....]
where the time goes in v14:
time: 41 us; the launch traced here: 40.8 us
  blocking collectives  12.8 us (31%)
  Pallas kernels  9.27 us (23%)
  starting transfers between devices  7.3 us (18%)
  waiting for transfers between devices  6.73 us (16%)
  other arithmetic  3.85 us (9%)
  local copies, waits for them, and re-layouts  0.76 us (2%)
    all_to_all x1, blocking collectives, all_to_all(): return lax.all_to_all(x, axes, split_axis=0, concat_axis=0, tiled=True)  12.8 us
    pallas_call x1, Pallas kernels, run_layers(): pl.pallas_call(kernel, out_shape=jax.ShapeDtypeStruct((rows, width), jnp....  9.27 us
    all_to_all x1, starting transfers between devices, all_to_all(): return lax.all_to_all(x, axes, split_axis=0, concat_axis=0, tiled=True)  7.3 us
    all_to_all x1, waiting for transfers between devices, all_to_all(): return lax.all_to_all(x, axes, split_axis=0, concat_axis=0, tiled=True)  6.73 us
    convert_element_type x2, other arithmetic, parts(): return (high.astype(jnp.bfloat16), (w - high).astype(jnp.bfloat16))  3.85 us
  transfers between devices with their start and end apart: 1, of which 1 were waited for; matrix products, arithmetic and copies ran while one was open for 9% of the time, Pallas kernels for 0%

profile of v14, /device:TPU:0, one launch (start us, length us, event | category | flops | bytes accessed | tf_op | source)
XLA Modules:
  0.0 40.8 jit_solution(4731898457163344722)
XLA Ops:
  0.0 7.3 %all-to-all-start = ((f32[32,8,256]{2,1,0:T(8,128)}), f32[32,8,256]{2,1,0:T(8,128)S(1)}, u32[]{:S(2)}, u32[]{:S(2)}) async-start(f32[32,8,256]{2,1,0:T(8,128)} %bitcast.7), calls=%async_computation | async-start | bytes 524288 | tf_op jit(solution)/shard_map/all_to_all | solution.py:124
  7.3 0.0 copy-start.3
  7.3 2.2 %fusion = (bf16[512,1024]{1,0:T(8,128)(2,1)S(1)}, bf16[512,1024]{1,0:T(8,128)(2,1)S(1)}) fusion(f32[512,1024]{1,0:T(8,128)} %param.10), kind=kLoop, calls=%fused_computation.4 | loop fusion | flops 2097152 | bytes 4194304 | tf_op jit(solution)/shard_map/convert_element_type | solution.py:137
  9.5 0.0 copy-done.3
  9.5 0.0 copy-start
  9.5 0.0 copy-start.1
  9.5 0.0 copy-start.2
  9.5 1.7 %fusion.1 = (bf16[1024,512]{1,0:T(8,128)(2,1)}, bf16[1024,512]{1,0:T(8,128)(2,1)}) fusion(f32[1024,512]{1,0:T(8,128)S(1)} %copy-done.3), kind=kLoop, calls=%fused_computation.5 | loop fusion | flops 2097152 | bytes 4194304 | tf_op jit(solution)/shard_map/convert_element_type | solution.py:137
  11.2 6.7 %all-to-all-done = f32[32,8,256]{2,1,0:T(8,128)S(1)} async-done(((f32[32,8,256]{2,1,0:T(8,128)}), f32[32,8,256]{2,1,0:T(8,128)S(1)}, u32[]{:S(2)}, u32[]{:S(2)}) %all-to-all-start) | async-done | bytes 262176 | tf_op jit(solution)/shard_map/all_to_all | solution.py:124
  18.0 0.0 copy-done
  18.0 0.0 copy-done.1
  18.0 0.0 copy-done.2
  18.0 9.3 %all_layers.1 = f32[256,256]{1,0:T(8,128)S(1)} custom-call(f32[256,256]{1,0:T(8,128)S(1)} %bitcast.4, f32[8,512]{1,0:T(8,128)S(1)} %copy-done.1, f32[8,1024]{1,0:T(8,128)S(1)} %copy-done, f32[8,512]{1,0:T(8,128)S(1)} %copy-done.2, bf16[512,1024]{1,0:T(8,128)(2,1)S(1)} %get-tuple-element.8.in_high_ref, bf16[512,1024]{1,0:T(8,128)(2,1)S(1)} %get-tuple-element.7.in_low_ref, ...), custom_call_target="tpu_custom_call" | custom-call | tf_op jit(solution)/shard_map/all_layers/pallas_call | solution.py:108
  27.2 12.8 %all_to_all.23 = f32[32,8,256]{2,1,0:T(8,128)S(1)} all-to-all(f32[32,8,256]{2,1,0:T(8,128)S(1)} %bitcast.5), channel_id=1, replica_groups=mesh['seqhi'=4,'seqlo'=8] {'seqhi','seqlo'}, dimensions={0} | all-to-all | bytes 524288 | tf_op jit(solution)/shard_map/all_to_all | solution.py:124
  40.1 0.7 %copy.8 = f32[256,256]{1,0:T(8,128)} copy(f32[256,256]{1,0:T(8,128)S(1)} %bitcast.6) | data formatting | bytes 524288
Async XLA Ops:
  0.0 18.0 %all-to-all-start = ((f32[32,8,256]{2,1,0:T(8,128)}), f32[32,8,256]{2,1,0:T(8,128)S(1)}, u32[]{:S(2)}, u32[]{:S(2)}) async-start(f32[32,8,256]{2,1,0:T(8,128)} %bitcast.7), calls=%async_computation | async-start | bytes 524288 | tf_op jit(solution)/shard_map/all_to_all | solution.py:124
  7.3 2.2 %copy-start.3 = (f32[1024,512]{1,0:T(8,128)S(1)}, f32[1024,512]{1,0:T(8,128)}, u32[]{:S(2)}) copy-start(f32[1024,512]{1,0:T(8,128)} %param.11) | copy-start | bytes 6291460
  9.5 8.4 %copy-start = (f32[8,1024]{1,0:T(8,128)S(1)}, f32[8,1024]{1,0:T(8,128)}, u32[]{:S(2)}) copy-start(f32[8,1024]{1,0:T(8,128)} %bias_ref.1) | copy-start | bytes 98308
  9.5 8.4 %copy-start.1 = (f32[8,512]{1,0:T(8,128)S(1)}, f32[8,512]{1,0:T(8,128)}, u32[]{:S(2)}) copy-start(f32[8,512]{1,0:T(8,128)} %gain_ref.1) | copy-start | bytes 49156
  9.5 8.4 %copy-start.2 = (f32[8,512]{1,0:T(8,128)S(1)}, f32[8,512]{1,0:T(8,128)}, u32[]{:S(2)}) copy-start(f32[8,512]{1,0:T(8,128)} %gate_ref.1) | copy-start | bytes 49156

commit v15 on v14

--- a/solution.py
+++ b/solution.py
@@ -49,9 +49,10 @@
         product = dot_parts(*scaled, lambda: in_high[:, cols], lambda: in_low[:, cols])
         entered = product * scale + bias[:, cols]
         parts.append(split_high_low(gelu(entered)))
-    high = jnp.concatenate([part[0] for part in parts], axis=1)
-    low = jnp.concatenate([part[1] for part in parts], axis=1)
-    return dot_parts(high, low, lambda: load(out_high), lambda: load(out_low), gate * pair)
+    out = gate * pair
+    for cols, (high, low) in zip(blocks, parts):
+        out = dot_parts(high, low, lambda: load(out_high, cols), lambda: load(out_low, cols), out)
+    return out
 
 
 def layers_kernel(
@@ -67,12 +68,12 @@
         copy.start()
         pending.append((target, copy))
 
-    def load(ref):
+    def load(ref, depth):
         for target, copy in list(pending):
             if target is ref:
                 copy.wait()
                 pending.remove((target, copy))
-        return ref[...]
+        return ref[depth, :]
 
     rows, width = x_ref.shape
     states = x_ref[...]

time: 41 us -> 41 us (level)
  no operation moved by 1% of the time
where the time goes in v15:
time: 41 us; the launch traced here: 40.8 us
  blocking collectives  12.8 us (31%)
  Pallas kernels  9.29 us (23%)
  starting transfers between devices  7.3 us (18%)
  waiting for transfers between devices  6.73 us (16%)
  other arithmetic  3.85 us (9%)
  local copies, waits for them, and re-layouts  0.76 us (2%)
    all_to_all x1, blocking collectives, all_to_all(): return lax.all_to_all(x, axes, split_axis=0, concat_axis=0, tiled=True)  12.8 us
    pallas_call x1, Pallas kernels, run_layers(): pl.pallas_call(kernel, out_shape=jax.ShapeDtypeStruct((rows, width), jnp....  9.29 us
    all_to_all x1, starting transfers between devices, all_to_all(): return lax.all_to_all(x, axes, split_axis=0, concat_axis=0, tiled=True)  7.3 us
    all_to_all x1, waiting for transfers between devices, all_to_all(): return lax.all_to_all(x, axes, split_axis=0, concat_axis=0, tiled=True)  6.73 us
    convert_element_type x2, other arithmetic, parts(): return (high.astype(jnp.bfloat16), (w - high).astype(jnp.bfloat16))  3.85 us
  transfers between devices with their start and end apart: 1, of which 1 were waited for; matrix products, arithmetic and copies ran while one was open for 9% of the time, Pallas kernels for 0%

profile of v15, /device:TPU:0, one launch (start us, length us, event | category | flops | bytes accessed | tf_op | source)
XLA Modules:
  0.0 40.8 jit_solution(1304598769297454215)
XLA Ops:
  0.0 7.3 %all-to-all-start = ((f32[32,8,256]{2,1,0:T(8,128)}), f32[32,8,256]{2,1,0:T(8,128)S(1)}, u32[]{:S(2)}, u32[]{:S(2)}) async-start(f32[32,8,256]{2,1,0:T(8,128)} %bitcast.7), calls=%async_computation | async-start | bytes 524288 | tf_op jit(solution)/shard_map/all_to_all | solution.py:125
  7.3 0.0 copy-start.3
  7.3 2.2 %fusion = (bf16[512,1024]{1,0:T(8,128)(2,1)S(1)}, bf16[512,1024]{1,0:T(8,128)(2,1)S(1)}) fusion(f32[512,1024]{1,0:T(8,128)} %param.10), kind=kLoop, calls=%fused_computation.4 | loop fusion | flops 2097152 | bytes 4194304 | tf_op jit(solution)/shard_map/convert_element_type | solution.py:138
  9.5 0.0 copy-done.3
  9.5 0.0 copy-start
  9.5 0.0 copy-start.1
  9.5 0.0 copy-start.2
  9.5 1.7 %fusion.1 = (bf16[1024,512]{1,0:T(8,128)(2,1)}, bf16[1024,512]{1,0:T(8,128)(2,1)}) fusion(f32[1024,512]{1,0:T(8,128)S(1)} %copy-done.3), kind=kLoop, calls=%fused_computation.5 | loop fusion | flops 2097152 | bytes 4194304 | tf_op jit(solution)/shard_map/convert_element_type | solution.py:138
  11.2 6.7 %all-to-all-done = f32[32,8,256]{2,1,0:T(8,128)S(1)} async-done(((f32[32,8,256]{2,1,0:T(8,128)}), f32[32,8,256]{2,1,0:T(8,128)S(1)}, u32[]{:S(2)}, u32[]{:S(2)}) %all-to-all-start) | async-done | bytes 262176 | tf_op jit(solution)/shard_map/all_to_all | solution.py:125
  18.0 0.0 copy-done
  18.0 0.0 copy-done.1
  18.0 0.0 copy-done.2
  18.0 9.3 %all_layers.1 = f32[256,256]{1,0:T(8,128)S(1)} custom-call(f32[256,256]{1,0:T(8,128)S(1)} %bitcast.4, f32[8,512]{1,0:T(8,128)S(1)} %copy-done.1, f32[8,1024]{1,0:T(8,128)S(1)} %copy-done, f32[8,512]{1,0:T(8,128)S(1)} %copy-done.2, bf16[512,1024]{1,0:T(8,128)(2,1)S(1)} %get-tuple-element.8.in_high_ref, bf16[512,1024]{1,0:T(8,128)(2,1)S(1)} %get-tuple-element.7.in_low_ref, ...), custom_call_target="tpu_custom_call" | custom-call | tf_op jit(solution)/shard_map/all_layers/pallas_call | solution.py:109
  27.3 12.8 %all_to_all.23 = f32[32,8,256]{2,1,0:T(8,128)S(1)} all-to-all(f32[32,8,256]{2,1,0:T(8,128)S(1)} %bitcast.5), channel_id=1, replica_groups=mesh['seqhi'=4,'seqlo'=8] {'seqhi','seqlo'}, dimensions={0} | all-to-all | bytes 524288 | tf_op jit(solution)/shard_map/all_to_all | solution.py:125
  40.1 0.7 %copy.8 = f32[256,256]{1,0:T(8,128)} copy(f32[256,256]{1,0:T(8,128)S(1)} %bitcast.6) | data formatting | bytes 524288
Async XLA Ops:
  0.0 18.0 %all-to-all-start = ((f32[32,8,256]{2,1,0:T(8,128)}), f32[32,8,256]{2,1,0:T(8,128)S(1)}, u32[]{:S(2)}, u32[]{:S(2)}) async-start(f32[32,8,256]{2,1,0:T(8,128)} %bitcast.7), calls=%async_computation | async-start | bytes 524288 | tf_op jit(solution)/shard_map/all_to_all | solution.py:125
  7.3 2.2 %copy-start.3 = (f32[1024,512]{1,0:T(8,128)S(1)}, f32[1024,512]{1,0:T(8,128)}, u32[]{:S(2)}) copy-start(f32[1024,512]{1,0:T(8,128)} %param.11) | copy-start | bytes 6291460
  9.5 8.4 %copy-start = (f32[8,1024]{1,0:T(8,128)S(1)}, f32[8,1024]{1,0:T(8,128)}, u32[]{:S(2)}) copy-start(f32[8,1024]{1,0:T(8,128)} %bias_ref.1) | copy-start | bytes 98308
  9.5 8.4 %copy-start.1 = (f32[8,512]{1,0:T(8,128)S(1)}, f32[8,512]{1,0:T(8,128)}, u32[]{:S(2)}) copy-start(f32[8,512]{1,0:T(8,128)} %gain_ref.1) | copy-start | bytes 49156
  9.5 8.4 %copy-start.2 = (f32[8,512]{1,0:T(8,128)S(1)}, f32[8,512]{1,0:T(8,128)}, u32[]{:S(2)}) copy-start(f32[8,512]{1,0:T(8,128)} %gate_ref.1) | copy-start | bytes 49156

commit v16 on v14

--- a/solution.py
+++ b/solution.py
@@ -22,36 +22,29 @@
     return jnp.dot(a, b, preferred_element_type=jnp.float32)
 
 
-def dot_parts(x_high, x_low, w_high, w_low, base=None):
-    rows = x_high.shape[0]
-    both = dot(jnp.concatenate([x_high, x_low], axis=0), w_high())
-    first = both[:rows] if base is None else base + both[:rows]
-    return (first + both[rows:]) + dot(x_high, w_low())
-
-
 def gelu(x):
     half = 0.5 * x
     return half + half * jnp.tanh(x * (GELU_SCALE + (GELU_SCALE * GELU_CUBE) * (x * x)))
 
 
-def switch_unit(pair, gain, bias, gate, w_in, w_out, hidden_block, load):
+def to_pairs(states, distance):
+    rows, width = states.shape
+    grouped = states.reshape(rows // (2 * distance), 2, distance, width)
+    sides = [grouped[:, side].reshape(rows // 2, width) for side in range(2)]
+    return jnp.concatenate(sides, axis=-1)
+
+
+def from_pairs(pair, distance):
+    half, double = pair.shape
+    width = double // 2
+    shape = (half // distance, 1, distance, width)
+    sides = [pair[:, :width].reshape(shape), pair[:, width:].reshape(shape)]
+    return jnp.concatenate(sides, axis=1).reshape(2 * half, width)
+
+
+def scaled_center(pair, gain):
     center = pair - jnp.mean(pair, axis=-1, keepdims=True)
-    spread = jnp.mean(center * center, axis=-1, keepdims=True)
-    scale = lax.rsqrt(spread + NORM_EPS)
-    scaled = split_high_low(center * gain)
-    in_high, in_low = w_in
-    out_high, out_low = w_out
-    hidden_count = in_high.shape[1]
-    blocks = [slice(c, c + hidden_block) for c in range(0, hidden_count, hidden_block)]
-
-    parts = []
-    for cols in blocks:
-        product = dot_parts(*scaled, lambda: in_high[:, cols], lambda: in_low[:, cols])
-        entered = product * scale + bias[:, cols]
-        parts.append(split_high_low(gelu(entered)))
-    high = jnp.concatenate([part[0] for part in parts], axis=1)
-    low = jnp.concatenate([part[1] for part in parts], axis=1)
-    return dot_parts(high, low, lambda: load(out_high), lambda: load(out_low), gate * pair)
+    return center, center * gain
 
 
 def layers_kernel(
@@ -74,30 +67,39 @@
                 pending.remove((target, copy))
         return ref[...]
 
-    rows, width = x_ref.shape
-    states = x_ref[...]
-    for step, distance in enumerate(distances):
-        k = first + step
-        groups = rows // (2 * distance)
-        grouped = states.reshape(groups, 2, distance, width)
-        pair = jnp.concatenate(
-            [grouped[:, 0].reshape(-1, width), grouped[:, 1].reshape(-1, width)], axis=-1
-        )
-        out = switch_unit(
-            pair,
-            gain_ref[k : k + 1, :],
-            bias_ref[k : k + 1, :],
-            jax.nn.sigmoid(gate_ref[k : k + 1, :]),
-            (in_high_ref, in_low_ref),
-            (out_high_ref, out_low_ref),
-            hidden_block,
-            load,
-        )
-        shape = (groups, 1, distance, width)
-        states = jnp.concatenate(
-            [out[:, :width].reshape(shape), out[:, width:].reshape(shape)], axis=1
-        ).reshape(rows, width)
-    y_ref[...] = states
+    half = x_ref.shape[0] // 2
+    hidden_count = in_high_ref.shape[1]
+    blocks = [slice(c, c + hidden_block) for c in range(0, hidden_count, hidden_block)]
+    layers = [(first + step, distance) for step, distance in enumerate(distances)]
+    states, late = x_ref[...], None
+    pair = to_pairs(states, distances[0])
+    x_high = scaled_center(pair, gain_ref[first : first + 1, :])[1].astype(jnp.bfloat16)
+    for step, (k, distance) in enumerate(layers):
+        bias = bias_ref[k : k + 1, :]
+        product_low = dot(x_high, in_low_ref[...])
+        if late is not None:
+            pair = to_pairs(from_pairs(near + late, distances[step - 1]), distance)
+        center, scaled = scaled_center(pair, gain_ref[k : k + 1, :])
+        scale = lax.rsqrt(jnp.mean(center * center, axis=-1, keepdims=True) + NORM_EPS)
+        x_low = (scaled - x_high.astype(jnp.float32)).astype(jnp.bfloat16)
+        stacked = jnp.concatenate([x_high, x_low], axis=0)
+        parts = []
+        for cols in blocks:
+            both = dot(stacked, in_high_ref[:, cols])
+            product = (both[:half] + both[half:]) + product_low[:, cols]
+            parts.append(split_high_low(gelu(product * scale + bias[:, cols])))
+        high = jnp.concatenate([part[0] for part in parts], axis=1)
+        low = jnp.concatenate([part[1] for part in parts], axis=1)
+        both = dot(jnp.concatenate([high, low], axis=0), load(out_high_ref))
+        gate = jax.nn.sigmoid(gate_ref[k : k + 1, :])
+        near = (gate * pair + both[:half]) + both[half:]
+        late = dot(high, load(out_low_ref))
+        if step + 1 < len(layers):
+            following, next_distance = layers[step + 1]
+            near_pair = to_pairs(from_pairs(near, distance), next_distance)
+            scaled = scaled_center(near_pair, gain_ref[following : following + 1, :])[1]
+            x_high = scaled.astype(jnp.bfloat16)
+    y_ref[...] = from_pairs(near + late, distances[-1])
 
 
 def run_layers(states, first, distances, params, name):

time: 41 us -> 40.1 us (0.978)
  Pallas kernels: 9.27 us -> 8.41 us
    pallas_call x1, Pallas kernels: 9.27 us -> 8.41 us  [run_layers(): pl.pallas_call(kernel, out_shape=jax.ShapeDtypeStruct((rows, width), jnp....]
  transfers between devices with their start and end apart: 1 -> 1, of which waited for: 1 -> 1; matrix products, arithmetic and copies ran while one was open for 9% -> 10% of each run, Pallas kernels for 0% -> 0%
where the time goes in v16:
time: 40.1 us; the launch traced here: 39.9 us
  blocking collectives  12.8 us (32%)
  Pallas kernels  8.41 us (21%)
  starting transfers between devices  7.3 us (18%)
  waiting for transfers between devices  6.73 us (17%)
  other arithmetic  3.85 us (10%)
  local copies, waits for them, and re-layouts  0.76 us (2%)
    all_to_all x1, blocking collectives, all_to_all(): return lax.all_to_all(x, axes, split_axis=0, concat_axis=0, tiled=True)  12.8 us
    pallas_call x1, Pallas kernels, run_layers(): pl.pallas_call(kernel, out_shape=jax.ShapeDtypeStruct((rows, width), jnp....  8.41 us
    all_to_all x1, starting transfers between devices, all_to_all(): return lax.all_to_all(x, axes, split_axis=0, concat_axis=0, tiled=True)  7.3 us
    all_to_all x1, waiting for transfers between devices, all_to_all(): return lax.all_to_all(x, axes, split_axis=0, concat_axis=0, tiled=True)  6.73 us
    convert_element_type x2, other arithmetic, parts(): return (high.astype(jnp.bfloat16), (w - high).astype(jnp.bfloat16))  3.85 us
  transfers between devices with their start and end apart: 1, of which 1 were waited for; matrix products, arithmetic and copies ran while one was open for 10% of the time, Pallas kernels for 0%

profile of v16, /device:TPU:0, one launch (start us, length us, event | category | flops | bytes accessed | tf_op | source)
XLA Modules:
  0.0 39.9 jit_solution(2310177999247495222)
XLA Ops:
  0.0 7.3 %all-to-all-start = ((f32[32,8,256]{2,1,0:T(8,128)}), f32[32,8,256]{2,1,0:T(8,128)S(1)}, u32[]{:S(2)}, u32[]{:S(2)}) async-start(f32[32,8,256]{2,1,0:T(8,128)} %bitcast.7), calls=%async_computation | async-start | bytes 524288 | tf_op jit(solution)/shard_map/all_to_all | solution.py:126
  7.3 0.0 copy-start.3
  7.3 2.2 %fusion = (bf16[512,1024]{1,0:T(8,128)(2,1)S(1)}, bf16[512,1024]{1,0:T(8,128)(2,1)S(1)}) fusion(f32[512,1024]{1,0:T(8,128)} %param.10), kind=kLoop, calls=%fused_computation.4 | loop fusion | flops 2097152 | bytes 4194304 | tf_op jit(solution)/shard_map/convert_element_type | solution.py:139
  9.5 0.0 copy-done.3
  9.5 0.0 copy-start
  9.5 0.0 copy-start.1
  9.5 0.0 copy-start.2
  9.5 1.7 %fusion.1 = (bf16[1024,512]{1,0:T(8,128)(2,1)}, bf16[1024,512]{1,0:T(8,128)(2,1)}) fusion(f32[1024,512]{1,0:T(8,128)S(1)} %copy-done.3), kind=kLoop, calls=%fused_computation.5 | loop fusion | flops 2097152 | bytes 4194304 | tf_op jit(solution)/shard_map/convert_element_type | solution.py:139
  11.2 6.7 %all-to-all-done = f32[32,8,256]{2,1,0:T(8,128)S(1)} async-done(((f32[32,8,256]{2,1,0:T(8,128)}), f32[32,8,256]{2,1,0:T(8,128)S(1)}, u32[]{:S(2)}, u32[]{:S(2)}) %all-to-all-start) | async-done | bytes 262176 | tf_op jit(solution)/shard_map/all_to_all | solution.py:126
  18.0 0.0 copy-done
  18.0 0.0 copy-done.1
  18.0 0.0 copy-done.2
  18.0 8.4 %all_layers.1 = f32[256,256]{1,0:T(8,128)S(1)} custom-call(f32[256,256]{1,0:T(8,128)S(1)} %bitcast.4, f32[8,512]{1,0:T(8,128)S(1)} %copy-done.1, f32[8,1024]{1,0:T(8,128)S(1)} %copy-done, f32[8,512]{1,0:T(8,128)S(1)} %copy-done.2, bf16[512,1024]{1,0:T(8,128)(2,1)S(1)} %get-tuple-element.8.in_high_ref, bf16[512,1024]{1,0:T(8,128)(2,1)S(1)} %get-tuple-element.7.in_low_ref, ...), custom_call_target="tpu_custom_call" | custom-call | tf_op jit(solution)/shard_map/all_layers/pallas_call | solution.py:110
  26.4 12.8 %all_to_all.23 = f32[32,8,256]{2,1,0:T(8,128)S(1)} all-to-all(f32[32,8,256]{2,1,0:T(8,128)S(1)} %bitcast.5), channel_id=1, replica_groups=mesh['seqhi'=4,'seqlo'=8] {'seqhi','seqlo'}, dimensions={0} | all-to-all | bytes 524288 | tf_op jit(solution)/shard_map/all_to_all | solution.py:126
  39.2 0.7 %copy.8 = f32[256,256]{1,0:T(8,128)} copy(f32[256,256]{1,0:T(8,128)S(1)} %bitcast.6) | data formatting | bytes 524288
Async XLA Ops:
  0.0 18.0 %all-to-all-start = ((f32[32,8,256]{2,1,0:T(8,128)}), f32[32,8,256]{2,1,0:T(8,128)S(1)}, u32[]{:S(2)}, u32[]{:S(2)}) async-start(f32[32,8,256]{2,1,0:T(8,128)} %bitcast.7), calls=%async_computation | async-start | bytes 524288 | tf_op jit(solution)/shard_map/all_to_all | solution.py:126
  7.3 2.2 %copy-start.3 = (f32[1024,512]{1,0:T(8,128)S(1)}, f32[1024,512]{1,0:T(8,128)}, u32[]{:S(2)}) copy-start(f32[1024,512]{1,0:T(8,128)} %param.11) | copy-start | bytes 6291460
  9.5 8.4 %copy-start = (f32[8,1024]{1,0:T(8,128)S(1)}, f32[8,1024]{1,0:T(8,128)}, u32[]{:S(2)}) copy-start(f32[8,1024]{1,0:T(8,128)} %bias_ref.1) | copy-start | bytes 98308
  9.5 8.4 %copy-start.1 = (f32[8,512]{1,0:T(8,128)S(1)}, f32[8,512]{1,0:T(8,128)}, u32[]{:S(2)}) copy-start(f32[8,512]{1,0:T(8,128)} %gain_ref.1) | copy-start | bytes 49156
  9.5 8.4 %copy-start.2 = (f32[8,512]{1,0:T(8,128)S(1)}, f32[8,512]{1,0:T(8,128)}, u32[]{:S(2)}) copy-start(f32[8,512]{1,0:T(8,128)} %gate_ref.1) | copy-start | bytes 49156

commit v17 on v16

--- a/solution.py
+++ b/solution.py
@@ -105,7 +105,7 @@
 def run_layers(states, first, distances, params, name):
     rows, width = states.shape
     hidden = params[1].shape[1]
-    kernel = functools.partial(layers_kernel, first, distances, min(hidden, 512))
+    kernel = functools.partial(layers_kernel, first, distances, min(hidden, 256))
     vmem = pl.BlockSpec(memory_space=pltpu.VMEM)
     return pl.pallas_call(
         kernel,

time: 40.1 us -> 40.1 us (level)
  no operation moved by 1% of the time
where the time goes in v17:
time: 40.1 us; the launch traced here: 39.9 us
  blocking collectives  12.8 us (32%)
  Pallas kernels  8.41 us (21%)
  starting transfers between devices  7.3 us (18%)
  waiting for transfers between devices  6.73 us (17%)
  other arithmetic  3.85 us (10%)
  local copies, waits for them, and re-layouts  0.76 us (2%)
    all_to_all x1, blocking collectives, all_to_all(): return lax.all_to_all(x, axes, split_axis=0, concat_axis=0, tiled=True)  12.8 us
    pallas_call x1, Pallas kernels, run_layers(): pl.pallas_call(kernel, out_shape=jax.ShapeDtypeStruct((rows, width), jnp....  8.41 us
    all_to_all x1, starting transfers between devices, all_to_all(): return lax.all_to_all(x, axes, split_axis=0, concat_axis=0, tiled=True)  7.3 us
    all_to_all x1, waiting for transfers between devices, all_to_all(): return lax.all_to_all(x, axes, split_axis=0, concat_axis=0, tiled=True)  6.73 us
    convert_element_type x2, other arithmetic, parts(): return (high.astype(jnp.bfloat16), (w - high).astype(jnp.bfloat16))  3.85 us
  transfers between devices with their start and end apart: 1, of which 1 were waited for; matrix products, arithmetic and copies ran while one was open for 10% of the time, Pallas kernels for 0%

profile of v17, /device:TPU:0, one launch (start us, length us, event | category | flops | bytes accessed | tf_op | source)
XLA Modules:
  0.0 39.9 jit_solution(2310177999247495222)
XLA Ops:
  0.0 7.3 %all-to-all-start = ((f32[32,8,256]{2,1,0:T(8,128)}), f32[32,8,256]{2,1,0:T(8,128)S(1)}, u32[]{:S(2)}, u32[]{:S(2)}) async-start(f32[32,8,256]{2,1,0:T(8,128)} %bitcast.7), calls=%async_computation | async-start | bytes 524288 | tf_op jit(solution)/shard_map/all_to_all | solution.py:126
  7.3 0.0 copy-start.3
  7.3 2.2 %fusion = (bf16[512,1024]{1,0:T(8,128)(2,1)S(1)}, bf16[512,1024]{1,0:T(8,128)(2,1)S(1)}) fusion(f32[512,1024]{1,0:T(8,128)} %param.10), kind=kLoop, calls=%fused_computation.4 | loop fusion | flops 2097152 | bytes 4194304 | tf_op jit(solution)/shard_map/convert_element_type | solution.py:139
  9.5 0.0 copy-done.3
  9.5 0.0 copy-start
  9.5 0.0 copy-start.1
  9.5 0.0 copy-start.2
  9.5 1.7 %fusion.1 = (bf16[1024,512]{1,0:T(8,128)(2,1)}, bf16[1024,512]{1,0:T(8,128)(2,1)}) fusion(f32[1024,512]{1,0:T(8,128)S(1)} %copy-done.3), kind=kLoop, calls=%fused_computation.5 | loop fusion | flops 2097152 | bytes 4194304 | tf_op jit(solution)/shard_map/convert_element_type | solution.py:139
  11.2 6.7 %all-to-all-done = f32[32,8,256]{2,1,0:T(8,128)S(1)} async-done(((f32[32,8,256]{2,1,0:T(8,128)}), f32[32,8,256]{2,1,0:T(8,128)S(1)}, u32[]{:S(2)}, u32[]{:S(2)}) %all-to-all-start) | async-done | bytes 262176 | tf_op jit(solution)/shard_map/all_to_all | solution.py:126
  18.0 0.0 copy-done
  18.0 0.0 copy-done.1
  18.0 0.0 copy-done.2
  18.0 8.4 %all_layers.1 = f32[256,256]{1,0:T(8,128)S(1)} custom-call(f32[256,256]{1,0:T(8,128)S(1)} %bitcast.4, f32[8,512]{1,0:T(8,128)S(1)} %copy-done.1, f32[8,1024]{1,0:T(8,128)S(1)} %copy-done, f32[8,512]{1,0:T(8,128)S(1)} %copy-done.2, bf16[512,1024]{1,0:T(8,128)(2,1)S(1)} %get-tuple-element.8.in_high_ref, bf16[512,1024]{1,0:T(8,128)(2,1)S(1)} %get-tuple-element.7.in_low_ref, ...), custom_call_target="tpu_custom_call" | custom-call | tf_op jit(solution)/shard_map/all_layers/pallas_call | solution.py:110
  26.4 12.8 %all_to_all.23 = f32[32,8,256]{2,1,0:T(8,128)S(1)} all-to-all(f32[32,8,256]{2,1,0:T(8,128)S(1)} %bitcast.5), channel_id=1, replica_groups=mesh['seqhi'=4,'seqlo'=8] {'seqhi','seqlo'}, dimensions={0} | all-to-all | bytes 524288 | tf_op jit(solution)/shard_map/all_to_all | solution.py:126
  39.2 0.7 %copy.8 = f32[256,256]{1,0:T(8,128)} copy(f32[256,256]{1,0:T(8,128)S(1)} %bitcast.6) | data formatting | bytes 524288
Async XLA Ops:
  0.0 18.0 %all-to-all-start = ((f32[32,8,256]{2,1,0:T(8,128)}), f32[32,8,256]{2,1,0:T(8,128)S(1)}, u32[]{:S(2)}, u32[]{:S(2)}) async-start(f32[32,8,256]{2,1,0:T(8,128)} %bitcast.7), calls=%async_computation | async-start | bytes 524288 | tf_op jit(solution)/shard_map/all_to_all | solution.py:126
  7.3 2.2 %copy-start.3 = (f32[1024,512]{1,0:T(8,128)S(1)}, f32[1024,512]{1,0:T(8,128)}, u32[]{:S(2)}) copy-start(f32[1024,512]{1,0:T(8,128)} %param.11) | copy-start | bytes 6291460
  9.5 8.4 %copy-start = (f32[8,1024]{1,0:T(8,128)S(1)}, f32[8,1024]{1,0:T(8,128)}, u32[]{:S(2)}) copy-start(f32[8,1024]{1,0:T(8,128)} %bias_ref.1) | copy-start | bytes 98308
  9.5 8.4 %copy-start.1 = (f32[8,512]{1,0:T(8,128)S(1)}, f32[8,512]{1,0:T(8,128)}, u32[]{:S(2)}) copy-start(f32[8,512]{1,0:T(8,128)} %gain_ref.1) | copy-start | bytes 49156
  9.5 8.4 %copy-start.2 = (f32[8,512]{1,0:T(8,128)S(1)}, f32[8,512]{1,0:T(8,128)}, u32[]{:S(2)}) copy-start(f32[8,512]{1,0:T(8,128)} %gate_ref.1) | copy-start | bytes 49156

commit v18 on v17

--- a/solution.py
+++ b/solution.py
@@ -76,7 +76,8 @@
     x_high = scaled_center(pair, gain_ref[first : first + 1, :])[1].astype(jnp.bfloat16)
     for step, (k, distance) in enumerate(layers):
         bias = bias_ref[k : k + 1, :]
-        product_low = dot(x_high, in_low_ref[...])
+        ahead = max(1, len(blocks) // 2)
+        low_products = [dot(x_high, in_low_ref[:, cols]) for cols in blocks[:ahead]]
         if late is not None:
             pair = to_pairs(from_pairs(near + late, distances[step - 1]), distance)
         center, scaled = scaled_center(pair, gain_ref[k : k + 1, :])
@@ -84,9 +85,11 @@
         x_low = (scaled - x_high.astype(jnp.float32)).astype(jnp.bfloat16)
         stacked = jnp.concatenate([x_high, x_low], axis=0)
         parts = []
-        for cols in blocks:
+        for number, cols in enumerate(blocks):
             both = dot(stacked, in_high_ref[:, cols])
-            product = (both[:half] + both[half:]) + product_low[:, cols]
+            if ahead + number < len(blocks):
+                low_products.append(dot(x_high, in_low_ref[:, blocks[ahead + number]]))
+            product = (both[:half] + both[half:]) + low_products[number]
             parts.append(split_high_low(gelu(product * scale + bias[:, cols])))
         high = jnp.concatenate([part[0] for part in parts], axis=1)
         low = jnp.concatenate([part[1] for part in parts], axis=1)

time: 40.1 us -> 40.3 us (level)
  no operation moved by 1% of the time
where the time goes in v18:
time: 40.3 us; the launch traced here: 40.1 us
  blocking collectives  12.8 us (32%)
  Pallas kernels  8.61 us (21%)
  starting transfers between devices  7.3 us (18%)
  waiting for transfers between devices  6.73 us (17%)
  other arithmetic  3.85 us (10%)
  local copies, waits for them, and re-layouts  0.76 us (2%)
    all_to_all x1, blocking collectives, all_to_all(): return lax.all_to_all(x, axes, split_axis=0, concat_axis=0, tiled=True)  12.8 us
    pallas_call x1, Pallas kernels, run_layers(): pl.pallas_call(kernel, out_shape=jax.ShapeDtypeStruct((rows, width), jnp....  8.61 us
    all_to_all x1, starting transfers between devices, all_to_all(): return lax.all_to_all(x, axes, split_axis=0, concat_axis=0, tiled=True)  7.3 us
    all_to_all x1, waiting for transfers between devices, all_to_all(): return lax.all_to_all(x, axes, split_axis=0, concat_axis=0, tiled=True)  6.73 us
    convert_element_type x2, other arithmetic, parts(): return (high.astype(jnp.bfloat16), (w - high).astype(jnp.bfloat16))  3.85 us
  transfers between devices with their start and end apart: 1, of which 1 were waited for; matrix products, arithmetic and copies ran while one was open for 10% of the time, Pallas kernels for 0%

profile of v18, /device:TPU:0, one launch (start us, length us, event | category | flops | bytes accessed | tf_op | source)
XLA Modules:
  0.0 40.1 jit_solution(16594916409097290669)
XLA Ops:
  0.0 7.3 %all-to-all-start = ((f32[32,8,256]{2,1,0:T(8,128)}), f32[32,8,256]{2,1,0:T(8,128)S(1)}, u32[]{:S(2)}, u32[]{:S(2)}) async-start(f32[32,8,256]{2,1,0:T(8,128)} %bitcast.7), calls=%async_computation | async-start | bytes 524288 | tf_op jit(solution)/shard_map/all_to_all | solution.py:129
  7.3 0.0 copy-start.3
  7.3 2.2 %fusion = (bf16[512,1024]{1,0:T(8,128)(2,1)S(1)}, bf16[512,1024]{1,0:T(8,128)(2,1)S(1)}) fusion(f32[512,1024]{1,0:T(8,128)} %param.10), kind=kLoop, calls=%fused_computation.4 | loop fusion | flops 2097152 | bytes 4194304 | tf_op jit(solution)/shard_map/convert_element_type | solution.py:142
  9.5 0.0 copy-done.3
  9.5 0.0 copy-start
  9.5 0.0 copy-start.1
  9.5 0.0 copy-start.2
  9.5 1.7 %fusion.1 = (bf16[1024,512]{1,0:T(8,128)(2,1)}, bf16[1024,512]{1,0:T(8,128)(2,1)}) fusion(f32[1024,512]{1,0:T(8,128)S(1)} %copy-done.3), kind=kLoop, calls=%fused_computation.5 | loop fusion | flops 2097152 | bytes 4194304 | tf_op jit(solution)/shard_map/convert_element_type | solution.py:142
  11.2 6.7 %all-to-all-done = f32[32,8,256]{2,1,0:T(8,128)S(1)} async-done(((f32[32,8,256]{2,1,0:T(8,128)}), f32[32,8,256]{2,1,0:T(8,128)S(1)}, u32[]{:S(2)}, u32[]{:S(2)}) %all-to-all-start) | async-done | bytes 262176 | tf_op jit(solution)/shard_map/all_to_all | solution.py:129
  18.0 0.0 copy-done
  18.0 0.0 copy-done.1
  18.0 0.0 copy-done.2
  18.0 8.6 %all_layers.1 = f32[256,256]{1,0:T(8,128)S(1)} custom-call(f32[256,256]{1,0:T(8,128)S(1)} %bitcast.4, f32[8,512]{1,0:T(8,128)S(1)} %copy-done.1, f32[8,1024]{1,0:T(8,128)S(1)} %copy-done, f32[8,512]{1,0:T(8,128)S(1)} %copy-done.2, bf16[512,1024]{1,0:T(8,128)(2,1)S(1)} %get-tuple-element.8.in_high_ref, bf16[512,1024]{1,0:T(8,128)(2,1)S(1)} %get-tuple-element.7.in_low_ref, ...), custom_call_target="tpu_custom_call" | custom-call | tf_op jit(solution)/shard_map/all_layers/pallas_call | solution.py:113
  26.6 12.8 %all_to_all.23 = f32[32,8,256]{2,1,0:T(8,128)S(1)} all-to-all(f32[32,8,256]{2,1,0:T(8,128)S(1)} %bitcast.5), channel_id=1, replica_groups=mesh['seqhi'=4,'seqlo'=8] {'seqhi','seqlo'}, dimensions={0} | all-to-all | bytes 524288 | tf_op jit(solution)/shard_map/all_to_all | solution.py:129
  39.4 0.7 %copy.8 = f32[256,256]{1,0:T(8,128)} copy(f32[256,256]{1,0:T(8,128)S(1)} %bitcast.6) | data formatting | bytes 524288
Async XLA Ops:
  0.0 18.0 %all-to-all-start = ((f32[32,8,256]{2,1,0:T(8,128)}), f32[32,8,256]{2,1,0:T(8,128)S(1)}, u32[]{:S(2)}, u32[]{:S(2)}) async-start(f32[32,8,256]{2,1,0:T(8,128)} %bitcast.7), calls=%async_computation | async-start | bytes 524288 | tf_op jit(solution)/shard_map/all_to_all | solution.py:129
  7.3 2.2 %copy-start.3 = (f32[1024,512]{1,0:T(8,128)S(1)}, f32[1024,512]{1,0:T(8,128)}, u32[]{:S(2)}) copy-start(f32[1024,512]{1,0:T(8,128)} %param.11) | copy-start | bytes 6291460
  9.5 8.4 %copy-start = (f32[8,1024]{1,0:T(8,128)S(1)}, f32[8,1024]{1,0:T(8,128)}, u32[]{:S(2)}) copy-start(f32[8,1024]{1,0:T(8,128)} %bias_ref.1) | copy-start | bytes 98308
  9.5 8.4 %copy-start.1 = (f32[8,512]{1,0:T(8,128)S(1)}, f32[8,512]{1,0:T(8,128)}, u32[]{:S(2)}) copy-start(f32[8,512]{1,0:T(8,128)} %gain_ref.1) | copy-start | bytes 49156
  9.5 8.4 %copy-start.2 = (f32[8,512]{1,0:T(8,128)S(1)}, f32[8,512]{1,0:T(8,128)}, u32[]{:S(2)}) copy-start(f32[8,512]{1,0:T(8,128)} %gate_ref.1) | copy-start | bytes 49156

commit v19 on v17

--- a/solution.py
+++ b/solution.py
@@ -105,7 +105,7 @@
 def run_layers(states, first, distances, params, name):
     rows, width = states.shape
     hidden = params[1].shape[1]
-    kernel = functools.partial(layers_kernel, first, distances, min(hidden, 256))
+    kernel = functools.partial(layers_kernel, first, distances, hidden)
     vmem = pl.BlockSpec(memory_space=pltpu.VMEM)
     return pl.pallas_call(
         kernel,

time: 40.1 us -> 40.1 us (level)
  no operation moved by 1% of the time
where the time goes in v19:
time: 40.1 us; the launch traced here: 39.9 us
  blocking collectives  12.8 us (32%)
  Pallas kernels  8.41 us (21%)
  starting transfers between devices  7.3 us (18%)
  waiting for transfers between devices  6.73 us (17%)
  other arithmetic  3.85 us (10%)
  local copies, waits for them, and re-layouts  0.76 us (2%)
    all_to_all x1, blocking collectives, all_to_all(): return lax.all_to_all(x, axes, split_axis=0, concat_axis=0, tiled=True)  12.8 us
    pallas_call x1, Pallas kernels, run_layers(): pl.pallas_call(kernel, out_shape=jax.ShapeDtypeStruct((rows, width), jnp....  8.41 us
    all_to_all x1, starting transfers between devices, all_to_all(): return lax.all_to_all(x, axes, split_axis=0, concat_axis=0, tiled=True)  7.3 us
    all_to_all x1, waiting for transfers between devices, all_to_all(): return lax.all_to_all(x, axes, split_axis=0, concat_axis=0, tiled=True)  6.73 us
    convert_element_type x2, other arithmetic, parts(): return (high.astype(jnp.bfloat16), (w - high).astype(jnp.bfloat16))  3.85 us
  transfers between devices with their start and end apart: 1, of which 1 were waited for; matrix products, arithmetic and copies ran while one was open for 10% of the time, Pallas kernels for 0%

profile of v19, /device:TPU:0, one launch (start us, length us, event | category | flops | bytes accessed | tf_op | source)
XLA Modules:
  0.0 39.9 jit_solution(2310177999247495222)
XLA Ops:
  0.0 7.3 %all-to-all-start = ((f32[32,8,256]{2,1,0:T(8,128)}), f32[32,8,256]{2,1,0:T(8,128)S(1)}, u32[]{:S(2)}, u32[]{:S(2)}) async-start(f32[32,8,256]{2,1,0:T(8,128)} %bitcast.7), calls=%async_computation | async-start | bytes 524288 | tf_op jit(solution)/shard_map/all_to_all | solution.py:126
  7.3 0.0 copy-start.3
  7.3 2.2 %fusion = (bf16[512,1024]{1,0:T(8,128)(2,1)S(1)}, bf16[512,1024]{1,0:T(8,128)(2,1)S(1)}) fusion(f32[512,1024]{1,0:T(8,128)} %param.10), kind=kLoop, calls=%fused_computation.4 | loop fusion | flops 2097152 | bytes 4194304 | tf_op jit(solution)/shard_map/convert_element_type | solution.py:139
  9.5 0.0 copy-done.3
  9.5 0.0 copy-start
  9.5 0.0 copy-start.1
  9.5 0.0 copy-start.2
  9.5 1.7 %fusion.1 = (bf16[1024,512]{1,0:T(8,128)(2,1)}, bf16[1024,512]{1,0:T(8,128)(2,1)}) fusion(f32[1024,512]{1,0:T(8,128)S(1)} %copy-done.3), kind=kLoop, calls=%fused_computation.5 | loop fusion | flops 2097152 | bytes 4194304 | tf_op jit(solution)/shard_map/convert_element_type | solution.py:139
  11.2 6.7 %all-to-all-done = f32[32,8,256]{2,1,0:T(8,128)S(1)} async-done(((f32[32,8,256]{2,1,0:T(8,128)}), f32[32,8,256]{2,1,0:T(8,128)S(1)}, u32[]{:S(2)}, u32[]{:S(2)}) %all-to-all-start) | async-done | bytes 262176 | tf_op jit(solution)/shard_map/all_to_all | solution.py:126
  18.0 0.0 copy-done
  18.0 0.0 copy-done.1
  18.0 0.0 copy-done.2
  18.0 8.4 %all_layers.1 = f32[256,256]{1,0:T(8,128)S(1)} custom-call(f32[256,256]{1,0:T(8,128)S(1)} %bitcast.4, f32[8,512]{1,0:T(8,128)S(1)} %copy-done.1, f32[8,1024]{1,0:T(8,128)S(1)} %copy-done, f32[8,512]{1,0:T(8,128)S(1)} %copy-done.2, bf16[512,1024]{1,0:T(8,128)(2,1)S(1)} %get-tuple-element.8.in_high_ref, bf16[512,1024]{1,0:T(8,128)(2,1)S(1)} %get-tuple-element.7.in_low_ref, ...), custom_call_target="tpu_custom_call" | custom-call | tf_op jit(solution)/shard_map/all_layers/pallas_call | solution.py:110
  26.4 12.8 %all_to_all.23 = f32[32,8,256]{2,1,0:T(8,128)S(1)} all-to-all(f32[32,8,256]{2,1,0:T(8,128)S(1)} %bitcast.5), channel_id=1, replica_groups=mesh['seqhi'=4,'seqlo'=8] {'seqhi','seqlo'}, dimensions={0} | all-to-all | bytes 524288 | tf_op jit(solution)/shard_map/all_to_all | solution.py:126
  39.2 0.7 %copy.8 = f32[256,256]{1,0:T(8,128)} copy(f32[256,256]{1,0:T(8,128)S(1)} %bitcast.6) | data formatting | bytes 524288
Async XLA Ops:
  0.0 18.0 %all-to-all-start = ((f32[32,8,256]{2,1,0:T(8,128)}), f32[32,8,256]{2,1,0:T(8,128)S(1)}, u32[]{:S(2)}, u32[]{:S(2)}) async-start(f32[32,8,256]{2,1,0:T(8,128)} %bitcast.7), calls=%async_computation | async-start | bytes 524288 | tf_op jit(solution)/shard_map/all_to_all | solution.py:126
  7.3 2.2 %copy-start.3 = (f32[1024,512]{1,0:T(8,128)S(1)}, f32[1024,512]{1,0:T(8,128)}, u32[]{:S(2)}) copy-start(f32[1024,512]{1,0:T(8,128)} %param.11) | copy-start | bytes 6291460
  9.5 8.4 %copy-start = (f32[8,1024]{1,0:T(8,128)S(1)}, f32[8,1024]{1,0:T(8,128)}, u32[]{:S(2)}) copy-start(f32[8,1024]{1,0:T(8,128)} %bias_ref.1) | copy-start | bytes 98308
  9.5 8.4 %copy-start.1 = (f32[8,512]{1,0:T(8,128)S(1)}, f32[8,512]{1,0:T(8,128)}, u32[]{:S(2)}) copy-start(f32[8,512]{1,0:T(8,128)} %gain_ref.1) | copy-start | bytes 49156
  9.5 8.4 %copy-start.2 = (f32[8,512]{1,0:T(8,128)S(1)}, f32[8,512]{1,0:T(8,128)}, u32[]{:S(2)}) copy-start(f32[8,512]{1,0:T(8,128)} %gate_ref.1) | copy-start | bytes 49156

commit v20 on v19

--- a/solution.py
+++ b/solution.py
@@ -48,7 +48,7 @@
 
 
 def layers_kernel(
-    first, distances, hidden_block,
+    first, distances, hidden_block, factor,
     x_ref, gain_ref, bias_ref, gate_ref, in_high_ref, in_low_ref, out_high_any, out_low_any,
     y_ref, out_high_ref, out_low_ref, copied,
 ):
@@ -99,13 +99,13 @@
             near_pair = to_pairs(from_pairs(near, distance), next_distance)
             scaled = scaled_center(near_pair, gain_ref[following : following + 1, :])[1]
             x_high = scaled.astype(jnp.bfloat16)
-    y_ref[...] = from_pairs(near + late, distances[-1])
+    y_ref[...] = factor * from_pairs(near + late, distances[-1])
 
 
-def run_layers(states, first, distances, params, name):
+def run_layers(states, first, distances, params, name, factor=1.0):
     rows, width = states.shape
     hidden = params[1].shape[1]
-    kernel = functools.partial(layers_kernel, first, distances, hidden)
+    kernel = functools.partial(layers_kernel, first, distances, min(hidden, 256), factor)
     vmem = pl.BlockSpec(memory_space=pltpu.VMEM)
     return pl.pallas_call(
         kernel,
@@ -144,8 +144,8 @@
         distances = [block * low_count * 2 ** (k % high_bits) for k in range(HI_LAYERS)]
         distances += [block * 2 ** (j % low_bits) for j in range(layer_total - HI_LAYERS)]
         states = all_to_all(features, ("seqhi", "seqlo"))
-        states = run_layers(states, 0, distances, params, "all_layers")
-        return all_to_all(states, ("seqhi", "seqlo"))
+        states = run_layers(states, 0, distances, params, "all_layers", 0.5)
+        return 2.0 * all_to_all(states, ("seqhi", "seqlo"))
     high_distances = [rows // high_count * 2 ** (k % high_bits) for k in range(HI_LAYERS)]
     low_distances = [rows // low_count * 2 ** (j % low_bits) for j in range(layer_total - HI_LAYERS)]
     states = all_to_all(features, "seqhi")

time: 40.1 us -> 40.2 us (level)
  other arithmetic: 3.85 us -> 4.57 us
  local copies, waits for them, and re-layouts: 0.76 us -> 0.05 us
    mul x0 -> x1, other arithmetic: none -> 0.72 us  [body(): return 2.0 * all_to_all(states, ('seqhi', 'seqlo'))]
    unnamed x9 -> x8, local copies, waits for them, and re-layouts: 0.76 us -> 0.05 us
where the time goes in v20:
time: 40.2 us; the launch traced here: 39.9 us
  blocking collectives  12.8 us (32%)
  Pallas kernels  8.41 us (21%)
  starting transfers between devices  7.3 us (18%)
  waiting for transfers between devices  6.73 us (17%)
  other arithmetic  4.57 us (11%)
    all_to_all x1, blocking collectives, all_to_all(): return lax.all_to_all(x, axes, split_axis=0, concat_axis=0, tiled=True)  12.8 us
    pallas_call x1, Pallas kernels, run_layers(): pl.pallas_call(kernel, out_shape=jax.ShapeDtypeStruct((rows, width), jnp....  8.41 us
    all_to_all x1, starting transfers between devices, all_to_all(): return lax.all_to_all(x, axes, split_axis=0, concat_axis=0, tiled=True)  7.3 us
    all_to_all x1, waiting for transfers between devices, all_to_all(): return lax.all_to_all(x, axes, split_axis=0, concat_axis=0, tiled=True)  6.73 us
    convert_element_type x2, other arithmetic, parts(): return (high.astype(jnp.bfloat16), (w - high).astype(jnp.bfloat16))  3.85 us
  transfers between devices with their start and end apart: 1, of which 1 were waited for; matrix products, arithmetic and copies ran while one was open for 10% of the time, Pallas kernels for 0%

profile of v20, /device:TPU:0, one launch (start us, length us, event | category | flops | bytes accessed | tf_op | source)
XLA Modules:
  0.0 39.9 jit_solution(10654123481969623374)
XLA Ops:
  0.0 7.3 %all-to-all-start = ((f32[32,8,256]{2,1,0:T(8,128)}), f32[32,8,256]{2,1,0:T(8,128)S(1)}, u32[]{:S(2)}, u32[]{:S(2)}) async-start(f32[32,8,256]{2,1,0:T(8,128)} %bitcast.7), calls=%async_computation | async-start | bytes 524288 | tf_op jit(solution)/shard_map/all_to_all | solution.py:126
  7.3 0.0 copy-start.3
  7.3 2.2 %fusion = (bf16[512,1024]{1,0:T(8,128)(2,1)S(1)}, bf16[512,1024]{1,0:T(8,128)(2,1)S(1)}) fusion(f32[512,1024]{1,0:T(8,128)} %param.10), kind=kLoop, calls=%fused_computation.4 | loop fusion | flops 2097152 | bytes 4194304 | tf_op jit(solution)/shard_map/convert_element_type | solution.py:139
  9.5 0.0 copy-done.3
  9.5 0.0 copy-start
  9.5 0.0 copy-start.1
  9.5 0.0 copy-start.2
  9.5 1.7 %fusion.1 = (bf16[1024,512]{1,0:T(8,128)(2,1)}, bf16[1024,512]{1,0:T(8,128)(2,1)}) fusion(f32[1024,512]{1,0:T(8,128)S(1)} %copy-done.3), kind=kLoop, calls=%fused_computation.5 | loop fusion | flops 2097152 | bytes 4194304 | tf_op jit(solution)/shard_map/convert_element_type | solution.py:139
  11.2 6.7 %all-to-all-done = f32[32,8,256]{2,1,0:T(8,128)S(1)} async-done(((f32[32,8,256]{2,1,0:T(8,128)}), f32[32,8,256]{2,1,0:T(8,128)S(1)}, u32[]{:S(2)}, u32[]{:S(2)}) %all-to-all-start) | async-done | bytes 262176 | tf_op jit(solution)/shard_map/all_to_all | solution.py:126
  18.0 0.0 copy-done
  18.0 0.0 copy-done.1
  18.0 0.0 copy-done.2
  18.0 8.4 %all_layers.1 = f32[256,256]{1,0:T(8,128)S(1)} custom-call(f32[256,256]{1,0:T(8,128)S(1)} %bitcast.5, f32[8,512]{1,0:T(8,128)S(1)} %copy-done.1, f32[8,1024]{1,0:T(8,128)S(1)} %copy-done, f32[8,512]{1,0:T(8,128)S(1)} %copy-done.2, bf16[512,1024]{1,0:T(8,128)(2,1)S(1)} %get-tuple-element.8.in_high_ref, bf16[512,1024]{1,0:T(8,128)(2,1)S(1)} %get-tuple-element.7.in_low_ref, ...), custom_call_target="tpu_custom_call" | custom-call | tf_op jit(solution)/shard_map/all_layers/pallas_call | solution.py:110
  26.4 12.8 %all_to_all.20 = f32[32,8,256]{2,1,0:T(8,128)S(1)} all-to-all(f32[32,8,256]{2,1,0:T(8,128)S(1)} %bitcast.6), channel_id=1, replica_groups=mesh['seqhi'=4,'seqlo'=8] {'seqhi','seqlo'}, dimensions={0} | all-to-all | bytes 524288 | tf_op jit(solution)/shard_map/all_to_all | solution.py:126
  39.2 0.7 %multiply_bitcast_fusion = f32[256,256]{1,0:T(8,128)} fusion(f32[32,8,256]{2,1,0:T(8,128)S(1)} %all_to_all.20), kind=kLoop, calls=%fused_computation.6 | loop fusion | flops 65536 | bytes 524288 | tf_op jit(solution)/shard_map/mul | solution.py:148
Async XLA Ops:
  0.0 18.0 %all-to-all-start = ((f32[32,8,256]{2,1,0:T(8,128)}), f32[32,8,256]{2,1,0:T(8,128)S(1)}, u32[]{:S(2)}, u32[]{:S(2)}) async-start(f32[32,8,256]{2,1,0:T(8,128)} %bitcast.7), calls=%async_computation | async-start | bytes 524288 | tf_op jit(solution)/shard_map/all_to_all | solution.py:126
  7.3 2.2 %copy-start.3 = (f32[1024,512]{1,0:T(8,128)S(1)}, f32[1024,512]{1,0:T(8,128)}, u32[]{:S(2)}) copy-start(f32[1024,512]{1,0:T(8,128)} %param.11) | copy-start | bytes 6291460
  9.5 8.4 %copy-start = (f32[8,1024]{1,0:T(8,128)S(1)}, f32[8,1024]{1,0:T(8,128)}, u32[]{:S(2)}) copy-start(f32[8,1024]{1,0:T(8,128)} %bias_ref.1) | copy-start | bytes 98308
  9.5 8.4 %copy-start.1 = (f32[8,512]{1,0:T(8,128)S(1)}, f32[8,512]{1,0:T(8,128)}, u32[]{:S(2)}) copy-start(f32[8,512]{1,0:T(8,128)} %gain_ref.1) | copy-start | bytes 49156
  9.5 8.4 %copy-start.2 = (f32[8,512]{1,0:T(8,128)S(1)}, f32[8,512]{1,0:T(8,128)}, u32[]{:S(2)}) copy-start(f32[8,512]{1,0:T(8,128)} %gate_ref.1) | copy-start | bytes 49156

commit v21 on v17

--- a/solution.py
+++ b/solution.py
@@ -117,7 +117,7 @@
             pltpu.VMEM(params[-1].shape, params[-1].dtype),
             pltpu.SemaphoreType.DMA((2,)),
         ],
-        compiler_params=pltpu.CompilerParams(vmem_limit_bytes=51 * 2**20),
+        compiler_params=pltpu.CompilerParams(vmem_limit_bytes=50 * 2**20),
         name=name,
     )(states, *params)
 

time: 40.1 us -> 39.8 us (level)
  transfers between devices with their start and end apart: 1 -> 1, of which waited for: 1 -> 1; matrix products, arithmetic and copies ran while one was open for 10% -> 9% of each run, Pallas kernels for 0% -> 0%
where the time goes in v21:
time: 39.8 us; the launch traced here: 39.6 us
  blocking collectives  12.8 us (32%)
  Pallas kernels  8.07 us (20%)
  starting transfers between devices  7.3 us (18%)
  waiting for transfers between devices  7.09 us (18%)
  other arithmetic  3.49 us (9%)
  local copies, waits for them, and re-layouts  0.76 us (2%)
    all_to_all x1, blocking collectives, all_to_all(): return lax.all_to_all(x, axes, split_axis=0, concat_axis=0, tiled=True)  12.8 us
    pallas_call x1, Pallas kernels, run_layers(): pl.pallas_call(kernel, out_shape=jax.ShapeDtypeStruct((rows, width), jnp....  8.07 us
    all_to_all x1, starting transfers between devices, all_to_all(): return lax.all_to_all(x, axes, split_axis=0, concat_axis=0, tiled=True)  7.3 us
    all_to_all x1, waiting for transfers between devices, all_to_all(): return lax.all_to_all(x, axes, split_axis=0, concat_axis=0, tiled=True)  7.09 us
    convert_element_type x2, other arithmetic, parts(): return (high.astype(jnp.bfloat16), (w - high).astype(jnp.bfloat16))  3.49 us
  transfers between devices with their start and end apart: 1, of which 1 were waited for; matrix products, arithmetic and copies ran while one was open for 9% of the time, Pallas kernels for 0%

profile of v21, /device:TPU:0, one launch (start us, length us, event | category | flops | bytes accessed | tf_op | source)
XLA Modules:
  0.0 39.6 jit_solution(3190352743839621172)
XLA Ops:
  0.0 7.3 %all-to-all-start = ((f32[32,8,256]{2,1,0:T(8,128)}), f32[32,8,256]{2,1,0:T(8,128)S(1)}, u32[]{:S(2)}, u32[]{:S(2)}) async-start(f32[32,8,256]{2,1,0:T(8,128)} %bitcast.7), calls=%async_computation | async-start | bytes 524288 | tf_op jit(solution)/shard_map/all_to_all | solution.py:126
  7.3 0.0 copy-start.3
  7.3 2.2 %fusion = (bf16[512,1024]{1,0:T(8,128)(2,1)S(1)}, bf16[512,1024]{1,0:T(8,128)(2,1)S(1)}) fusion(f32[512,1024]{1,0:T(8,128)} %param.10), kind=kLoop, calls=%fused_computation.4 | loop fusion | flops 2097152 | bytes 4194304 | tf_op jit(solution)/shard_map/convert_element_type | solution.py:139
  9.5 0.0 copy-done.3
  9.5 0.0 copy-start
  9.5 0.0 copy-start.1
  9.5 0.0 copy-start.2
  9.5 1.3 %fusion.1 = (bf16[1024,512]{1,0:T(8,128)(2,1)}, bf16[1024,512]{1,0:T(8,128)(2,1)S(1)}) fusion(f32[1024,512]{1,0:T(8,128)S(1)} %copy-done.3), kind=kLoop, calls=%fused_computation.5 | loop fusion | flops 2097152 | bytes 4194304 | tf_op jit(solution)/shard_map/convert_element_type | solution.py:139
  10.9 7.1 %all-to-all-done = f32[32,8,256]{2,1,0:T(8,128)S(1)} async-done(((f32[32,8,256]{2,1,0:T(8,128)}), f32[32,8,256]{2,1,0:T(8,128)S(1)}, u32[]{:S(2)}, u32[]{:S(2)}) %all-to-all-start) | async-done | bytes 262176 | tf_op jit(solution)/shard_map/all_to_all | solution.py:126
  18.0 0.0 copy-done
  18.0 0.0 copy-done.1
  18.0 0.0 copy-done.2
  18.0 8.1 %all_layers.1 = f32[256,256]{1,0:T(8,128)S(1)} custom-call(f32[256,256]{1,0:T(8,128)S(1)} %bitcast.4, f32[8,512]{1,0:T(8,128)S(1)} %copy-done.1, f32[8,1024]{1,0:T(8,128)S(1)} %copy-done, f32[8,512]{1,0:T(8,128)S(1)} %copy-done.2, bf16[512,1024]{1,0:T(8,128)(2,1)S(1)} %get-tuple-element.8.in_high_ref, bf16[512,1024]{1,0:T(8,128)(2,1)S(1)} %get-tuple-element.7.in_low_ref, ...), custom_call_target="tpu_custom_call" | custom-call | tf_op jit(solution)/shard_map/all_layers/pallas_call | solution.py:110
  26.0 12.8 %all_to_all.23 = f32[32,8,256]{2,1,0:T(8,128)S(1)} all-to-all(f32[32,8,256]{2,1,0:T(8,128)S(1)} %bitcast.5), channel_id=1, replica_groups=mesh['seqhi'=4,'seqlo'=8] {'seqhi','seqlo'}, dimensions={0} | all-to-all | bytes 524288 | tf_op jit(solution)/shard_map/all_to_all | solution.py:126
  38.9 0.7 %copy.8 = f32[256,256]{1,0:T(8,128)} copy(f32[256,256]{1,0:T(8,128)S(1)} %bitcast.6) | data formatting | bytes 524288
Async XLA Ops:
  0.0 18.0 %all-to-all-start = ((f32[32,8,256]{2,1,0:T(8,128)}), f32[32,8,256]{2,1,0:T(8,128)S(1)}, u32[]{:S(2)}, u32[]{:S(2)}) async-start(f32[32,8,256]{2,1,0:T(8,128)} %bitcast.7), calls=%async_computation | async-start | bytes 524288 | tf_op jit(solution)/shard_map/all_to_all | solution.py:126
  7.3 2.2 %copy-start.3 = (f32[1024,512]{1,0:T(8,128)S(1)}, f32[1024,512]{1,0:T(8,128)}, u32[]{:S(2)}) copy-start(f32[1024,512]{1,0:T(8,128)} %param.11) | copy-start | bytes 6291460
  9.5 8.4 %copy-start = (f32[8,1024]{1,0:T(8,128)S(1)}, f32[8,1024]{1,0:T(8,128)}, u32[]{:S(2)}) copy-start(f32[8,1024]{1,0:T(8,128)} %bias_ref.1) | copy-start | bytes 98308
  9.5 8.4 %copy-start.1 = (f32[8,512]{1,0:T(8,128)S(1)}, f32[8,512]{1,0:T(8,128)}, u32[]{:S(2)}) copy-start(f32[8,512]{1,0:T(8,128)} %gain_ref.1) | copy-start | bytes 49156
  9.5 8.4 %copy-start.2 = (f32[8,512]{1,0:T(8,128)S(1)}, f32[8,512]{1,0:T(8,128)}, u32[]{:S(2)}) copy-start(f32[8,512]{1,0:T(8,128)} %gate_ref.1) | copy-start | bytes 49156

commit v22 on v21

--- a/solution.py
+++ b/solution.py
@@ -49,12 +49,12 @@
 
 def layers_kernel(
     first, distances, hidden_block,
-    x_ref, gain_ref, bias_ref, gate_ref, in_high_ref, in_low_ref, out_high_any, out_low_any,
-    y_ref, out_high_ref, out_low_ref, copied,
+    x_ref, gain_ref, bias_ref, gate_ref, in_high_ref, in_low_ref, out_high_ref, out_low_any,
+    y_ref, out_low_ref, copied,
 ):
     pending = []
     for number, (source, target) in enumerate(
-        [(out_high_any, out_high_ref), (out_low_any, out_low_ref)]
+        [(out_low_any, out_low_ref)]
     ):
         copy = pltpu.make_async_copy(source, target, copied.at[number])
         copy.start()
@@ -110,12 +110,11 @@
     return pl.pallas_call(
         kernel,
         out_shape=jax.ShapeDtypeStruct((rows, width), jnp.float32),
-        in_specs=[vmem] * 6 + [pl.BlockSpec(memory_space=pl.ANY)] * 2,
+        in_specs=[vmem] * 7 + [pl.BlockSpec(memory_space=pl.ANY)],
         out_specs=vmem,
         scratch_shapes=[
-            pltpu.VMEM(params[-2].shape, params[-2].dtype),
             pltpu.VMEM(params[-1].shape, params[-1].dtype),
-            pltpu.SemaphoreType.DMA((2,)),
+            pltpu.SemaphoreType.DMA((1,)),
         ],
         compiler_params=pltpu.CompilerParams(vmem_limit_bytes=50 * 2**20),
         name=name,

time: 39.8 us -> 39.7 us (level)
  no operation moved by 1% of the time
where the time goes in v22:
time: 39.7 us; the launch traced here: 39.5 us
  blocking collectives  12.8 us (32%)
  Pallas kernels  7.97 us (20%)
  starting transfers between devices  7.3 us (18%)
  waiting for transfers between devices  7.09 us (18%)
  other arithmetic  3.49 us (9%)
  local copies, waits for them, and re-layouts  0.76 us (2%)
    all_to_all x1, blocking collectives, all_to_all(): return lax.all_to_all(x, axes, split_axis=0, concat_axis=0, tiled=True)  12.8 us
    pallas_call x1, Pallas kernels, run_layers(): pl.pallas_call(kernel, out_shape=jax.ShapeDtypeStruct((rows, width), jnp....  7.97 us
    all_to_all x1, starting transfers between devices, all_to_all(): return lax.all_to_all(x, axes, split_axis=0, concat_axis=0, tiled=True)  7.3 us
    all_to_all x1, waiting for transfers between devices, all_to_all(): return lax.all_to_all(x, axes, split_axis=0, concat_axis=0, tiled=True)  7.09 us
    convert_element_type x2, other arithmetic, parts(): return (high.astype(jnp.bfloat16), (w - high).astype(jnp.bfloat16))  3.49 us
  transfers between devices with their start and end apart: 1, of which 1 were waited for; matrix products, arithmetic and copies ran while one was open for 9% of the time, Pallas kernels for 0%

profile of v22, /device:TPU:0, one launch (start us, length us, event | category | flops | bytes accessed | tf_op | source)
XLA Modules:
  0.0 39.5 jit_solution(17916945685713612017)
XLA Ops:
  0.0 7.3 %all-to-all-start = ((f32[32,8,256]{2,1,0:T(8,128)}), f32[32,8,256]{2,1,0:T(8,128)S(1)}, u32[]{:S(2)}, u32[]{:S(2)}) async-start(f32[32,8,256]{2,1,0:T(8,128)} %bitcast.7), calls=%async_computation | async-start | bytes 524288 | tf_op jit(solution)/shard_map/all_to_all | solution.py:125
  7.3 0.0 copy-start.3
  7.3 2.2 %fusion = (bf16[512,1024]{1,0:T(8,128)(2,1)S(1)}, bf16[512,1024]{1,0:T(8,128)(2,1)S(1)}) fusion(f32[512,1024]{1,0:T(8,128)} %param.10), kind=kLoop, calls=%fused_computation.4 | loop fusion | flops 2097152 | bytes 4194304 | tf_op jit(solution)/shard_map/convert_element_type | solution.py:138
  9.5 0.0 copy-done.3
  9.5 0.0 copy-start
  9.5 0.0 copy-start.1
  9.5 0.0 copy-start.2
  9.5 1.3 %fusion.1 = (bf16[1024,512]{1,0:T(8,128)(2,1)}, bf16[1024,512]{1,0:T(8,128)(2,1)S(1)}) fusion(f32[1024,512]{1,0:T(8,128)S(1)} %copy-done.3), kind=kLoop, calls=%fused_computation.5 | loop fusion | flops 2097152 | bytes 4194304 | tf_op jit(solution)/shard_map/convert_element_type | solution.py:138
  10.9 7.1 %all-to-all-done = f32[32,8,256]{2,1,0:T(8,128)S(1)} async-done(((f32[32,8,256]{2,1,0:T(8,128)}), f32[32,8,256]{2,1,0:T(8,128)S(1)}, u32[]{:S(2)}, u32[]{:S(2)}) %all-to-all-start) | async-done | bytes 262176 | tf_op jit(solution)/shard_map/all_to_all | solution.py:125
  18.0 0.0 copy-done
  18.0 0.0 copy-done.1
  18.0 0.0 copy-done.2
  18.0 8.0 %all_layers.1 = f32[256,256]{1,0:T(8,128)S(1)} custom-call(f32[256,256]{1,0:T(8,128)S(1)} %bitcast.4, f32[8,512]{1,0:T(8,128)S(1)} %copy-done.1, f32[8,1024]{1,0:T(8,128)S(1)} %copy-done, f32[8,512]{1,0:T(8,128)S(1)} %copy-done.2, bf16[512,1024]{1,0:T(8,128)(2,1)S(1)} %get-tuple-element.8.in_high_ref, bf16[512,1024]{1,0:T(8,128)(2,1)S(1)} %get-tuple-element.7.in_low_ref, ...), custom_call_target="tpu_custom_call" | custom-call | tf_op jit(solution)/shard_map/all_layers/pallas_call | solution.py:110
  25.9 12.8 %all_to_all.23 = f32[32,8,256]{2,1,0:T(8,128)S(1)} all-to-all(f32[32,8,256]{2,1,0:T(8,128)S(1)} %bitcast.5), channel_id=1, replica_groups=mesh['seqhi'=4,'seqlo'=8] {'seqhi','seqlo'}, dimensions={0} | all-to-all | bytes 524288 | tf_op jit(solution)/shard_map/all_to_all | solution.py:125
  38.8 0.7 %copy.8 = f32[256,256]{1,0:T(8,128)} copy(f32[256,256]{1,0:T(8,128)S(1)} %bitcast.6) | data formatting | bytes 524288
Async XLA Ops:
  0.0 18.0 %all-to-all-start = ((f32[32,8,256]{2,1,0:T(8,128)}), f32[32,8,256]{2,1,0:T(8,128)S(1)}, u32[]{:S(2)}, u32[]{:S(2)}) async-start(f32[32,8,256]{2,1,0:T(8,128)} %bitcast.7), calls=%async_computation | async-start | bytes 524288 | tf_op jit(solution)/shard_map/all_to_all | solution.py:125
  7.3 2.2 %copy-start.3 = (f32[1024,512]{1,0:T(8,128)S(1)}, f32[1024,512]{1,0:T(8,128)}, u32[]{:S(2)}) copy-start(f32[1024,512]{1,0:T(8,128)} %param.11) | copy-start | bytes 6291460
  9.5 8.4 %copy-start = (f32[8,1024]{1,0:T(8,128)S(1)}, f32[8,1024]{1,0:T(8,128)}, u32[]{:S(2)}) copy-start(f32[8,1024]{1,0:T(8,128)} %bias_ref.1) | copy-start | bytes 98308
  9.5 8.4 %copy-start.1 = (f32[8,512]{1,0:T(8,128)S(1)}, f32[8,512]{1,0:T(8,128)}, u32[]{:S(2)}) copy-start(f32[8,512]{1,0:T(8,128)} %gain_ref.1) | copy-start | bytes 49156
  9.5 8.4 %copy-start.2 = (f32[8,512]{1,0:T(8,128)S(1)}, f32[8,512]{1,0:T(8,128)}, u32[]{:S(2)}) copy-start(f32[8,512]{1,0:T(8,128)} %gate_ref.1) | copy-start | bytes 49156
